TPU v7x, 128 devices: a whole 4x4x4 slice. The times are simulated.
128 devices in a mesh: rep: 16 (over y_lo, x, core), fsdp: 8 (over z, y_hi).
Axes of the slice: x: 4, y: 4 (y_hi: 2, y_lo: 2; y = y_hi * 2 + y_lo), z: 4, core: 2. Of those that a mesh axis runs over, the one named last changes fastest.
Arguments:
- inputs: bfloat16 [16, 1024, 1536], P('rep', 'fsdp'), may hold values from -6 to 6
- segments: int32 [16, 1024], P('rep'), may hold values from 0 to 4, as said below
- first_gain: bfloat16 [1536], P('fsdp'), may hold values from 0.25 to 1.75
- query_matrix: bfloat16 [1536, 1536], P('fsdp'), may hold values from -0.15625 to 0.15625
- key_matrix: bfloat16 [1536, 256], P('fsdp'), may hold values from -0.15625 to 0.15625
- value_matrix: bfloat16 [1536, 256], P('fsdp'), may hold values from -0.15625 to 0.15625
- output_matrix: bfloat16 [1536, 1536], P('fsdp'), may hold values from -0.625 to 0.625
- second_gain: bfloat16 [1536], P('fsdp'), may hold values from 0.25 to 1.75
- expert_ids: int32 [16, 1024, 4], P('rep', 'fsdp'), may hold values from 0 to 7, all different within a row
- gate_values: float32 [16, 1024, 4], P('rep', 'fsdp'), may hold values from 0.1 to 0.5
- priority: int32 [16, 8, 512], P('rep', 'fsdp'), may hold values from 0 to 511, each once within a row
- gate_weight: bfloat16 [8, 1536, 768], P('fsdp'), may hold values from -0.15625 to 0.15625
- up_weight: bfloat16 [8, 1536, 768], P('fsdp'), may hold values from -0.15625 to 0.15625
- down_weight: bfloat16 [8, 768, 1536], P('fsdp'), may hold values from -0.4375 to 0.4375
- cotangent: bfloat16 [16, 1024, 1536], P('rep', 'fsdp'), may hold values from -6 to 6
Outputs:
- outputs: bfloat16 [16, 1024, 1536], P('rep', 'fsdp')
- input_grad: bfloat16 [16, 1024, 1536], P('rep', 'fsdp')
- first_gain_grad: float32 [1536], P('fsdp')
- query_grad: float32 [1536, 1536], P('fsdp')
- key_grad: float32 [1536, 256], P('fsdp')
- value_grad: float32 [1536, 256], P('fsdp')
- output_grad: float32 [1536, 1536], P('fsdp')
- second_gain_grad: float32 [1536], P('fsdp')
- gate_grad: float32 [8, 1536, 768], P('fsdp')
- up_grad: float32 [8, 1536, 768], P('fsdp')
- down_grad: float32 [8, 768, 1536], P('fsdp')
Inputs may be any that keep to these rules, and one draw needn't show every extreme that they name: `segments`: segment numbers never fall along a sequence. `expert_ids`: each token names 4 different experts. `priority`: each device's row is a permutation.
All inputs are finite; a program needn't handle non-finite values.
Results may differ from a plain program's by a relative error of at most 0.025.
Values may be sent and summed in bfloat16 or wider, within the bound.
No kernel may reach another device: no remote copies, remote signals or barrier semaphores. Data moves between devices by JAX's collectives and lax.ppermute only.
A program may use at most 128 MiB of HBM per device.

v0:
```python
import jax
import jax.numpy as jnp
from jax import lax
from jax.experimental import pallas as pl
from jax.experimental.pallas import tpu as pltpu
from jax.sharding import Mesh
from jax.sharding import PartitionSpec as P

HEADS = 12
KV_HEADS = 2
HEAD_DIM = 128
TOP = 4
WINDOW = 1024

EPSILON = 1e-06
THETA = 10000.0
NEGATIVE = -1e30

YLO, XS, CORES = 2, 4, 2
REP = ("ylo", "x", "core")
BF = jnp.bfloat16
F32 = jnp.float32


def angles(positions):
    half_width = HEAD_DIM // 2
    frequency = THETA ** (-(jnp.arange(half_width, dtype=F32) * 2.0) / HEAD_DIM)
    phase = positions.astype(F32)[:, None] * frequency[None, :]
    cosine, sine = jnp.cos(phase), jnp.sin(phase)
    return (
        jnp.concatenate([cosine, cosine], axis=1),
        jnp.concatenate([-sine, sine], axis=1),
    )


def dot(a, b):
    return jnp.dot(a, b, preferred_element_type=F32)


def dot_t(a, b):
    return lax.dot_general(a, b, (((1,), (1,)), ((), ())), preferred_element_type=F32)


def t_dot(a, b):
    return lax.dot_general(a, b, (((0,), (0,)), ((), ())), preferred_element_type=F32)


def add(a, b):
    return (a.astype(F32) + b.astype(F32)).astype(BF)


def turn(piece, cosine, sine):
    return piece * cosine + pltpu.roll(piece, HEAD_DIM // 2, 1) * sine


def turn_back(piece, cosine, sine):
    return piece * cosine - pltpu.roll(piece, HEAD_DIM // 2, 1) * sine


def key_kernel(place, src, gain, raw_own, raw_other, cos, sin, normed_o, scale_o, send_o, weight_o):
    core = place[0]
    groups, kv_rows, width = raw_own.shape
    kv_width = weight_o.shape[1] // 2
    parts = width // kv_width
    source = src[...].astype(F32)
    scale = lax.rsqrt(jnp.mean(source * source, axis=-1, keepdims=True) + EPSILON)
    scale_o[...] = jnp.broadcast_to(scale, scale_o.shape)
    normed = (source * scale * gain[...]).astype(BF)
    normed_o[...] = normed
    for raw, which in ((raw_own, core), (raw_other, 1 - core)):
        at = pl.ds(pl.multiple_of(which * kv_width, kv_width), kv_width)
        for f in range(groups):
            for j in range(parts):
                weight_o[pl.ds((f * parts + j) * kv_rows, kv_rows), at] = raw[
                    f, :, pl.ds(j * kv_width, kv_width)
                ]
    pre = dot(normed, weight_o[...])
    for head in range(2 * KV_HEADS):
        low, high = head * HEAD_DIM, (head + 1) * HEAD_DIM
        piece = pre[:, low:high]
        if head < KV_HEADS:
            piece = turn(piece, cos[...], sin[...])
        for f in range(groups):
            send_o[f, :, low:high] = piece.astype(BF)


def put_weight(place, weight_o, pieces, which, spots):
    groups, quarter, half = pieces[0].shape
    at = pl.ds(pl.multiple_of(which * half, half), half)
    for block, (s, t) in zip(pieces, spots):
        for f in range(groups):
            start = (f * XS + 2 * s + t) * quarter
            weight_o[pl.ds(pl.multiple_of(start, quarter), quarter), at] = block[f]


def query_kernel(place, normed, a, b, c, d, e, f, g, h, cos, sin, weight_o, query_o):
    core, s, t = place[0], place[2], place[3]
    spots = ((s, t), (s, 1 - t), (1 - s, t), (1 - s, 1 - t))
    put_weight(place, weight_o, (a, b, c, d), core, spots)
    put_weight(place, weight_o, (e, f, g, h), 1 - core, spots)
    pre = dot(normed[...], weight_o[...])
    for head in range(HEADS):
        low, high = head * HEAD_DIM, (head + 1) * HEAD_DIM
        query_o[:, low:high] = turn(pre[:, low:high], cos[...], sin[...]).astype(BF)


def attend_kernel(place, q, kv, seg_row, seg_col, mixed_o, probs_o, bias):
    base = place[1]
    length, tok = bias.shape
    kv_width = kv.shape[1] // 2
    key_place = lax.broadcasted_iota(jnp.int32, (length, tok), 0)
    query_place = base + lax.broadcasted_iota(jnp.int32, (length, tok), 1)
    allowed = (
        (key_place <= query_place)
        & (query_place - key_place < WINDOW)
        & (seg_col[...] == seg_row[...])
    )
    bias[...] = jnp.where(allowed, 0.0, NEGATIVE)
    for head in range(HEADS):
        group = head // (HEADS // KV_HEADS)
        at = pl.ds(head * HEAD_DIM, HEAD_DIM)
        keys = kv[:, pl.ds(group * HEAD_DIM, HEAD_DIM)]
        values = kv[:, pl.ds(kv_width + group * HEAD_DIM, HEAD_DIM)]
        scores = dot_t(keys, q[:, at]) * HEAD_DIM ** (-0.5) + bias[...]
        weights = jnp.exp(scores - jnp.max(scores, axis=0, keepdims=True))
        probs = (weights * (1.0 / jnp.sum(weights, axis=0, keepdims=True))).astype(BF)
        probs_o[head] = probs
        mixed_o[:, at] = t_dot(probs, values).astype(BF)


def residual_kernel(
    place, mixed, a, b, c, d, e, f, g, h, src, gain, hot, weight_o, resid_o, scale_o, send_o
):
    core, s, t = place[0], place[2], place[3]
    spots = ((s, t), (1 - s, t), (s, 1 - t), (1 - s, 1 - t))
    put_weight(place, weight_o, (a, b, c, d), core, spots)
    put_weight(place, weight_o, (e, f, g, h), 1 - core, spots)
    resid = src[...].astype(F32) + dot(mixed[...], weight_o[...])
    resid_o[...] = resid
    scale = lax.rsqrt(jnp.mean(resid * resid, axis=-1, keepdims=True) + EPSILON)
    scale_o[...] = jnp.broadcast_to(scale, scale_o.shape)
    second = (resid * scale * gain[...]).astype(BF)
    send_o[...] = dot(hot[...], second).astype(BF)


def expert_kernel(place, rows, grad_hidden, gate_w, up_w, hidden_o, pre_o, back_o):
    core = place[0]
    count = rows.shape[0]
    step = count // 2
    for low in range(0, count, step):
        at = pl.ds(low, step)
        block = rows[at, :]
        gate = dot(block, gate_w[...])
        up = dot(block, up_w[...])
        sigmoid = 1.0 / (1.0 + jnp.exp(-gate))
        silu = gate * sigmoid
        hidden_o[at, :] = (silu * up).astype(BF)
        grad = grad_hidden[at, :]
        grad_gate = (grad * up * (sigmoid * (1.0 + gate * (1.0 - sigmoid)))).astype(BF)
        grad_up = (grad * silu).astype(BF)
        pre_o[core, at, :] = grad_gate
        pre_o[1 - core, at, :] = grad_up
        back_o[at, :] = (dot_t(grad_gate, gate_w[...]) + dot_t(grad_up, up_w[...])).astype(BF)


def sent_expert_kernel(place, rows, pre, hidden, arrived, out):
    width, half = rows.shape[1], hidden.shape[1]
    upper = arrived[:, pl.ds(pl.multiple_of((1 - place[0]) * half, half), half)]
    step = 256
    for low in range(0, width, step):
        out[pl.ds(low, step), :] = t_dot(rows[:, pl.ds(low, step)], pre[1]).astype(BF)
    for low in range(0, half, step):
        out[pl.ds(width + low, step), :] = t_dot(hidden[:, pl.ds(low, step)], upper).astype(BF)


def own_expert_kernel(
    place, rows, pre, hidden, arrived, got, down_w, keep_a, send_a, keep_b, send_b, out_o, total
):
    s, t = place[2], place[3]
    width, half = rows.shape[1], hidden.shape[1]
    upper = arrived[:, pl.ds(pl.multiple_of(place[0] * half, half), half)]
    step = 256
    for low in range(0, width, step):
        at = pl.ds(low, step)
        total[at, :] = (t_dot(rows[:, at], pre[0]) + got[at, :].astype(F32)).astype(BF)
    for low in range(0, half, step):
        at = pl.ds(width + low, step)
        part = t_dot(hidden[:, pl.ds(low, step)], upper)
        total[at, :] = (part + got[at, :].astype(F32)).astype(BF)
    big, small = width // 8, half // 8
    for out, side, spots in (
        (send_a, 0, ((1 - s, 0), (1 - s, 1))),
        (keep_a, 0, ((s, 0), (s, 1))),
        (send_b, 1, ((0, 1 - t), (1, 1 - t))),
        (keep_b, 1, ((0, t), (1, t))),
    ):
        for j, (row_s, row_t) in enumerate(spots):
            piece = side * 4 + 2 * row_s + row_t
            out[j, pl.ds(0, big), :] = total[pl.ds(pl.multiple_of(piece * big, big), big), :]
            start = pl.multiple_of(width + piece * small, small)
            out[j, pl.ds(big, small), :] = total[pl.ds(start, small), :]
    out_o[...] = dot(hidden[...], down_w[...]).astype(BF)


def expert_step_kernel(place, keep_a, got_a, keep_b, got_b, keep_ao, send_ao, keep_bo, send_bo):
    s, t = place[2], place[3]
    keep_ao[...] = add(keep_a[t], got_a[t])
    send_ao[...] = add(keep_a[1 - t], got_a[1 - t])
    keep_bo[...] = add(keep_b[s], got_b[s])
    send_bo[...] = add(keep_b[1 - s], got_b[1 - s])


def expert_end_kernel(place, keep_a, got_a, keep_b, got_b, out):
    out[0] = add(keep_a[...], got_a[...])
    out[1] = add(keep_b[...], got_b[...])


def pair_kernel(place, a, b, out):
    out[...] = add(a[...], b[...])


def expert_out_kernel(place, *refs):
    core, s, t = place[0], place[2], place[3]
    gate_o, up_o, down_o = refs[10:]
    width, half = gate_o.shape
    big, small = width // 8, half // 8

    def put(pieces, which, first):
        own, one_a, one_b, two_a, two_b = pieces
        blocks = (
            (0, s, t, own.at[0]),
            (0, s, 1 - t, one_a),
            (0, 1 - s, t, two_a.at[0]),
            (0, 1 - s, 1 - t, two_a.at[1]),
            (1, s, t, own.at[1]),
            (1, 1 - s, t, one_b),
            (1, s, 1 - t, two_b.at[0]),
            (1, 1 - s, 1 - t, two_b.at[1]),
        )
        at = pl.ds(pl.multiple_of(which * half, half), half)
        for side, row_s, row_t, block in blocks:
            piece = side * 4 + 2 * row_s + row_t
            first[pl.ds(pl.multiple_of(piece * big, big), big), :] = block[
                pl.ds(0, big), :
            ].astype(F32)
            down_o[pl.ds(pl.multiple_of(piece * small, small), small), at] = block[
                pl.ds(big, small), :
            ].astype(F32)

    @pl.when(core == 0)
    def _():
        put(refs[:5], 0, gate_o)
        put(refs[5:10], 1, up_o)

    @pl.when(core == 1)
    def _():
        put(refs[:5], 1, up_o)
        put(refs[5:10], 0, gate_o)


def back_kernel(
    place, back, hot_t, resid_i, scale_i, gain, cot, weight, probs_i, kv, q, cos, sin,
    grad_resid_o, attended_o, gain_o, query_o, kv_o,
):
    kv_width = kv.shape[1] // 2
    resid = resid_i[...]
    scale = scale_i[:, :1]
    grad_second = dot(hot_t[...], back[...])
    weighted = grad_second * gain[...]
    inner = jnp.sum(weighted * resid, axis=-1, keepdims=True)
    grad_resid = (
        cot[...].astype(F32)
        + scale * weighted
        - resid * (scale * scale * scale * inner * (1.0 / resid.shape[-1]))
    )
    gain_o[...] = jnp.sum(grad_second * resid * scale, axis=0, keepdims=True)
    grad_resid_o[...] = grad_resid
    attended = grad_resid.astype(BF)
    attended_o[...] = attended
    grad_mixed = dot_t(attended, weight[...]).astype(BF)
    heads = HEADS // KV_HEADS
    for group in range(KV_HEADS):
        keys = kv[:, pl.ds(group * HEAD_DIM, HEAD_DIM)]
        values = kv[:, pl.ds(kv_width + group * HEAD_DIM, HEAD_DIM)]
        grad_keys = jnp.zeros(keys.shape, F32)
        grad_values = jnp.zeros(keys.shape, F32)
        for head in range(group * heads, (group + 1) * heads):
            low, high = head * HEAD_DIM, (head + 1) * HEAD_DIM
            upper = grad_mixed[:, low:high]
            probs = probs_i[head]
            wide = probs.astype(F32)
            grad_probs = dot_t(values, upper)
            total = jnp.sum(wide * grad_probs, axis=0, keepdims=True)
            grad_scores = (wide * (grad_probs - total)).astype(BF)
            grad_values = grad_values + dot(probs, upper)
            grad_keys = grad_keys + dot(grad_scores, q[:, low:high])
            grad_query = t_dot(grad_scores, keys) * HEAD_DIM ** (-0.5)
            query_o[:, low:high] = turn_back(grad_query, cos[...], sin[...]).astype(BF)
        at = pl.ds(group * HEAD_DIM, HEAD_DIM)
        kv_o[:, at] = (grad_keys * HEAD_DIM ** (-0.5)).astype(BF)
        kv_o[:, pl.ds(kv_width + group * HEAD_DIM, HEAD_DIM)] = grad_values.astype(BF)


def square_weight_kernel(own, place, mixed, attended, normed, query, out):
    half = mixed.shape[1] // 2
    which = place[0] if own else 1 - place[0]
    at = pl.ds(pl.multiple_of(which * half, half), half)
    step = 256
    for k, (left, right) in enumerate(((mixed, attended), (normed, query))):
        part = right[:, at]
        for low in range(0, 2 * half, step):
            out[k, pl.ds(low, step), :] = t_dot(left[:, pl.ds(low, step)], part).astype(BF)


def split_kernel(place, own_a, got_a, own_b, got_b, keep_a, send_a, keep_b, send_b):
    s, t = place[2], place[3]
    groups, _, quarter, _ = keep_a.shape
    for f in range(groups):
        for j in range(2):
            for out, own, got, row_s, row_t in (
                (send_a, own_a, got_a, 1 - s, j),
                (keep_a, own_a, got_a, s, j),
                (send_b, own_b, got_b, j, 1 - t),
                (keep_b, own_b, got_b, j, t),
            ):
                start = (f * XS + 2 * row_s + row_t) * quarter
                at = pl.ds(pl.multiple_of(start, quarter), quarter)
                out[f, j] = add(own[at, :], got[at, :])


def step_kernel(
    place, qk_a, qg_a, kk_a, kg_a, qk_b, qg_b, kk_b, kg_b, keep_a, send_a, keep_b, send_b
):
    s, t = place[2], place[3]
    size = qk_a.shape[-1]
    extra = kk_a.shape[-1]
    groups = qk_a.shape[0]
    for f in range(groups):
        for out, which, big, big_got, small, small_got in (
            (send_a, 1 - t, qk_a, qg_a, kk_a, kg_a),
            (keep_a, t, qk_a, qg_a, kk_a, kg_a),
            (send_b, 1 - s, qk_b, qg_b, kk_b, kg_b),
            (keep_b, s, qk_b, qg_b, kk_b, kg_b),
        ):
            out[f, :, pl.ds(0, size)] = add(big[f, which], big_got[f, which])
            out[f, :, pl.ds(size, extra)] = add(small[f, which], small_got[f, which])


def pack_kernel(place, keep_a, got_a, keep_b, got_b, gains, out):
    size = keep_a.shape[-1]
    for y, (keep, got) in enumerate(((keep_a, got_a), (keep_b, got_b))):
        out[y, :, :, pl.ds(0, size)] = add(keep[...], got[...])
        out[y, :, :, pl.ds(size, gains.shape[-1])] = gains[...]


def sum_kernel(place, parts, out):
    total = parts[0].astype(F32)
    for k in range(1, parts.shape[0]):
        total = total + parts[k].astype(F32)
    total = total.astype(BF)
    for k in range(out.shape[0]):
        out[k] = total


def final_kernel(place, own, other, output_o, query_o, key_o, value_o, gains_o):
    core = place[0]
    quarter = own.shape[1]
    half = output_o.shape[1] // 2
    part = key_o.shape[1] // 2
    size = half + part
    for refs, which in ((own, core), (other, 1 - core)):
        at = pl.ds(pl.multiple_of(which * half, half), half)
        for piece, x in enumerate(PLACE):
            rows = pl.ds(piece * quarter, quarter)
            output_o[rows, at] = refs[x, :, pl.ds(0, half)].astype(F32)
            query_o[rows, at] = refs[XS + x, :, pl.ds(0, half)].astype(F32)
    for piece, x in enumerate(PLACE):
        rows = pl.ds(piece * quarter, quarter)
        for y in range(2):
            at = pl.ds(y * part, part)
            mine = own[y * XS + x, :, pl.ds(half, part)].astype(F32)
            others = other[y * XS + x, :, pl.ds(half, part)].astype(F32)
            even = core == 0
            key_o[rows, at] = jnp.where(even, mine, others)
            value_o[rows, at] = jnp.where(even, others, mine)
    total = jnp.zeros(gains_o.shape, F32)
    for refs in (own, other):
        for x in range(XS):
            total = total + refs[x, :, pl.ds(size, gains_o.shape[1])].astype(F32)
    gains_o[...] = total


def key_weight_kernel(place, parts, cos, sin, normed, own_o, sent_o, pre_o):
    core = place[0]
    kv_width = parts.shape[-1] // 2
    total = parts[0].astype(F32)
    for k in range(1, parts.shape[0]):
        total = total + parts[k].astype(F32)
    for head in range(2 * KV_HEADS):
        low, high = head * HEAD_DIM, (head + 1) * HEAD_DIM
        piece = total[:, low:high]
        if head < KV_HEADS:
            piece = turn_back(piece, cos[...], sin[...])
        pre_o[:, low:high] = piece.astype(BF)
    for out, which in ((sent_o, 1 - core), (own_o, core)):
        part = pre_o[:, pl.ds(pl.multiple_of(which * kv_width, kv_width), kv_width)]
        grad = t_dot(normed[...], part).astype(BF)
        out[0] = grad[:, : kv_width // 2]
        out[1] = grad[:, kv_width // 2 :]


def input_kernel(
    place, query, pre, src, scale_i, gain, query_w, kv_w, grad_resid, input_o, gain_o
):
    grad_normed = dot_t(query[...], query_w[...]) + dot_t(pre[...], kv_w[...])
    source = src[...].astype(F32)
    scale = scale_i[:, :1]
    weighted = grad_normed * gain[...]
    inner = jnp.sum(weighted * source, axis=-1, keepdims=True)
    input_o[...] = (
        grad_resid[...]
        + scale * weighted
        - source * (scale * scale * scale * inner * (1.0 / source.shape[-1]))
    ).astype(BF)
    gain_o[...] = jnp.sum(grad_normed * source * scale, axis=0, keepdims=True)


def call(kernel, args, outs, scratch=(), micros=0):
    return pl.pallas_call(
        kernel,
        out_shape=[jax.ShapeDtypeStruct(shape, kind) for shape, kind in outs],
        in_specs=[pl.BlockSpec(memory_space=pltpu.SMEM)]
        + [pl.BlockSpec(memory_space=pltpu.VMEM)] * (len(args) - 1),
        out_specs=[pl.BlockSpec(memory_space=pltpu.VMEM)] * len(outs),
        scratch_shapes=list(scratch),
        compiler_params=pltpu.CompilerParams(vmem_limit_bytes=48 * 1024 * 1024),
        cost_estimate=pl.CostEstimate(flops=int(micros * 1e9), bytes_accessed=0, transcendentals=0),
    )(*args)


def swap(v):
    return lax.ppermute(v, "core", [(0, 1), (1, 0)])


def swap_y(v):
    return lax.ppermute(v, "ylo", [(0, 1), (1, 0)])


def exchange(v, axis):
    return lax.all_to_all(v, axis, 0, 0, tiled=True)


def copies(v, n):
    return lax.optimization_barrier(jnp.broadcast_to(v[None], (n,) + v.shape))


def tie(*values):
    return lax.optimization_barrier(values)


PAIRS_S = [(0, 1), (1, 0), (2, 3), (3, 2)]
PAIRS_T = [(0, 3), (3, 0), (1, 2), (2, 1)]
PLACE = (0, 3, 1, 2)


def x_bits():
    x = lax.axis_index("x")
    return ((x + 1) // 2) % 2, x // 2


def flip(v, pairs):
    return lax.ppermute(v, "x", pairs)


def body(
    inputs,
    segments,
    first_gain,
    query_matrix,
    key_matrix,
    value_matrix,
    output_matrix,
    second_gain,
    expert_ids,
    gate_values,
    priority,
    gate_weight,
    up_weight,
    down_weight,
    cotangent,
):
    tok = inputs.shape[1]
    width = inputs.shape[2]
    rows = query_matrix.shape[0]
    groups = lax.axis_size("fsdp")
    member = lax.axis_index("fsdp")
    core = lax.axis_index("core")
    even = core == 0
    experts = groups
    capacity = 5 * tok * TOP // (4 * experts)
    slots_all = experts * capacity
    half = width // 2
    kv_width = key_matrix.shape[1]
    length = groups * tok
    quarter = rows // XS
    bit_s, bit_t = x_bits()
    place_at = jnp.stack([core, member * tok, bit_s, bit_t]).astype(jnp.int32)

    def pick(a, b):
        return jnp.where(even, a, b)

    def qo_blocks(q_spot, o_spot):
        return jnp.concatenate(
            [
                lax.dynamic_slice(
                    matrix, ((2 * spot[0] + spot[1]) * quarter, core * half), (quarter, half)
                )
                for matrix, spot in ((query_matrix, q_spot), (output_matrix, o_spot))
            ],
            axis=1,
        )

    parts = width // kv_width
    kv_rows = rows // parts
    kv_half = pick(key_matrix, value_matrix).reshape(parts, kv_rows, kv_width)
    kv_piece = jnp.concatenate([kv_half[j] for j in range(parts)], axis=1)
    gains = jnp.pad(jnp.stack([first_gain, second_gain]), ((0, 6), (0, width - rows)))
    qo_first = qo_blocks((bit_s, bit_t), (bit_s, bit_t))
    qo_second = qo_blocks((bit_s, 1 - bit_t), (1 - bit_s, bit_t))
    gathered = exchange(
        copies(jnp.concatenate([kv_piece, gains, qo_first], axis=0), groups), "fsdp"
    )

    ids = expert_ids[0].reshape(-1)
    order = priority[0, 0]
    earlier = (order[None, :] < order[:, None]) & (ids[None, :] == ids[:, None])
    slots = jnp.sum(earlier.astype(jnp.int32), axis=1)
    kept = slots < capacity
    expert_list = jnp.arange(experts, dtype=jnp.int32)
    chosen = (ids[:, None] == expert_list[None, :]) & kept[:, None]
    slot_of = jnp.sum(
        jnp.where(chosen, slots[:, None] + 1, 0).reshape(tok, TOP, experts), axis=1
    )
    slot_of = slot_of - 1
    gate_table = jnp.sum(
        jnp.where(chosen, gate_values[0].reshape(-1)[:, None], 0.0).reshape(tok, TOP, experts),
        axis=1,
    )
    slot_list = jnp.arange(capacity, dtype=jnp.int32)
    hits = slot_of.T[:, None, :] == slot_list[None, :, None]
    one_hot = hits.astype(BF).reshape(slots_all, tok)
    gate_hot = jnp.where(hits, gate_table.T[:, None, :], 0.0).reshape(slots_all, tok)
    slot_gate = jnp.sum(gate_hot, axis=1, keepdims=True)
    gate_high = gate_hot.astype(BF)
    gate_low = (gate_hot - gate_high.astype(F32)).astype(BF)
    send_grad = (dot(one_hot, cotangent[0]) * slot_gate).astype(BF)

    cosine, sine = angles(member * tok + jnp.arange(tok, dtype=jnp.int32))
    segment_row = segments[0]
    query_segments = lax.dynamic_slice_in_dim(segment_row, member * tok, tok)
    segment_column = segment_row[:, None]
    one_hot_t = one_hot.T
    qo_second = copies(qo_second, groups)
    (gathered, qo_second, one_hot, one_hot_t, gate_high, gate_low, send_grad, cosine, sine,
     segment_column, place_at) = tie(
        gathered, qo_second, one_hot, one_hot_t, gate_high, gate_low, send_grad, cosine, sine,
        segment_column, place_at)
    kv_raw = gathered[:, :kv_rows]
    gain_one = gathered[:, kv_rows, :rows].reshape(1, width).astype(F32)
    gain_two = gathered[:, kv_rows + 1, :rows].reshape(1, width).astype(F32)
    second_blocks = exchange(qo_second, "fsdp")
    kv_raw_other = swap(kv_raw)
    q_first, o_first = gathered[:, kv_rows + 8 :, :half], gathered[:, kv_rows + 8 :, half:]

    square = (width, width)
    normed, scale_one, kv_send, kv_weight = call(
        key_kernel,
        [place_at, inputs[0], gain_one, kv_raw, kv_raw_other, cosine, sine],
        [((tok, width), BF), ((tok, HEAD_DIM), F32), ((groups, tok, 2 * kv_width), BF),
         ((width, 2 * kv_width), BF)],
    )
    kv_send, second_blocks = tie(kv_send, second_blocks)
    q_second, o_second = second_blocks[..., :half], second_blocks[..., half:]
    kv_all = exchange(kv_send, "fsdp").reshape(length, 2 * kv_width)
    send_grad, kv_all = tie(send_grad, kv_all)
    arrived_grad = exchange(send_grad, "fsdp")
    q_own = (q_first, q_second, flip(q_first, PAIRS_S), flip(q_second, PAIRS_S))
    o_own = (o_first, o_second, flip(o_first, PAIRS_T), flip(o_second, PAIRS_T))
    q_other = tuple(swap(v) for v in q_own)
    o_other = tuple(swap(v) for v in o_own)
    query_weight, query_rot = call(
        query_kernel,
        [place_at, normed, *q_own, *q_other, cosine, sine],
        [(square, BF), ((tok, width), BF)],
    )
    mixed, probs = call(
        attend_kernel,
        [place_at, query_rot, kv_all, query_segments[None], segment_column],
        [((tok, width), BF), ((HEADS, length, tok), BF)],
        [pltpu.VMEM((length, tok), F32)],
    )
    output_weight, residual, scale_two, send_rows = call(
        residual_kernel,
        [place_at, mixed, *o_own, *o_other, inputs[0], gain_two, one_hot],
        [(square, BF), ((tok, width), F32), ((tok, HEAD_DIM), F32), ((slots_all, width), BF)],
    )

    send_rows, arrived_grad = tie(send_rows, arrived_grad)
    arrived = exchange(send_rows, "fsdp")
    grad_hidden = dot_t(arrived_grad, down_weight[0])
    arrived, grad_hidden = tie(arrived, grad_hidden)
    hidden, grad_pre, grad_rows = call(
        expert_kernel,
        [place_at, arrived, grad_hidden, gate_weight[0], up_weight[0]],
        [((slots_all, half), BF), ((2, slots_all, half), BF), ((slots_all, width), BF)],
    )
    back_rows = exchange(grad_rows, "fsdp")
    expert_rows = width + half

    e_sent = call(
        sent_expert_kernel,
        [place_at, arrived, grad_pre, hidden, arrived_grad],
        [((expert_rows, half), BF)],
        micros=40,
    )[0]
    e_part = (2, expert_rows // 8, half)
    e_keep_a, e_send_a, e_keep_b, e_send_b, expert_out = call(
        own_expert_kernel,
        [place_at, arrived, grad_pre, hidden, arrived_grad, swap(e_sent), down_weight[0]],
        [(e_part, BF)] * 4 + [((slots_all, width), BF)],
        [pltpu.VMEM((expert_rows, half), BF)],
    )
    e_got_a, e_got_b = flip(e_send_a, PAIRS_S), flip(e_send_b, PAIRS_T)
    back_rows, expert_out, e_keep_a, e_keep_b = tie(back_rows, expert_out, e_keep_a, e_keep_b)

    grad_residual, grad_attended, gain_two_part, grad_query_pre, kv_back = call(
        back_kernel,
        [place_at, back_rows, one_hot_t, residual, scale_two, gain_two, cotangent[0],
         output_weight, probs, kv_all, query_rot, cosine, sine],
        [((tok, width), F32), ((tok, width), BF), ((1, width), F32), ((tok, width), BF),
         ((length, 2 * kv_width), BF)],
    )
    kv_back, e_got_a, e_got_b = tie(kv_back, e_got_a, e_got_b)
    kv_got = exchange(kv_back, "fsdp")
    e_keep_a, e_send_a, e_keep_b, e_send_b = call(
        expert_step_kernel,
        [place_at, e_keep_a, e_got_a, e_keep_b, e_got_b],
        [(e_part[1:], BF)] * 4,
    )
    e_got_a, e_got_b = flip(e_send_a, PAIRS_T), flip(e_send_b, PAIRS_S)

    def square_weights(own, micros):
        def kernel(*refs):
            square_weight_kernel(own, *refs)

        return call(
            kernel,
            [place_at, mixed, grad_attended, normed, grad_query_pre],
            [((2, width, half), BF)],
            micros=micros,
        )[0]

    qo_got = swap(square_weights(False, 30))
    qo_own = square_weights(True, 0)
    big_part, small_part = (groups, 2, quarter, half), (groups, 2, quarter, kv_width // 2)
    qo_keep_a, qo_send_a, qo_keep_b, qo_send_b = call(
        split_kernel,
        [place_at, qo_own[0], qo_got[0], qo_own[1], qo_got[1]],
        [(big_part, BF)] * 4,
    )
    kv_got, expert_out, qo_send_a, qo_send_b, e_got_a, e_got_b = tie(
        kv_got, expert_out, qo_send_a, qo_send_b, e_got_a, e_got_b
    )
    qo_got_a, qo_got_b = flip(qo_send_a, PAIRS_S), flip(qo_send_b, PAIRS_T)
    returned = exchange(expert_out, "fsdp")
    kv_grad_own, kv_grad_sent, grad_kv_pre = call(
        key_weight_kernel,
        [place_at, kv_got.reshape(groups, tok, 2 * kv_width), cosine, sine, normed],
        [((2, width, kv_width // 2), BF)] * 2 + [((tok, 2 * kv_width), BF)],
        micros=30,
    )
    kv_grad_got = swap(kv_grad_sent)
    kv_keep_a, kv_send_a, kv_keep_b, kv_send_b = call(
        split_kernel,
        [place_at, kv_grad_own[0], kv_grad_got[0], kv_grad_own[1], kv_grad_got[1]],
        [(small_part, BF)] * 4,
    )
    kv_got_a, kv_got_b = flip(kv_send_a, PAIRS_S), flip(kv_send_b, PAIRS_T)
    e_sum = call(
        expert_end_kernel,
        [place_at, e_keep_a, e_got_a, e_keep_b, e_got_b],
        [(e_part, BF)],
    )[0]
    e_other_y = swap_y(e_sum)
    input_grad, gain_one_part = call(
        input_kernel,
        [place_at, grad_query_pre, grad_kv_pre, inputs[0], scale_one, gain_one, query_weight,
         kv_weight, grad_residual],
        [((tok, width), BF), ((1, width), F32)],
    )

    both_part = (groups, quarter, half + kv_width // 2)
    keep_a, send_a, keep_b, send_b = call(
        step_kernel,
        [place_at, qo_keep_a, qo_got_a, kv_keep_a, kv_got_a, qo_keep_b, qo_got_b, kv_keep_b,
         kv_got_b],
        [(both_part, BF)] * 4,
    )
    got_a, got_b = flip(send_a, PAIRS_T), flip(send_b, PAIRS_S)
    spare = HEAD_DIM
    gain_parts = jnp.stack([gain_one_part, gain_two_part]).reshape(2, groups, quarter, XS)
    gain_parts = gain_parts.transpose(1, 2, 0, 3).reshape(groups, quarter, 2 * XS).astype(BF)
    gain_parts = jnp.pad(gain_parts, ((0, 0), (0, 0), (0, spare - 2 * XS)))
    packed_width = both_part[-1] + spare
    packed = call(
        pack_kernel,
        [place_at, keep_a, got_a, keep_b, got_b, gain_parts],
        [((YLO, groups, quarter, packed_width), BF)],
    )[0]
    packed, returned, e_sum, e_other_y = tie(packed, returned, e_sum, e_other_y)
    packed = exchange(packed.reshape(YLO * groups, quarter, packed_width), ("ylo", "fsdp"))
    e_sum = call(pair_kernel, [place_at, e_sum, e_other_y], [(e_part, BF)])[0]
    e_one_a, e_one_b = flip(e_sum[0], PAIRS_T), flip(e_sum[1], PAIRS_S)
    e_two_a = flip(jnp.stack([e_sum[0], e_one_a]), PAIRS_S)
    e_two_b = flip(jnp.stack([e_sum[1], e_one_b]), PAIRS_T)
    e_pieces = [e_sum, e_one_a, e_one_b, e_two_a, e_two_b]
    grad_gate, grad_up, grad_down = call(
        expert_out_kernel,
        [place_at, *e_pieces, *[swap(v) for v in e_pieces]],
        [((width, half), F32), ((width, half), F32), ((half, width), F32)],
    )
    mixture = t_dot(gate_high, returned) + t_dot(gate_low, returned)
    outputs = (residual + mixture).astype(BF)
    packed = call(sum_kernel, [place_at, packed], [((YLO * XS, quarter, packed_width), BF)])[0]
    spreaded = exchange(packed, ("ylo", "x"))
    grad_output_w, grad_query_w, grad_key_w, grad_value_w, gains_sum = call(
        final_kernel,
        [place_at, spreaded, swap(spreaded)],
        [((rows, width), F32), ((rows, width), F32), ((rows, kv_width), F32),
         ((rows, kv_width), F32), ((quarter, spare), F32)],
    )
    gains_sum = gains_sum[:, : 2 * XS].reshape(quarter, 2, XS).transpose(1, 0, 2)
    gains_sum = gains_sum.reshape(2, rows)
    return (
        outputs[None],
        input_grad[None],
        gains_sum[0],
        grad_query_w,
        grad_key_w,
        grad_value_w,
        grad_output_w,
        gains_sum[1],
        grad_gate[None],
        grad_up[None],
        grad_down[None],
    )


def solution(mesh):
    shape = mesh.devices.shape
    fine = Mesh(
        mesh.devices.reshape(YLO, XS, CORES, shape[1]), ("ylo", "x", "core", "fsdp")
    )
    return jax.shard_map(
        body,
        mesh=fine,
        in_specs=(
            P(REP, "fsdp", None),
            P(REP, None),
            P("fsdp"),
            P("fsdp", None),
            P("fsdp", None),
            P("fsdp", None),
            P("fsdp", None),
            P("fsdp"),
            P(REP, "fsdp", None),
            P(REP, "fsdp", None),
            P(REP, "fsdp", None),
            P("fsdp", None, None),
            P("fsdp", None, None),
            P("fsdp", None, None),
            P(REP, "fsdp", None),
        ),
        out_specs=(
            P(REP, "fsdp", None),
            P(REP, "fsdp", None),
            P("fsdp"),
            P("fsdp", None),
            P("fsdp", None),
            P("fsdp", None),
            P("fsdp", None),
            P("fsdp"),
            P("fsdp", None, None),
            P("fsdp", None, None),
            P("fsdp", None, None),
        ),
        check_vma=False,
    )
```

profile of v0, /device:TPU:1, one launch (start us, length us, event | category | flops | bytes accessed | tf_op | source)
XLA Modules:
  0.0 427.9 jit_solution(9357196005848196559)
XLA Ops:
  5.6 8.6 %all-to-all-start = ((bf16[8,88,1536]{2,1,0:T(8,128)(2,1)}), bf16[8,88,1536]{2,1,0:T(8,128)(2,1)S(1)}, u32[]{:S(2)}, u32[]{:S(2)}) async-start(bf16[8,88,1536]{2,1,0:T(8,128)(2,1)} %broadcast_in_dim.79), calls=%async_computation | async-start | bytes 4325376 | tf_op jit(solution)/shard_map/all_to_all | solution.py:450
  21.9 20.5 %all-to-all-done = bf16[8,88,1536]{2,1,0:T(8,128)(2,1)S(1)} async-done(((bf16[8,88,1536]{2,1,0:T(8,128)(2,1)}), bf16[8,88,1536]{2,1,0:T(8,128)(2,1)S(1)}, u32[]{:S(2)}, u32[]{:S(2)}) %all-to-all-start) | async-done | bytes 2162720 | tf_op jit(solution)/shard_map/all_to_all | solution.py:450
  42.4 4.4 %all-to-all-start.1 = ((bf16[8,48,1536]{2,1,0:T(8,128)(2,1)}), bf16[8,48,1536]{2,1,0:T(8,128)(2,1)}, u32[]{:S(2)}, u32[]{:S(2)}) async-start(bf16[8,48,1536]{2,1,0:T(8,128)(2,1)} %broadcast_in_dim.80), calls=%async_computation.1 | async-start | bytes 2359296 | tf_op jit(solution)/shard_map/all_to_all | solution.py:450
  58.1 5.2 %all-to-all-done.1 = bf16[8,48,1536]{2,1,0:T(8,128)(2,1)} async-done(((bf16[8,48,1536]{2,1,0:T(8,128)(2,1)}), bf16[8,48,1536]{2,1,0:T(8,128)(2,1)}, u32[]{:S(2)}, u32[]{:S(2)}) %all-to-all-start.1) | async-done | bytes 1179680 | tf_op jit(solution)/shard_map/all_to_all | solution.py:450
  72.0 10.5 %all-to-all-done.2 = bf16[8,128,512]{2,1,0:T(8,128)(2,1)S(1)} async-done(((bf16[8,128,512]{2,1,0:T(8,128)(2,1)}), bf16[8,128,512]{2,1,0:T(8,128)(2,1)S(1)}, u32[]{:S(2)}, u32[]{:S(2)}) %all-to-all-start.2) | async-done | bytes 1048608 | tf_op jit(solution)/shard_map/all_to_all | solution.py:450
  82.5 4.3 %all-to-all-start.3 = ((bf16[8,80,1536]{2,1,0:T(8,128)(2,1)}), bf16[8,80,1536]{2,1,0:T(8,128)(2,1)}, u32[]{:S(2)}, u32[]{:S(2)}) async-start(bf16[8,80,1536]{2,1,0:T(8,128)(2,1)} %bitcast.91), calls=%async_computation.3 | async-start | bytes 3932160 | tf_op jit(solution)/shard_map/all_to_all | solution.py:450
  118.7 4.8 %shard_map.231 = (bf16[1536,1536]{1,0:T(8,128)(2,1)}, bf16[128,1536]{1,0:T(8,128)(2,1)S(1)}) custom-call(s32[4]{0:T(128)S(1)} %pad_add_fusion.place.refs_0_, bf16[128,1536]{1,0:T(8,128)(2,1)S(1)} %copy-done.21, bf16[8,48,768]{2,1,0:T(8,128)(2,1)S(1)} %get-tuple-element.200.a, bf16[8,48,768]{2,1,0:T(8,128)(2,1)S(1)} %copy-done.9, ...), custom_call_target="tpu_custom_call" | custom-call | tf_op jit(solution)/shard_map/pallas_call | solution.py:429
  123.5 4.3 %shard_map.232 = (bf16[128,1536]{1,0:T(8,128)(2,1)S(1)}, bf16[12,1024,128]{2,1,0:T(8,128)(2,1)S(1)}) custom-call(s32[4]{0:T(128)S(1)} %pad_add_fusion.place.refs_0_, bf16[128,1536]{1,0:T(8,128)(2,1)S(1)} %get-tuple-element.109.q, bf16[1024,512]{1,0:T(8,128)(2,1)S(1)} %bitcast.82, s32[1,128]{1,0:T(1,128)S(1)} %constant_dynamic-slice_fusion.seg_row, ...), custom_call_target="tpu_custom_call" | custom-call | tf_op jit(solution)/shard_map/pallas_call | solution.py:429
  129.6 5.4 %shard_map.233 = (bf16[1536,1536]{1,0:T(8,128)(2,1)}, f32[128,1536]{1,0:T(8,128)}, f32[128,128]{1,0:T(8,128)S(1)}, bf16[640,1536]{1,0:T(8,128)(2,1)}) custom-call(s32[4]{0:T(128)S(1)} %pad_add_fusion.place.refs_0_, bf16[128,1536]{1,0:T(8,128)(2,1)S(1)} %get-tuple-element.114.mixed.refs_1_, bf16[8,48,768]{2,1,0:T(8,128)(2,1)S(1)} %get-tuple-element.199.a, ...), custom_call_target="tpu_custom_call" | custom-call | tf_op jit(solution)/shard_map/pallas_call | solution.py:429
  136.3 7.4 %all-to-all-start.4 = ((bf16[8,80,1536]{2,1,0:T(8,128)(2,1)}), bf16[8,80,1536]{2,1,0:T(8,128)(2,1)S(1)}, u32[]{:S(2)}, u32[]{:S(2)}) async-start(bf16[8,80,1536]{2,1,0:T(8,128)(2,1)} %bitcast.96), calls=%async_computation.4 | async-start | bytes 3932160 | tf_op jit(solution)/shard_map/all_to_all | solution.py:450
  143.7 5.2 %fusion.11.grad_hidden = f32[640,768]{1,0:T(8,128)} fusion(bf16[640,1536]{1,0:T(8,128)(2,1)} %bitcast.18.arrived, bf16[1,768,1536]{2,1,0:T(8,128)(2,1)} %param.28), kind=kOutput, calls=%fused_computation.60 | convolution fusion | flops 1509949440 | bytes 6291456 | tf_op jit(solution)/shard_map/dot_general | solution.py:41
  148.9 21.1 %all-to-all-done.4 = bf16[8,80,1536]{2,1,0:T(8,128)(2,1)S(1)} async-done(((bf16[8,80,1536]{2,1,0:T(8,128)(2,1)}), bf16[8,80,1536]{2,1,0:T(8,128)(2,1)S(1)}, u32[]{:S(2)}, u32[]{:S(2)}) %all-to-all-start.4) | async-done | bytes 1966112 | tf_op jit(solution)/shard_map/all_to_all | solution.py:450
  171.3 11.6 %shard_map.234 = (bf16[640,768]{1,0:T(8,128)(2,1)S(1)}, bf16[2,640,768]{2,1,0:T(8,128)(2,1)S(1)}, bf16[640,1536]{1,0:T(8,128)(2,1)}) custom-call(s32[4]{0:T(128)S(1)} %pad_add_fusion.place.refs_0_, bf16[640,1536]{1,0:T(8,128)(2,1)} %bitcast.79, f32[640,768]{1,0:T(8,128)} %fusion.11.grad_hidden, bf16[1536,768]{1,0:T(8,128)(2,1)} %bitcast.93, ...), custom_call_target="tpu_custom_call" | custom-call | tf_op jit(solution)/shard_map/pallas_call | solution.py:429
  185.5 6.3 %shard_map.235 = bf16[2304,768]{1,0:T(8,128)(2,1)} custom-call(s32[4]{0:T(128)S(1)} %pad_add_fusion.place.refs_0_, bf16[640,1536]{1,0:T(8,128)(2,1)S(1)} %bitcast.81, bf16[2,640,768]{2,1,0:T(8,128)(2,1)S(1)} %get-tuple-element.125.pre, bf16[640,768]{1,0:T(8,128)(2,1)S(1)} %get-tuple-element.126.hidden, bf16[640,1536]{1,0:T(8,128)(2,1)} %bitcast.18.arrived), custom_call_target="tpu_custom_call" | custom-call | flops 40000000000 | tf_op jit(solution)/shard_map/pallas_call | solution.py:429
  193.5 4.5 %all-to-all-start.5 = ((bf16[8,80,1536]{2,1,0:T(8,128)(2,1)}), bf16[8,80,1536]{2,1,0:T(8,128)(2,1)}, u32[]{:S(2)}, u32[]{:S(2)}) async-start(bf16[8,80,1536]{2,1,0:T(8,128)(2,1)} %bitcast.24), calls=%async_computation.5 | async-start | bytes 3932160 | tf_op jit(solution)/shard_map/all_to_all | solution.py:450
  200.9 10.7 %shard_map.236 = (bf16[2,288,768]{2,1,0:T(8,128)(2,1)S(1)}, bf16[2,288,768]{2,1,0:T(8,128)(2,1)S(1)}, bf16[2,288,768]{2,1,0:T(8,128)(2,1)S(1)}, bf16[2,288,768]{2,1,0:T(8,128)(2,1)S(1)}, bf16[640,1536]{1,0:T(8,128)(2,1)}) custom-call(s32[4]{0:T(128)S(1)} %pad_add_fusion.place.refs_0_, bf16[640,1536]{1,0:T(8,128)(2,1)} %bitcast.80, ...), custom_call_target="tpu_custom_call" | custom-call | tf_op jit(solution)/shard_map/pallas_call | solution.py:429
  215.4 9.9 %all-to-all-done.5 = bf16[8,80,1536]{2,1,0:T(8,128)(2,1)} async-done(((bf16[8,80,1536]{2,1,0:T(8,128)(2,1)}), bf16[8,80,1536]{2,1,0:T(8,128)(2,1)}, u32[]{:S(2)}, u32[]{:S(2)}) %all-to-all-start.5) | async-done | bytes 1966112 | tf_op jit(solution)/shard_map/all_to_all | solution.py:450
  227.0 12.9 %shard_map.237 = (f32[128,1536]{1,0:T(8,128)S(1)}, bf16[128,1536]{1,0:T(8,128)(2,1)S(1)}, f32[1,1536]{1,0:T(1,128)S(1)}, bf16[128,1536]{1,0:T(8,128)(2,1)S(1)}, bf16[1024,512]{1,0:T(8,128)(2,1)}) custom-call(s32[4]{0:T(128)S(1)} %pad_add_fusion.place.refs_0_, bf16[640,1536]{1,0:T(8,128)(2,1)} %bitcast.25.back, bf16[128,640]{1,0:T(8,128)(2,1)S(1)} %copy-done.40, ...), custom_call_target="tpu_custom_call" | custom-call | tf_op jit(solution)/shard_map/pallas_call | solution.py:429
  251.2 15.1 %collective-permute-done.15.got_a = bf16[2,288,768]{2,1,0:T(8,128)(2,1)S(1)} collective-permute-done((bf16[2,288,768]{2,1,0:T(8,128)(2,1)S(1)}, bf16[2,288,768]{2,1,0:T(8,128)(2,1)S(1)}, u32[]{:S(2)}, u32[]{:S(2)}) %collective-permute-start.15) | collective-permute-done | bytes 884768 | tf_op jit(solution)/shard_map/ppermute | solution.py:472
  272.0 5.0 %slice_bitcast_fusion.1 = (bf16[1536,768]{1,0:T(8,128)(2,1)}, bf16[1536,768]{1,0:T(8,128)(2,1)}) fusion(bf16[2,1536,768]{2,1,0:T(8,128)(2,1)} %shard_map.238), kind=kLoop, calls=%fused_computation.5 | loop fusion | bytes 9437184 | tf_op jit(solution)/shard_map/squeeze | solution.py:668
  279.9 4.9 %slice_bitcast_fusion = (bf16[1536,768]{1,0:T(8,128)(2,1)}, bf16[1536,768]{1,0:T(8,128)(2,1)}) fusion(bf16[2,1536,768]{2,1,0:T(8,128)(2,1)} %collective-permute-done.14), kind=kLoop, calls=%fused_computation.4 | loop fusion | bytes 9437184 | tf_op jit(solution)/shard_map/squeeze | solution.py:668
  284.7 6.2 %shard_map.240 = (bf16[8,2,48,768]{3,2,1,0:T(8,128)(2,1)S(1)}, bf16[8,2,48,768]{3,2,1,0:T(8,128)(2,1)}, bf16[8,2,48,768]{3,2,1,0:T(8,128)(2,1)S(1)}, bf16[8,2,48,768]{3,2,1,0:T(8,128)(2,1)}) custom-call(s32[4]{0:T(128)S(1)} %pad_add_fusion.place.refs_0_, bf16[1536,768]{1,0:T(8,128)(2,1)} %get-tuple-element.198.own_a, ...), custom_call_target="tpu_custom_call" | custom-call | tf_op jit(solution)/shard_map/pallas_call | solution.py:429
  300.1 6.8 %all-to-all-start.7 = ((bf16[8,80,1536]{2,1,0:T(8,128)(2,1)}), bf16[8,80,1536]{2,1,0:T(8,128)(2,1)}, u32[]{:S(2)}, u32[]{:S(2)}) async-start(bf16[8,80,1536]{2,1,0:T(8,128)(2,1)} %bitcast.95), calls=%async_computation.7 | async-start | bytes 3932160 | tf_op jit(solution)/shard_map/all_to_all | solution.py:450
  312.4 17.7 %collective-permute-done.21.kg_a = bf16[8,2,48,128]{3,2,1,0:T(8,128)(2,1)S(1)} collective-permute-done((bf16[8,2,48,128]{3,2,1,0:T(8,128)(2,1)S(1)}, bf16[8,2,48,128]{3,2,1,0:T(8,128)(2,1)S(1)}, u32[]{:S(2)}, u32[]{:S(2)}) %collective-permute-start.21) | collective-permute-done | bytes 196640 | tf_op jit(solution)/shard_map/ppermute | solution.py:472
  341.6 5.7 %shard_map.245 = (bf16[128,1536]{1,0:T(8,128)(2,1)}, f32[1,1536]{1,0:T(1,128)S(1)}) custom-call(s32[4]{0:T(128)S(1)} %pad_add_fusion.place.refs_0_, bf16[128,1536]{1,0:T(8,128)(2,1)S(1)} %get-tuple-element.136.refs_4_.query, bf16[128,512]{1,0:T(8,128)(2,1)S(1)} %copy-done.56, bf16[128,1536]{1,0:T(8,128)(2,1)S(1)} %bitcast.86, f32[128,128]{1,0:T(8,128)S(1)} %copy-done.58, ...), custom_call_target="tpu_custom_call" | custom-call | tf_op jit(solution)/shard_map/pallas_call | solution.py:429
  347.8 7.4 %collective-permute-done.24.got_a = bf16[8,48,896]{2,1,0:T(8,128)(2,1)} collective-permute-done((bf16[8,48,896]{2,1,0:T(8,128)(2,1)}, bf16[8,48,896]{2,1,0:T(8,128)(2,1)}, u32[]{:S(2)}, u32[]{:S(2)}) %collective-permute-start.24) | collective-permute-done | bytes 688160 | tf_op jit(solution)/shard_map/ppermute | solution.py:472
  358.0 7.1 %all-to-all-start.8 = ((bf16[16,48,1024]{2,1,0:T(8,128)(2,1)}), bf16[16,48,1024]{2,1,0:T(8,128)(2,1)S(1)}, u32[]{:S(2)}, u32[]{:S(2)}) async-start(bf16[16,48,1024]{2,1,0:T(8,128)(2,1)} %bitcast.43), calls=%async_computation.8 | async-start | bytes 3145728 | tf_op jit(solution)/shard_map/all_to_all | solution.py:450
  368.2 7.9 %collective-permute-done.29.refs_2_ = bf16[288,768]{1,0:T(8,128)(2,1)S(1)} collective-permute-done((bf16[288,768]{1,0:T(8,128)(2,1)S(1)}, bf16[288,768]{1,0:T(8,128)(2,1)S(1)}, u32[]{:S(2)}, u32[]{:S(2)}) %collective-permute-start.29) | collective-permute-done | bytes 442400 | tf_op jit(solution)/shard_map/ppermute | solution.py:472
  379.0 6.0 %all-to-all-done.8.parts = bf16[16,48,1024]{2,1,0:T(8,128)(2,1)S(1)} async-done(((bf16[16,48,1024]{2,1,0:T(8,128)(2,1)}), bf16[16,48,1024]{2,1,0:T(8,128)(2,1)S(1)}, u32[]{:S(2)}, u32[]{:S(2)}) %all-to-all-start.8) | async-done | bytes 1572896 | tf_op jit(solution)/shard_map/all_to_all | solution.py:450
  396.5 8.4 %collective-permute-start.36 = (bf16[2,288,768]{2,1,0:T(8,128)(2,1)}, bf16[2,288,768]{2,1,0:T(8,128)(2,1)}, u32[]{:S(2)}, u32[]{:S(2)}) collective-permute-start(bf16[2,288,768]{2,1,0:T(8,128)(2,1)} %collective-permute-done.31.refs_4_), channel_id=1, source_target_pairs={{0,8},{8,0},{1,9},{9,1},{2,10},{10,2},{3,11},{11,3},{4,12},{12,4},... | collective-permute-start | bytes 2654216 | tf_op jit(solution)/shard_map/ppermute | solution.py:442
  405.6 4.4 %collective-permute-start.27 = (bf16[8,48,1024]{2,1,0:T(8,128)(2,1)S(1)}, bf16[8,48,1024]{2,1,0:T(8,128)(2,1)S(1)}, u32[]{:S(2)}, u32[]{:S(2)}) collective-permute-start(bf16[8,48,1024]{2,1,0:T(8,128)(2,1)S(1)} %all-to-all-done.9.own), channel_id=1, source_target_pairs={{0,8},{8,0},{1,9},{9,1},{2,10},{10,2},{3,11},{11,3},{4,12},{12,4},... | collective-permute-start | bytes 2359304 | tf_op jit(solution)/shard_map/ppermute | solution.py:442
  415.3 8.3 %shard_map.251 = (f32[1536,768]{1,0:T(8,128)}, f32[1536,768]{1,0:T(8,128)}, f32[768,1536]{1,0:T(8,128)}) custom-call(s32[4]{0:T(128)S(1)} %pad_add_fusion.place.refs_0_, bf16[2,288,768]{2,1,0:T(8,128)(2,1)S(1)} %shard_map.250.refs_0_, bf16[288,768]{1,0:T(8,128)(2,1)S(1)} %collective-permute-done.28.refs_1_, ...), custom_call_target="tpu_custom_call" | custom-call | tf_op jit(solution)/shard_map/pallas_call | solution.py:429
  (317 shorter events, 157.5 us)
Async XLA Ops:
  5.6 36.9 %all-to-all-start = ((bf16[8,88,1536]{2,1,0:T(8,128)(2,1)}), bf16[8,88,1536]{2,1,0:T(8,128)(2,1)S(1)}, u32[]{:S(2)}, u32[]{:S(2)}) async-start(bf16[8,88,1536]{2,1,0:T(8,128)(2,1)} %broadcast_in_dim.79), calls=%async_computation | async-start | bytes 4325376 | tf_op jit(solution)/shard_map/all_to_all | solution.py:450
  42.4 20.8 %all-to-all-start.1 = ((bf16[8,48,1536]{2,1,0:T(8,128)(2,1)}), bf16[8,48,1536]{2,1,0:T(8,128)(2,1)}, u32[]{:S(2)}, u32[]{:S(2)}) async-start(bf16[8,48,1536]{2,1,0:T(8,128)(2,1)} %broadcast_in_dim.80), calls=%async_computation.1 | async-start | bytes 2359296 | tf_op jit(solution)/shard_map/all_to_all | solution.py:450
  63.3 19.2 %all-to-all-start.2 = ((bf16[8,128,512]{2,1,0:T(8,128)(2,1)}), bf16[8,128,512]{2,1,0:T(8,128)(2,1)S(1)}, u32[]{:S(2)}, u32[]{:S(2)}) async-start(bf16[8,128,512]{2,1,0:T(8,128)(2,1)} %copy-done.25), calls=%async_computation.2 | async-start | bytes 2097152 | tf_op jit(solution)/shard_map/all_to_all | solution.py:450
  68.9 24.1 %collective-permute-start.1 = (bf16[8,48,768]{2,1,0:T(8,128)(2,1)S(1)}, bf16[8,48,768]{2,1,0:T(8,128)(2,1)}, u32[]{:S(2)}, u32[]{:S(2)}) collective-permute-start(bf16[8,48,768]{2,1,0:T(8,128)(2,1)S(1)} %get-tuple-element.200.a), channel_id=1, source_target_pairs={{0,16},{16,0},{32,48},{48,32},{1,17},{17,1},{33,49},{49,33},{2,18}... | collective-permute-start | bytes 1769480 | tf_op jit(solution)/shard_map/ppermute | solution.py:472
  70.2 24.6 %collective-permute-start.7 = (bf16[8,48,768]{2,1,0:T(8,128)(2,1)S(1)}, bf16[8,48,768]{2,1,0:T(8,128)(2,1)}, u32[]{:S(2)}, u32[]{:S(2)}) collective-permute-start(bf16[8,48,768]{2,1,0:T(8,128)(2,1)S(1)} %get-tuple-element.199.a), channel_id=1, source_target_pairs={{0,48},{48,0},{16,32},{32,16},{1,49},{49,1},{17,33},{33,17},{2,50}... | collective-permute-start | bytes 1769480 | tf_op jit(solution)/shard_map/ppermute | solution.py:472
  82.5 53.8 %all-to-all-start.3 = ((bf16[8,80,1536]{2,1,0:T(8,128)(2,1)}), bf16[8,80,1536]{2,1,0:T(8,128)(2,1)}, u32[]{:S(2)}, u32[]{:S(2)}) async-start(bf16[8,80,1536]{2,1,0:T(8,128)(2,1)} %bitcast.91), calls=%async_computation.3 | async-start | bytes 3932160 | tf_op jit(solution)/shard_map/all_to_all | solution.py:450
  93.0 15.7 %collective-permute-start.8 = (bf16[8,48,768]{2,1,0:T(8,128)(2,1)S(1)}, bf16[8,48,768]{2,1,0:T(8,128)(2,1)}, u32[]{:S(2)}, u32[]{:S(2)}) collective-permute-start(bf16[8,48,768]{2,1,0:T(8,128)(2,1)S(1)} %get-tuple-element.201.b), channel_id=1, source_target_pairs={{0,48},{48,0},{16,32},{32,16},{1,49},{49,1},{17,33},{33,17},{2,50}... | collective-permute-start | bytes 1769480 | tf_op jit(solution)/shard_map/ppermute | solution.py:472
  104.9 24.6 %collective-permute-start.9 = (bf16[8,48,768]{2,1,0:T(8,128)(2,1)S(1)}, bf16[8,48,768]{2,1,0:T(8,128)(2,1)}, u32[]{:S(2)}, u32[]{:S(2)}) collective-permute-start(bf16[8,48,768]{2,1,0:T(8,128)(2,1)S(1)} %get-tuple-element.199.a), channel_id=1, source_target_pairs={{0,8},{8,0},{1,9},{9,1},{2,10},{10,2},{3,11},{11,3},{4,12},{12,4},... | collective-permute-start | bytes 1769480 | tf_op jit(solution)/shard_map/ppermute | solution.py:442
  105.7 23.8 %collective-permute-start.11 = (bf16[8,48,768]{2,1,0:T(8,128)(2,1)}, bf16[8,48,768]{2,1,0:T(8,128)(2,1)}, u32[]{:S(2)}, u32[]{:S(2)}) collective-permute-start(bf16[8,48,768]{2,1,0:T(8,128)(2,1)} %collective-permute-done.7.c), channel_id=1, source_target_pairs={{0,8},{8,0},{1,9},{9,1},{2,10},{10,2},{3,11},{11,3},{4,12},{12,4},... | collective-permute-start | bytes 1769480 | tf_op jit(solution)/shard_map/ppermute | solution.py:442
  108.7 20.8 %collective-permute-start.10 = (bf16[8,48,768]{2,1,0:T(8,128)(2,1)S(1)}, bf16[8,48,768]{2,1,0:T(8,128)(2,1)}, u32[]{:S(2)}, u32[]{:S(2)}) collective-permute-start(bf16[8,48,768]{2,1,0:T(8,128)(2,1)S(1)} %get-tuple-element.201.b), channel_id=1, source_target_pairs={{0,8},{8,0},{1,9},{9,1},{2,10},{10,2},{3,11},{11,3},{4,12},{12,4},... | collective-permute-start | bytes 1769480 | tf_op jit(solution)/shard_map/ppermute | solution.py:442
  110.9 18.7 %collective-permute-start.12 = (bf16[8,48,768]{2,1,0:T(8,128)(2,1)}, bf16[8,48,768]{2,1,0:T(8,128)(2,1)}, u32[]{:S(2)}, u32[]{:S(2)}) collective-permute-start(bf16[8,48,768]{2,1,0:T(8,128)(2,1)} %collective-permute-done.8.d), channel_id=1, source_target_pairs={{0,8},{8,0},{1,9},{9,1},{2,10},{10,2},{3,11},{11,3},{4,12},{12,4},... | collective-permute-start | bytes 1769480 | tf_op jit(solution)/shard_map/ppermute | solution.py:442
  136.3 33.7 %all-to-all-start.4 = ((bf16[8,80,1536]{2,1,0:T(8,128)(2,1)}), bf16[8,80,1536]{2,1,0:T(8,128)(2,1)S(1)}, u32[]{:S(2)}, u32[]{:S(2)}) async-start(bf16[8,80,1536]{2,1,0:T(8,128)(2,1)} %bitcast.96), calls=%async_computation.4 | async-start | bytes 3932160 | tf_op jit(solution)/shard_map/all_to_all | solution.py:450
  193.5 31.7 %all-to-all-start.5 = ((bf16[8,80,1536]{2,1,0:T(8,128)(2,1)}), bf16[8,80,1536]{2,1,0:T(8,128)(2,1)}, u32[]{:S(2)}, u32[]{:S(2)}) async-start(bf16[8,80,1536]{2,1,0:T(8,128)(2,1)} %bitcast.24), calls=%async_computation.5 | async-start | bytes 3932160 | tf_op jit(solution)/shard_map/all_to_all | solution.py:450
  244.1 35.8 %collective-permute-start.14 = (bf16[2,1536,768]{2,1,0:T(8,128)(2,1)}, bf16[2,1536,768]{2,1,0:T(8,128)(2,1)}, u32[]{:S(2)}, u32[]{:S(2)}) collective-permute-start(bf16[2,1536,768]{2,1,0:T(8,128)(2,1)} %shard_map.239), channel_id=1, source_target_pairs={{0,8},{8,0},{1,9},{9,1},{2,10},{10,2},{3,11},{11,3},{4,12},{12,4},... | collective-permute-start | bytes 14155784 | tf_op jit(solution)/shard_map/ppermute | solution.py:442
  245.0 21.4 %collective-permute-start.15 = (bf16[2,288,768]{2,1,0:T(8,128)(2,1)S(1)}, bf16[2,288,768]{2,1,0:T(8,128)(2,1)S(1)}, u32[]{:S(2)}, u32[]{:S(2)}) collective-permute-start(bf16[2,288,768]{2,1,0:T(8,128)(2,1)S(1)} %copy-done.68), channel_id=1, source_target_pairs={{0,16},{16,0},{32,48},{48,32},{1,17},{17,1},{33,49},{49,33},{2,18}... | collective-permute-start | bytes 2654216 | tf_op jit(solution)/shard_map/ppermute | solution.py:472
  245.2 22.5 %collective-permute-start.16 = (bf16[2,288,768]{2,1,0:T(8,128)(2,1)S(1)}, bf16[2,288,768]{2,1,0:T(8,128)(2,1)S(1)}, u32[]{:S(2)}, u32[]{:S(2)}) collective-permute-start(bf16[2,288,768]{2,1,0:T(8,128)(2,1)S(1)} %copy-done.66), channel_id=1, source_target_pairs={{0,48},{48,0},{16,32},{32,16},{1,49},{49,1},{17,33},{33,17},{2,50}... | collective-permute-start | bytes 2654216 | tf_op jit(solution)/shard_map/ppermute | solution.py:472
  267.7 25.8 %all-to-all-start.6 = ((bf16[8,128,512]{2,1,0:T(8,128)(2,1)}), bf16[8,128,512]{2,1,0:T(8,128)(2,1)}, u32[]{:S(2)}, u32[]{:S(2)}) async-start(bf16[8,128,512]{2,1,0:T(8,128)(2,1)} %bitcast.30), calls=%async_computation.6 | async-start | bytes 2097152 | tf_op jit(solution)/shard_map/all_to_all | solution.py:450
  297.5 34.8 %collective-permute-start.19 = (bf16[8,2,48,768]{3,2,1,0:T(8,128)(2,1)}, bf16[8,2,48,768]{3,2,1,0:T(8,128)(2,1)}, u32[]{:S(2)}, u32[]{:S(2)}) collective-permute-start(bf16[8,2,48,768]{3,2,1,0:T(8,128)(2,1)} %get-tuple-element.151), channel_id=1, source_target_pairs={{0,16},{16,0},{32,48},{48,32},{1,17},{17,1},{33,49},{49,33},{2,18}... | collective-permute-start | bytes 3538952 | tf_op jit(solution)/shard_map/ppermute | solution.py:472
  299.3 33.0 %collective-permute-start.22 = (bf16[8,2,48,768]{3,2,1,0:T(8,128)(2,1)}, bf16[8,2,48,768]{3,2,1,0:T(8,128)(2,1)}, u32[]{:S(2)}, u32[]{:S(2)}) collective-permute-start(bf16[8,2,48,768]{3,2,1,0:T(8,128)(2,1)} %get-tuple-element.158), channel_id=1, source_target_pairs={{0,48},{48,0},{16,32},{32,16},{1,49},{49,1},{17,33},{33,17},{2,50}... | collective-permute-start | bytes 3538952 | tf_op jit(solution)/shard_map/ppermute | solution.py:472
  300.1 57.9 %all-to-all-start.7 = ((bf16[8,80,1536]{2,1,0:T(8,128)(2,1)}), bf16[8,80,1536]{2,1,0:T(8,128)(2,1)}, u32[]{:S(2)}, u32[]{:S(2)}) async-start(bf16[8,80,1536]{2,1,0:T(8,128)(2,1)} %bitcast.95), calls=%async_computation.7 | async-start | bytes 3932160 | tf_op jit(solution)/shard_map/all_to_all | solution.py:450
  309.1 21.0 %collective-permute-start.21 = (bf16[8,2,48,128]{3,2,1,0:T(8,128)(2,1)S(1)}, bf16[8,2,48,128]{3,2,1,0:T(8,128)(2,1)S(1)}, u32[]{:S(2)}, u32[]{:S(2)}) collective-permute-start(bf16[8,2,48,128]{3,2,1,0:T(8,128)(2,1)S(1)} %get-tuple-element.156), channel_id=1, source_target_pairs={{0,16},{16,0},{32,48},{48,32},{1,17},{17,1},{33,49},{49,33},{2,18}... | collective-permute-start | bytes 589832 | tf_op jit(solution)/shard_map/ppermute | solution.py:472
  309.2 23.1 %collective-permute-start.23 = (bf16[8,2,48,128]{3,2,1,0:T(8,128)(2,1)S(1)}, bf16[8,2,48,128]{3,2,1,0:T(8,128)(2,1)S(1)}, u32[]{:S(2)}, u32[]{:S(2)}) collective-permute-start(bf16[8,2,48,128]{3,2,1,0:T(8,128)(2,1)S(1)} %get-tuple-element.160), channel_id=1, source_target_pairs={{0,48},{48,0},{16,32},{32,16},{1,49},{49,1},{17,33},{33,17},{2,50}... | collective-permute-start | bytes 589832 | tf_op jit(solution)/shard_map/ppermute | solution.py:472
  311.8 46.2 %collective-permute-start.26 = (bf16[2,288,768]{2,1,0:T(8,128)(2,1)S(1)}, bf16[2,288,768]{2,1,0:T(8,128)(2,1)}, u32[]{:S(2)}, u32[]{:S(2)}) collective-permute-start(bf16[2,288,768]{2,1,0:T(8,128)(2,1)S(1)} %shard_map.247.a), channel_id=1, source_target_pairs={{0,64},{64,0},{1,65},{65,1},{2,66},{66,2},{3,67},{67,3},{4,68},{68... | collective-permute-start | bytes 2654216 | tf_op jit(solution)/shard_map/ppermute | solution.py:446
  337.7 17.5 %collective-permute-start.24 = (bf16[8,48,896]{2,1,0:T(8,128)(2,1)}, bf16[8,48,896]{2,1,0:T(8,128)(2,1)}, u32[]{:S(2)}, u32[]{:S(2)}) collective-permute-start(bf16[8,48,896]{2,1,0:T(8,128)(2,1)} %get-tuple-element.162), channel_id=1, source_target_pairs={{0,48},{48,0},{16,32},{32,16},{1,49},{49,1},{17,33},{33,17},{2,50}... | collective-permute-start | bytes 2064392 | tf_op jit(solution)/shard_map/ppermute | solution.py:472
  338.6 16.6 %collective-permute-start.25 = (bf16[8,48,896]{2,1,0:T(8,128)(2,1)}, bf16[8,48,896]{2,1,0:T(8,128)(2,1)}, u32[]{:S(2)}, u32[]{:S(2)}) collective-permute-start(bf16[8,48,896]{2,1,0:T(8,128)(2,1)} %get-tuple-element.164), channel_id=1, source_target_pairs={{0,16},{16,0},{32,48},{48,32},{1,17},{17,1},{33,49},{49,33},{2,18}... | collective-permute-start | bytes 2064392 | tf_op jit(solution)/shard_map/ppermute | solution.py:472
  358.0 27.0 %all-to-all-start.8 = ((bf16[16,48,1024]{2,1,0:T(8,128)(2,1)}), bf16[16,48,1024]{2,1,0:T(8,128)(2,1)S(1)}, u32[]{:S(2)}, u32[]{:S(2)}) async-start(bf16[16,48,1024]{2,1,0:T(8,128)(2,1)} %bitcast.43), calls=%async_computation.8 | async-start | bytes 3145728 | tf_op jit(solution)/shard_map/all_to_all | solution.py:450
  377.1 19.4 %collective-permute-start.31 = (bf16[2,288,768]{2,1,0:T(8,128)(2,1)}, bf16[2,288,768]{2,1,0:T(8,128)(2,1)}, u32[]{:S(2)}, u32[]{:S(2)}) collective-permute-start(bf16[2,288,768]{2,1,0:T(8,128)(2,1)} %pad_maximum_fusion.1), channel_id=1, source_target_pairs={{0,48},{48,0},{16,32},{32,16},{1,49},{49,1},{17,33},{33,17},{2,50}... | collective-permute-start | bytes 2654216 | tf_op jit(solution)/shard_map/ppermute | solution.py:472
  379.0 25.9 %collective-permute-start.30 = (bf16[2,288,768]{2,1,0:T(8,128)(2,1)}, bf16[2,288,768]{2,1,0:T(8,128)(2,1)}, u32[]{:S(2)}, u32[]{:S(2)}) collective-permute-start(bf16[2,288,768]{2,1,0:T(8,128)(2,1)} %pad_maximum_fusion), channel_id=1, source_target_pairs={{0,16},{16,0},{32,48},{48,32},{1,17},{17,1},{33,49},{49,33},{2,18}... | collective-permute-start | bytes 2654216 | tf_op jit(solution)/shard_map/ppermute | solution.py:472
  386.6 18.9 %all-to-all-start.9 = ((bf16[8,48,1024]{2,1,0:T(8,128)(2,1)}), bf16[8,48,1024]{2,1,0:T(8,128)(2,1)S(1)}, u32[]{:S(2)}, u32[]{:S(2)}) async-start(bf16[8,48,1024]{2,1,0:T(8,128)(2,1)} %shard_map.248), calls=%async_computation.9 | async-start | bytes 1572864 | tf_op jit(solution)/shard_map/all_to_all | solution.py:450
  390.3 19.7 %collective-permute-start.32 = (bf16[2,288,768]{2,1,0:T(8,128)(2,1)S(1)}, bf16[2,288,768]{2,1,0:T(8,128)(2,1)}, u32[]{:S(2)}, u32[]{:S(2)}) collective-permute-start(bf16[2,288,768]{2,1,0:T(8,128)(2,1)S(1)} %shard_map.250.refs_0_), channel_id=1, source_target_pairs={{0,8},{8,0},{1,9},{9,1},{2,10},{10,2},{3,11},{11,3},{4,12},{12,4},... | collective-permute-start | bytes 2654216 | tf_op jit(solution)/shard_map/ppermute | solution.py:442
  396.5 18.8 %collective-permute-start.36 = (bf16[2,288,768]{2,1,0:T(8,128)(2,1)}, bf16[2,288,768]{2,1,0:T(8,128)(2,1)}, u32[]{:S(2)}, u32[]{:S(2)}) collective-permute-start(bf16[2,288,768]{2,1,0:T(8,128)(2,1)} %collective-permute-done.31.refs_4_), channel_id=1, source_target_pairs={{0,8},{8,0},{1,9},{9,1},{2,10},{10,2},{3,11},{11,3},{4,12},{12,4},... | collective-permute-start | bytes 2654216 | tf_op jit(solution)/shard_map/ppermute | solution.py:442
  405.6 18.1 %collective-permute-start.27 = (bf16[8,48,1024]{2,1,0:T(8,128)(2,1)S(1)}, bf16[8,48,1024]{2,1,0:T(8,128)(2,1)S(1)}, u32[]{:S(2)}, u32[]{:S(2)}) collective-permute-start(bf16[8,48,1024]{2,1,0:T(8,128)(2,1)S(1)} %all-to-all-done.9.own), channel_id=1, source_target_pairs={{0,8},{8,0},{1,9},{9,1},{2,10},{10,2},{3,11},{11,3},{4,12},{12,4},... | collective-permute-start | bytes 2359304 | tf_op jit(solution)/shard_map/ppermute | solution.py:442
  (92 other events, 634.7 us)
where the time goes:
time: 436 us; the launch traced here: 428 us
  waiting for transfers between devices  136 us (31%)
  starting transfers between devices  108 us (25%)
  Pallas kernels  103 us (24%)
  local copies, waits for them, and re-layouts  60.1 us (14%)
  matrix products  12 us (3%)
  other arithmetic  7.85 us (2%)
    pallas_call x22, Pallas kernels, call(): pl.pallas_call(kernel, out_shape=[jax.ShapeDtypeStruct(shape, kind) for s...  103 us
    all_to_all x10, waiting for transfers between devices, exchange(): return lax.all_to_all(v, axis, 0, 0, tiled=True)  73.1 us
    ppermute x18, waiting for transfers between devices, flip(): return lax.ppermute(v, 'x', pairs)  60.3 us
    all_to_all x10, starting transfers between devices, exchange(): return lax.all_to_all(v, axis, 0, 0, tiled=True)  55.3 us
    unnamed x160, local copies, waits for them, and re-layouts  35.4 us
    ppermute x18, starting transfers between devices, swap(): return lax.ppermute(v, 'core', [(0, 1), (1, 0)])  33.8 us
    ppermute x18, starting transfers between devices, flip(): return lax.ppermute(v, 'x', pairs)  18.1 us
  transfers between devices with their start and end apart: 47, of which 17 were waited for; matrix products, arithmetic and copies ran while one was open for 9% of the time, Pallas kernels for 15%

commit v1 on v0

v1 whole, which is shorter than its diff:
```python
import jax
import jax.numpy as jnp
from jax import lax
from jax.experimental import pallas as pl
from jax.experimental.pallas import tpu as pltpu
from jax.sharding import Mesh
from jax.sharding import PartitionSpec as P

HEADS = 12
KV_HEADS = 2
HEAD_DIM = 128
TOP = 4
WINDOW = 1024

EPSILON = 1e-06
THETA = 10000.0
NEGATIVE = -1e30

YLO, XS, CORES = 2, 4, 2
REP = ("ylo", "x", "core")
BF = jnp.bfloat16
F32 = jnp.float32


def angles(positions):
    half_width = HEAD_DIM // 2
    frequency = THETA ** (-(jnp.arange(half_width, dtype=F32) * 2.0) / HEAD_DIM)
    phase = positions.astype(F32)[:, None] * frequency[None, :]
    cosine, sine = jnp.cos(phase), jnp.sin(phase)
    return (
        jnp.concatenate([cosine, cosine], axis=1),
        jnp.concatenate([-sine, sine], axis=1),
    )


def dot(a, b):
    return jnp.dot(a, b, preferred_element_type=F32)


def dot_t(a, b):
    return lax.dot_general(a, b, (((1,), (1,)), ((), ())), preferred_element_type=F32)


def t_dot(a, b):
    return lax.dot_general(a, b, (((0,), (0,)), ((), ())), preferred_element_type=F32)


def add(a, b):
    return (a.astype(F32) + b.astype(F32)).astype(BF)


def turn(piece, cosine, sine):
    return piece * cosine + pltpu.roll(piece, HEAD_DIM // 2, 1) * sine


def turn_back(piece, cosine, sine):
    return piece * cosine - pltpu.roll(piece, HEAD_DIM // 2, 1) * sine


def stacked(ref, pair):
    low = 2 * pair * HEAD_DIM
    return jnp.concatenate(
        [ref[:, pl.ds(low, HEAD_DIM)], ref[:, pl.ds(low + HEAD_DIM, HEAD_DIM)]], axis=0
    )


def unstack(ref, pair, value):
    low, rows = 2 * pair * HEAD_DIM, value.shape[0] // 2
    ref[:, pl.ds(low, HEAD_DIM)] = value[:rows]
    ref[:, pl.ds(low + HEAD_DIM, HEAD_DIM)] = value[rows:]


def key_kernel(place, src, gain, raw_own, raw_other, cos, sin, normed_o, scale_o, send_o, weight_o):
    core = place[0]
    groups, kv_rows, width = raw_own.shape
    kv_width = weight_o.shape[1] // 2
    parts = width // kv_width
    source = src[...].astype(F32)
    scale = lax.rsqrt(jnp.mean(source * source, axis=-1, keepdims=True) + EPSILON)
    scale_o[...] = jnp.broadcast_to(scale, scale_o.shape)
    normed = (source * scale * gain[...]).astype(BF)
    normed_o[...] = normed
    send(scale_o, normed_o)
    for raw, which in ((raw_own, core), (raw_other, 1 - core)):
        at = pl.ds(pl.multiple_of(which * kv_width, kv_width), kv_width)
        for f in range(groups):
            for j in range(parts):
                weight_o[pl.ds((f * parts + j) * kv_rows, kv_rows), at] = raw[
                    f, :, pl.ds(j * kv_width, kv_width)
                ]
    send(weight_o)
    pre = dot(normed, weight_o[...])
    for head in range(2 * KV_HEADS):
        low, high = head * HEAD_DIM, (head + 1) * HEAD_DIM
        piece = pre[:, low:high]
        if head < KV_HEADS:
            piece = turn(piece, cos[...], sin[...])
        for f in range(groups):
            send_o[f, :, low:high] = piece.astype(BF)


def front_kernel(place, normed, kv, bias, src, gain, hot_t, cos, sin, *refs):
    pieces = refs[:8]
    query_w, output_w, query_o, mixed_o, probs_o, resid_o, scale_o, send_o, sems = refs[8:]
    core, s, t = place[0], place[2], place[3]
    _, rows, half = pieces[0].shape
    copies = []
    for n, block in enumerate(pieces):
        weight, bit = ((query_w, s), (output_w, t))[n // 4]
        which = core if n % 4 < 2 else 1 - core
        part = bit if n % 2 == 0 else 1 - bit
        at = pl.ds(pl.multiple_of(part * rows, rows), rows)
        cols = pl.ds(pl.multiple_of(which * half, half), half)
        copy = pltpu.make_async_copy(block, weight.ref.at[:, at, cols], sems.at[n])
        copy.start()
        copies.append(copy)
    width = 2 * half
    for copy in copies[:4]:
        copy.wait()
    query_w.send()
    pre = dot(normed[...], query_w[...].reshape(width, width))
    for head in range(HEADS):
        low, high = head * HEAD_DIM, (head + 1) * HEAD_DIM
        query_o[:, low:high] = turn(pre[:, low:high], cos[...], sin[...]).astype(BF)
    query_o.send()
    kv_width = kv.shape[1] // 2
    for pair in range(HEADS // 2):
        group = 2 * pair // (HEADS // KV_HEADS)
        keys = kv[:, pl.ds(group * HEAD_DIM, HEAD_DIM)]
        values = kv[:, pl.ds(kv_width + group * HEAD_DIM, HEAD_DIM)]
        scores = dot_t(keys, stacked(query_o, pair)) * HEAD_DIM ** (-0.5) + bias[...]
        weights = jnp.exp(scores - jnp.max(scores, axis=0, keepdims=True))
        probs = (weights * (1.0 / jnp.sum(weights, axis=0, keepdims=True))).astype(BF)
        probs_o[pair] = probs
        unstack(mixed_o, pair, t_dot(probs, values).astype(BF))
    send(probs_o, mixed_o)
    for copy in copies[4:]:
        copy.wait()
    output_w.send()
    resid = src[...].astype(F32) + dot(mixed_o[...], output_w[...].reshape(width, width))
    resid_o[...] = resid
    resid_o.send()
    scale = lax.rsqrt(jnp.mean(resid * resid, axis=-1, keepdims=True) + EPSILON)
    scale_o[...] = jnp.broadcast_to(scale, scale_o.shape)
    second = (resid * scale * gain[...]).astype(BF)
    send_o[...] = t_dot(hot_t[...], second).astype(BF)


def expert_kernel(place, rows, grad_hidden, gate_w, up_w, hidden_o, own_o, sent_o, back_o):
    core = place[0]
    count = rows.shape[0]
    step = count // 2
    for n, low in enumerate(range(0, count, step)):
        at = pl.ds(low, step)
        block = rows[at, :]
        gate = dot(block, gate_w[...])
        up = dot(block, up_w[...])
        sigmoid = 1.0 / (1.0 + jnp.exp(-gate))
        silu = gate * sigmoid
        hidden_o[at, :] = (silu * up).astype(BF)
        grad = grad_hidden[at, :]
        grad_gate = (grad * up * (sigmoid * (1.0 + gate * (1.0 - sigmoid)))).astype(BF)
        grad_up = (grad * silu).astype(BF)
        own_o[at, :] = jnp.where(core == 0, grad_gate, grad_up)
        sent_o[at, :] = jnp.where(core == 0, grad_up, grad_gate)
        for result in (sent_o, hidden_o, own_o):
            result.send(n + 1)
        back_o[at, :] = (dot_t(grad_gate, gate_w[...]) + dot_t(grad_up, up_w[...])).astype(BF)
        back_o.send(n + 1)


def expert_weight_kernel(
    place, rows, rows_got, pre, pre_got, hidden, hidden_got, arrived, upper_got,
    keep_a, send_a, keep_b, send_b, total,
):
    s, t = place[2], place[3]
    width, half = rows.shape[1], hidden.shape[1]
    upper = arrived[:, pl.ds(pl.multiple_of(place[0] * half, half), half)]
    step = 256
    for low in range(0, width, step):
        at = pl.ds(low, step)
        total[at, :] = (t_dot(rows[:, at], pre[...]) + t_dot(rows_got[:, at], pre_got[...])).astype(
            BF
        )
    for low in range(0, half, step):
        at = pl.ds(low, step)
        total[pl.ds(width + low, step), :] = (
            t_dot(hidden[:, at], upper) + t_dot(hidden_got[:, at], upper_got[...])
        ).astype(BF)
    big, small = width // 8, half // 8
    for out, side, spots in (
        (send_a, 0, ((1 - s, 0), (1 - s, 1))),
        (send_b, 1, ((0, 1 - t), (1, 1 - t))),
        (keep_a, 0, ((s, 0), (s, 1))),
        (keep_b, 1, ((0, t), (1, t))),
    ):
        for j, (row_s, row_t) in enumerate(spots):
            piece = side * 4 + 2 * row_s + row_t
            out[j, pl.ds(0, big), :] = total[pl.ds(pl.multiple_of(piece * big, big), big), :]
            start = pl.multiple_of(width + piece * small, small)
            out[j, pl.ds(big, small), :] = total[pl.ds(start, small), :]
        out.send()


def expert_step_kernel(place, keep_a, got_a, keep_b, got_b, keep_ao, send_ao, keep_bo, send_bo):
    s, t = place[2], place[3]
    send_ao[...] = add(keep_a[1 - t], got_a[1 - t])
    send_ao.send()
    send_bo[...] = add(keep_b[1 - s], got_b[1 - s])
    send_bo.send()
    keep_ao[...] = add(keep_a[t], got_a[t])
    keep_ao.send()
    keep_bo[...] = add(keep_b[s], got_b[s])


def expert_end_kernel(place, keep_a, got_a, keep_b, got_b, out):
    out[0] = add(keep_a[...], got_a[...])
    out[1] = add(keep_b[...], got_b[...])


def pair_kernel(place, a, b, one, two):
    one[...] = add(a[0], b[0])
    one.send()
    two[...] = add(a[1], b[1])


def place_experts(place, blocks, outs, stage, sems):
    core = place[0]
    gate_o, up_o, down_o = outs
    half = stage.shape[2]
    big = gate_o.shape[0] // 8
    small = stage.shape[1] - big
    moves = []
    for n, (side, row_s, row_t, which, block) in enumerate(blocks):
        stage[n] = block[...].astype(F32)
        piece = side * 4 + 2 * row_s + row_t
        at = pl.ds(pl.multiple_of(piece * big, big), big)
        cols = pl.ds(pl.multiple_of(which * half, half), half)
        to_gate = pltpu.make_async_copy(stage.at[n, pl.ds(0, big)], gate_o.at[at], sems.at[2 * n])
        to_up = pltpu.make_async_copy(stage.at[n, pl.ds(0, big)], up_o.at[at], sems.at[2 * n])
        to_down = pltpu.make_async_copy(
            stage.at[n, pl.ds(big, small)],
            down_o.at[pl.ds(pl.multiple_of(piece * small, small), small), cols],
            sems.at[2 * n + 1],
        )

        @pl.when(which == 0)
        def _():
            to_gate.start()

        @pl.when(which == 1)
        def _():
            to_up.start()

        to_down.start()
        moves.append((which, to_gate, to_up, to_down))
    for which, to_gate, to_up, to_down in moves:

        @pl.when(which == 0)
        def _():
            to_gate.wait()

        @pl.when(which == 1)
        def _():
            to_up.wait()

        to_down.wait()


def expert_most_kernel(place, *refs):
    core, s, t = place[0], place[2], place[3]
    gate_o, up_o, down_o, mark_o, stage, sems = refs[12:]
    mark_o[...] = jnp.zeros(mark_o.shape, F32)
    blocks = []
    for first, which in ((0, core), (6, 1 - core)):
        zero_a, zero_b, one_a, one_b, two_a, two_b = refs[first : first + 6]
        blocks += [
            (0, s, t, which, zero_a),
            (1, s, t, which, zero_b),
            (0, s, 1 - t, which, one_a),
            (1, 1 - s, t, which, one_b),
            (0, 1 - s, t, which, two_a),
            (1, s, 1 - t, which, two_b),
        ]
    place_experts(place, blocks, (gate_o, up_o, down_o), stage, sems)


def expert_rest_kernel(place, *refs):
    core, s, t = place[0], place[2], place[3]
    gate_o, up_o, down_o, mark_o, stage, sems = refs[9:]
    mark_o[...] = jnp.zeros(mark_o.shape, F32)
    blocks = []
    for first, which in ((0, core), (2, 1 - core)):
        for side in range(2):
            blocks.append((side, 1 - s, 1 - t, which, refs[first + side]))
    place_experts(place, blocks, (gate_o, up_o, down_o), stage, sems)


def expert_outputs(kernel, args, before, part, width, half):
    near = pl.BlockSpec(memory_space=pltpu.VMEM)
    away = pl.BlockSpec(memory_space=pl.ANY)
    shapes = [
        jax.ShapeDtypeStruct(shape, F32)
        for shape in ((width, half), (width, half), (half, width), (8, HEAD_DIM))
    ]
    blocks = 12 if not before else 4
    return pl.pallas_call(
        kernel,
        out_shape=shapes,
        in_specs=[pl.BlockSpec(memory_space=pltpu.SMEM)]
        + [near] * (len(args) - 1)
        + [away] * len(before),
        out_specs=[away] * 3 + [near],
        scratch_shapes=[
            pltpu.VMEM((blocks,) + part, F32),
            pltpu.SemaphoreType.DMA((2 * blocks,)),
        ],
        input_output_aliases={len(args) + n: n for n in range(len(before))},
        compiler_params=pltpu.CompilerParams(vmem_limit_bytes=56 * 1024 * 1024),
        cost_estimate=pl.CostEstimate(flops=0, bytes_accessed=0, transcendentals=0),
    )(*args, *before)


def back_kernel(
    place, back, hot_t, resid_i, scale_i, gain, cot, weight, probs_i, kv, q, cos, sin,
    grad_resid_o, attended_o, gain_o, query_o, kv_o, sent_o,
):
    kv_width = kv.shape[1] // 2
    resid = resid_i[...]
    scale = scale_i[:, :1]
    grad_second = dot(hot_t[...], back[...])
    weighted = grad_second * gain[...]
    inner = jnp.sum(weighted * resid, axis=-1, keepdims=True)
    grad_resid = (
        cot[...].astype(F32)
        + scale * weighted
        - resid * (scale * scale * scale * inner * (1.0 / resid.shape[-1]))
    )
    gain_o[...] = jnp.sum(grad_second * resid * scale, axis=0, keepdims=True)
    grad_resid_o[...] = grad_resid
    grad_resid_o.send()
    attended = grad_resid.astype(BF)
    attended_o[...] = attended
    grad_mixed = dot_t(attended, weight[...]).astype(BF)
    pairs = HEADS // KV_HEADS // 2
    rows = resid.shape[0]
    for group in range(KV_HEADS):
        keys = kv[:, pl.ds(group * HEAD_DIM, HEAD_DIM)]
        values = kv[:, pl.ds(kv_width + group * HEAD_DIM, HEAD_DIM)]
        grad_keys = jnp.zeros(keys.shape, F32)
        grad_values = jnp.zeros(keys.shape, F32)
        for pair in range(group * pairs, (group + 1) * pairs):
            low, high = 2 * pair * HEAD_DIM, (2 * pair + 1) * HEAD_DIM
            upper = jnp.concatenate(
                [grad_mixed[:, low:high], grad_mixed[:, high : high + HEAD_DIM]], axis=0
            )
            probs = probs_i[pair]
            wide = probs.astype(F32)
            grad_probs = dot_t(values, upper)
            total = jnp.sum(wide * grad_probs, axis=0, keepdims=True)
            grad_scores = (wide * (grad_probs - total)).astype(BF)
            grad_values = grad_values + dot(probs, upper)
            grad_keys = grad_keys + dot(grad_scores, stacked(q, pair))
            grad_query = t_dot(grad_scores, keys) * HEAD_DIM ** (-0.5)
            for at, part in ((low, grad_query[:rows]), (high, grad_query[rows:])):
                turned = turn_back(part, cos[...], sin[...])
                query_o[:, pl.ds(at, HEAD_DIM)] = turned.astype(BF)
        at = pl.ds(group * HEAD_DIM, HEAD_DIM)
        kv_o[:, at] = (grad_keys * HEAD_DIM ** (-0.5)).astype(BF)
        kv_o[:, pl.ds(kv_width + group * HEAD_DIM, HEAD_DIM)] = grad_values.astype(BF)
    kv_o.send()
    half = resid.shape[1] // 2
    at = pl.ds(pl.multiple_of((1 - place[0]) * half, half), half)
    sent_o[0] = attended_o[:, at]
    sent_o[1] = query_o[:, at]


def put_split(s, t, total, keep_a, send_a, keep_b, send_b, which=(0, 1)):
    groups, _, quarter, _ = keep_a.shape
    outs = (
        (send_a, 0, ((1 - s, 0), (1 - s, 1))),
        (send_b, 1, ((0, 1 - t), (1, 1 - t))),
        (keep_a, 0, ((s, 0), (s, 1))),
        (keep_b, 1, ((0, t), (1, t))),
    )
    for out, k, spots in outs:
        if k not in which:
            continue
        for f in range(groups):
            for j, (row_s, row_t) in enumerate(spots):
                start = (f * XS + 2 * row_s + row_t) * quarter
                out[f, j] = total[k, pl.ds(pl.multiple_of(start, quarter), quarter), :]
        out.send()


def square_weight_kernel(
    place, mixed, mixed_got, attended, normed, normed_got, query, got,
    keep_a, send_a, keep_b, send_b, total,
):
    half = mixed.shape[1] // 2
    at = pl.ds(pl.multiple_of(place[0] * half, half), half)
    step = 256
    for k, (left, left_got, right) in enumerate(
        ((mixed, mixed_got, attended), (normed, normed_got, query))
    ):
        part = right[:, at]
        for low in range(0, 2 * half, step):
            cols = pl.ds(low, step)
            total[k, cols, :] = (
                t_dot(left[:, cols], part) + t_dot(left_got[:, cols], got[k])
            ).astype(BF)
        put_split(place[2], place[3], total, keep_a, send_a, keep_b, send_b, (k,))


def step_kernel(
    place, qk_a, qg_a, kk_a, kg_a, qk_b, qg_b, kk_b, kg_b, keep_a, send_a, keep_b, send_b
):
    s, t = place[2], place[3]
    size = qk_a.shape[-1]
    extra = kk_a.shape[-1]
    groups = qk_a.shape[0]
    for out, which, big, big_got, small, small_got in (
        (send_a, 1 - t, qk_a, qg_a, kk_a, kg_a),
        (send_b, 1 - s, qk_b, qg_b, kk_b, kg_b),
        (keep_a, t, qk_a, qg_a, kk_a, kg_a),
        (keep_b, s, qk_b, qg_b, kk_b, kg_b),
    ):
        for f in range(groups):
            out[f, :, pl.ds(0, size)] = add(big[f, which], big_got[f, which])
            out[f, :, pl.ds(size, extra)] = add(small[f, which], small_got[f, which])
        out.send()


def pack_kernel(place, keep_a, got_a, keep_b, got_b, gains, out):
    size = keep_a.shape[-1]
    for y, (keep, got) in enumerate(((keep_a, got_a), (keep_b, got_b))):
        out[y, :, :, pl.ds(0, size)] = add(keep[...], got[...])
        out[y, :, :, pl.ds(size, gains.shape[-1])] = gains[...]
        out.send(y + 1)


def sum_kernel(place, parts, out):
    total = parts[0].astype(F32)
    for k in range(1, parts.shape[0]):
        total = total + parts[k].astype(F32)
    total = total.astype(BF)
    for k in range(out.shape[0]):
        out[k] = total


def final_kernel(place, own, other, mark, output_o, query_o, key_o, value_o, gains_o):
    core = place[0]
    quarter = own.shape[1]
    half = output_o.shape[1] // 2
    part = key_o.shape[1] // 2
    size = half + part
    for refs, which in ((own, core), (other, 1 - core)):
        at = pl.ds(pl.multiple_of(which * half, half), half)
        for piece, x in enumerate(PLACE):
            rows = pl.ds(piece * quarter, quarter)
            output_o[rows, at] = refs[x, :, pl.ds(0, half)].astype(F32)
            query_o[rows, at] = refs[XS + x, :, pl.ds(0, half)].astype(F32)
    send(output_o, query_o)
    for piece, x in enumerate(PLACE):
        rows = pl.ds(piece * quarter, quarter)
        for y in range(2):
            at = pl.ds(y * part, part)
            mine = own[y * XS + x, :, pl.ds(half, part)].astype(F32)
            others = other[y * XS + x, :, pl.ds(half, part)].astype(F32)
            even = core == 0
            key_o[rows, at] = jnp.where(even, mine, others)
            value_o[rows, at] = jnp.where(even, others, mine)
    total = jnp.zeros(gains_o.shape, F32)
    for refs in (own, other):
        for x in range(XS):
            total = total + refs[x, :, pl.ds(size, gains_o.shape[1])].astype(F32)
    gains_o[...] = total


def key_back_kernel(place, parts, cos, sin, pre_o, sent_o):
    kv_width = parts.shape[-1] // 2
    total = parts[0].astype(F32)
    for k in range(1, parts.shape[0]):
        total = total + parts[k].astype(F32)
    for head in range(2 * KV_HEADS):
        low, high = head * HEAD_DIM, (head + 1) * HEAD_DIM
        piece = total[:, low:high]
        if head < KV_HEADS:
            piece = turn_back(piece, cos[...], sin[...])
        pre_o[:, low:high] = piece.astype(BF)
    sent_o[...] = pre_o[:, pl.ds(pl.multiple_of((1 - place[0]) * kv_width, kv_width), kv_width)]


def key_weight_kernel(
    place, normed, normed_got, pre, pre_got, keep_a, send_a, keep_b, send_b, total
):
    kv_width = pre_got.shape[1]
    part = pre[:, pl.ds(pl.multiple_of(place[0] * kv_width, kv_width), kv_width)]
    grad = (t_dot(normed[...], part) + t_dot(normed_got[...], pre_got[...])).astype(BF)
    total[0] = grad[:, : kv_width // 2]
    total[1] = grad[:, kv_width // 2 :]
    put_split(place[2], place[3], total, keep_a, send_a, keep_b, send_b)


def input_kernel(
    place, query, pre, src, scale_i, gain, query_w, kv_w, grad_resid, input_o, gain_o
):
    grad_normed = dot_t(query[...], query_w[...]) + dot_t(pre[...], kv_w[...])
    source = src[...].astype(F32)
    scale = scale_i[:, :1]
    weighted = grad_normed * gain[...]
    inner = jnp.sum(weighted * source, axis=-1, keepdims=True)
    input_o[...] = (
        grad_resid[...]
        + scale * weighted
        - source * (scale * scale * scale * inner * (1.0 / source.shape[-1]))
    ).astype(BF)
    gain_o[...] = jnp.sum(grad_normed * source * scale, axis=0, keepdims=True)


class Far:
    def __init__(self, value, kind=None, parts=1):
        self.value, self.kind, self.parts = value, kind, parts


class Coming:
    def __init__(self, source, ref, sem):
        self.copy, self.ref, self.waits = pltpu.make_async_copy(source, ref, sem), ref, True
        self.shape = ref.shape
        self.copy.start()

    def now(self):
        if self.waits:
            self.copy.wait()
            self.waits = False
        return self.ref

    def __getitem__(self, index):
        return self.now()[index]

    @property
    def at(self):
        return self.now().at


class Going:
    def __init__(self, ref, target, sems, parts):
        self.ref, self.target, self.shape, self.sent = ref, target, ref.shape, 0
        rows = ref.shape[0] // parts
        self.copies = [
            pltpu.make_async_copy(
                ref.at[pl.ds(n * rows, rows)], target.at[pl.ds(n * rows, rows)], sem
            )
            for n, sem in enumerate(sems)
        ]

    def __getitem__(self, index):
        return self.ref[index]

    def __setitem__(self, index, value):
        self.ref[index] = value

    def send(self, upto=None):
        upto = len(self.copies) if upto is None else upto
        for copy in self.copies[self.sent : upto]:
            copy.start()
        self.sent = max(self.sent, upto)


def send(self):
        if not self.sent:
            self.copy.start()
            self.sent = True


def send(*results):
    for result in results:
        result.send()


def call(kernel, args, outs, scratch=(), micros=0, raw=()):
    outs = [out if isinstance(out, Far) else Far(*out) for out in outs]
    values = [a.value if isinstance(a, Far) else a for a in args]
    far = [i for i, a in enumerate(args) if isinstance(a, Far) and i not in raw]
    count, made = len(args), len(outs)

    def whole(*refs):
        ins, results = list(refs[:count]), refs[count : count + made]
        own = refs[count + made : count + made + len(scratch)]
        rest = refs[count + made + len(scratch) :]
        landing, leaving, sems = rest[: len(far)], rest[len(far) : len(far) + made], rest[-1]
        for n, i in enumerate(far):
            ins[i] = Coming(ins[i], landing[n], sems.at[n])
        going, used = [], len(far)
        for out, ref, target in zip(outs, leaving, results):
            going.append(
                Going(ref, target, [sems.at[used + n] for n in range(out.parts)], out.parts)
            )
            used += out.parts
        kernel(*ins, *going, *own)
        for i in far:
            ins[i].now()
        send(*going)
        for result in going:
            for copy in result.copies:
                copy.wait()

    near = pl.BlockSpec(memory_space=pltpu.VMEM)
    away = pl.BlockSpec(memory_space=pl.ANY)
    specs = [away if isinstance(a, Far) else near for a in args]
    specs[0] = pl.BlockSpec(memory_space=pltpu.SMEM)
    return pl.pallas_call(
        whole,
        out_shape=[jax.ShapeDtypeStruct(out.value, out.kind) for out in outs],
        in_specs=specs,
        out_specs=[away] * made,
        scratch_shapes=[
            *scratch,
            *[pltpu.VMEM(values[i].shape, values[i].dtype) for i in far],
            *[pltpu.VMEM(out.value, out.kind) for out in outs],
            pltpu.SemaphoreType.DMA((len(far) + sum(out.parts for out in outs),)),
        ],
        compiler_params=pltpu.CompilerParams(vmem_limit_bytes=56 * 1024 * 1024),
        cost_estimate=pl.CostEstimate(
            flops=int(micros * 1e9), bytes_accessed=0, transcendentals=0
        ),
    )(*values)


def swap(v):
    return lax.ppermute(v, "core", [(0, 1), (1, 0)])


def swap_y(v):
    return lax.ppermute(v, "ylo", [(0, 1), (1, 0)])


def exchange(v, axis):
    return lax.all_to_all(v, axis, 0, 0, tiled=True)


def copies(v, n):
    return lax.optimization_barrier(jnp.broadcast_to(v[None], (n,) + v.shape))


def tie(*values):
    return lax.optimization_barrier(values)


PAIRS_S = [(0, 1), (1, 0), (2, 3), (3, 2)]
PAIRS_T = [(0, 3), (3, 0), (1, 2), (2, 1)]
PLACE = (0, 3, 1, 2)


def x_bits():
    x = lax.axis_index("x")
    return ((x + 1) // 2) % 2, x // 2


def flip(v, pairs):
    return lax.ppermute(v, "x", pairs)


def body(
    inputs,
    segments,
    first_gain,
    query_matrix,
    key_matrix,
    value_matrix,
    output_matrix,
    second_gain,
    expert_ids,
    gate_values,
    priority,
    gate_weight,
    up_weight,
    down_weight,
    cotangent,
):
    tok = inputs.shape[1]
    width = inputs.shape[2]
    rows = query_matrix.shape[0]
    groups = lax.axis_size("fsdp")
    member = lax.axis_index("fsdp")
    core = lax.axis_index("core")
    even = core == 0
    experts = groups
    capacity = 5 * tok * TOP // (4 * experts)
    slots_all = experts * capacity
    half = width // 2
    kv_width = key_matrix.shape[1]
    length = groups * tok
    quarter = rows // XS
    bit_s, bit_t = x_bits()
    place_at = jnp.stack([core, member * tok, bit_s, bit_t]).astype(jnp.int32)

    def pick(a, b):
        return jnp.where(even, a, b)

    parts = width // kv_width
    kv_rows = rows // parts
    kv_half = pick(key_matrix, value_matrix).reshape(parts, kv_rows, kv_width)
    kv_piece = jnp.concatenate([kv_half[j] for j in range(parts)], axis=1)
    gains = jnp.pad(jnp.stack([first_gain, second_gain]), ((0, 6), (0, width - rows)))
    square_piece = jnp.concatenate(
        [
            lax.dynamic_slice(matrix, (bit * (rows // 2), core * half), (rows // 2, half))
            for matrix, bit in ((query_matrix, bit_s), (output_matrix, bit_t))
        ],
        axis=1,
    )
    weights = jnp.concatenate([kv_piece, gains, square_piece], axis=0)
    gathered = exchange(copies(weights, groups), "fsdp")

    ids = expert_ids[0].reshape(-1)
    order = priority[0, 0]
    earlier = (order[None, :] < order[:, None]) & (ids[None, :] == ids[:, None])
    slots = jnp.sum(earlier.astype(jnp.int32), axis=1)
    kept = slots < capacity
    expert_list = jnp.arange(experts, dtype=jnp.int32)
    chosen = (ids[:, None] == expert_list[None, :]) & kept[:, None]
    slot_of = jnp.sum(
        jnp.where(chosen, slots[:, None] + 1, 0).reshape(tok, TOP, experts), axis=1
    )
    slot_of = slot_of - 1
    gate_table = jnp.sum(
        jnp.where(chosen, gate_values[0].reshape(-1)[:, None], 0.0).reshape(tok, TOP, experts),
        axis=1,
    )
    slot_list = jnp.arange(capacity, dtype=jnp.int32)
    hits = slot_of.T[:, None, :] == slot_list[None, :, None]
    one_hot = hits.astype(BF).reshape(slots_all, tok)
    one_hot_t = (slot_of[:, :, None] == slot_list[None, None, :]).astype(BF)
    one_hot_t = one_hot_t.reshape(tok, slots_all)
    gate_hot = jnp.where(hits, gate_table.T[:, None, :], 0.0).reshape(slots_all, tok)
    slot_gate = jnp.sum(gate_hot, axis=1, keepdims=True)
    gate_high = gate_hot.astype(BF)
    gate_low = (gate_hot - gate_high.astype(F32)).astype(BF)
    send_grad = (dot(one_hot, cotangent[0]) * slot_gate).astype(BF)

    cosine, sine = angles(member * tok + jnp.arange(tok, dtype=jnp.int32))
    segment_row = segments[0]
    query_segments = lax.dynamic_slice_in_dim(segment_row, member * tok, tok)
    key_place = jnp.arange(length, dtype=jnp.int32)[:, None]
    query_place = (member * tok + jnp.arange(tok, dtype=jnp.int32))[None, :]
    allowed = (
        (key_place <= query_place)
        & (query_place - key_place < WINDOW)
        & (segment_row[:, None] == query_segments[None, :])
    )
    bias = jnp.where(allowed, 0.0, NEGATIVE).astype(F32)
    bias = jnp.concatenate([bias, bias], axis=1)
    gathered, cosine, sine, place_at, one_hot_t, gate_high, gate_low, send_grad, bias = tie(
        gathered, cosine, sine, place_at, one_hot_t, gate_high, gate_low, send_grad, bias
    )
    kv_raw = gathered[:, :kv_rows]
    gain_one = gathered[:, kv_rows, :rows].reshape(1, width).astype(F32)
    gain_two = gathered[:, kv_rows + 1, :rows].reshape(1, width).astype(F32)
    kv_raw_other = swap(kv_raw)

    square = (width, width)
    normed, scale_one, kv_send, kv_weight = call(
        key_kernel,
        [place_at, Far(inputs[0]), gain_one, Far(kv_raw), Far(kv_raw_other), cosine, sine],
        [((tok, width), BF), ((tok, HEAD_DIM), F32), ((groups, tok, 2 * kv_width), BF),
         ((width, 2 * kv_width), BF)],
    )
    q_own, o_own = gathered[:, kv_rows + 8 :, :half], gathered[:, kv_rows + 8 :, half:]
    kv_all = exchange(kv_send, "fsdp").reshape(length, 2 * kv_width)
    q_got, o_got = flip(q_own, PAIRS_S), flip(o_own, PAIRS_T)
    send_grad, kv_all = tie(send_grad, kv_all)
    arrived_grad = exchange(send_grad, "fsdp")
    normed_other = swap(normed)
    far_pieces = [
        Far(v)
        for v in (q_own, q_got, swap(q_own), swap(q_got), o_own, o_got, swap(o_own), swap(o_got))
    ]
    weight_parts = (groups, rows, width)
    (query_weight, output_weight, query_rot, mixed, probs, residual, scale_two,
     send_rows) = call(
        front_kernel,
        [place_at, Far(normed), Far(kv_all), Far(bias), Far(inputs[0]), gain_two, Far(one_hot_t),
         cosine, sine, *far_pieces],
        [(weight_parts, BF), (weight_parts, BF), ((tok, width), BF), ((tok, width), BF),
         ((HEADS // 2, length, 2 * tok), BF), ((tok, width), F32), ((tok, HEAD_DIM), F32),
         ((slots_all, width), BF)],
        [pltpu.SemaphoreType.DMA((8,))],
        raw=range(9, 17),
    )
    query_weight = query_weight.reshape(square)
    output_weight = output_weight.reshape(square)

    send_rows, arrived_grad = tie(send_rows, arrived_grad)
    arrived = exchange(send_rows, "fsdp")
    mixed_other = swap(mixed)
    upper_other = swap(lax.dynamic_slice_in_dim(arrived_grad, (1 - core) * half, half, 1))
    grad_hidden = dot_t(arrived_grad, down_weight[0])
    arrived, grad_hidden, mixed_other, upper_other = tie(
        arrived, grad_hidden, mixed_other, upper_other
    )
    arrived_other = swap(arrived)
    hidden, own_pre, sent_pre, grad_rows = call(
        expert_kernel,
        [place_at, Far(arrived), Far(grad_hidden), gate_weight[0], up_weight[0]],
        [Far((slots_all, half), BF, 2)] * 3 + [Far((slots_all, width), BF, 2)],
    )
    back_rows = exchange(grad_rows, "fsdp")
    expert_rows = width + half

    e_part = (2, expert_rows // 8, half)
    e_keep_a, e_send_a, e_keep_b, e_send_b = call(
        expert_weight_kernel,
        [place_at] + [Far(v) for v in (arrived, arrived_other, own_pre, swap(sent_pre), hidden,
                                       swap(hidden), arrived_grad, upper_other)],
        [(e_part, BF)] * 4,
        [pltpu.VMEM((expert_rows, half), BF)],
    )
    expert_out = dot(hidden, down_weight[0]).astype(BF)
    e_got_a, e_got_b = flip(e_send_a, PAIRS_S), flip(e_send_b, PAIRS_T)
    back_rows, expert_out, e_keep_a, e_keep_b = tie(back_rows, expert_out, e_keep_a, e_keep_b)

    grad_residual, grad_attended, gain_two_part, grad_query_pre, kv_back, qo_sent = call(
        back_kernel,
        [place_at, Far(back_rows), Far(one_hot_t), Far(residual), Far(scale_two), gain_two,
         Far(cotangent[0]), Far(output_weight), Far(probs), Far(kv_all), Far(query_rot), cosine,
         sine],
        [((tok, width), F32), ((tok, width), BF), ((1, width), F32), ((tok, width), BF),
         ((length, 2 * kv_width), BF), ((2, tok, half), BF)],
    )
    kv_got = exchange(kv_back, "fsdp")
    e_keep_a, e_send_a, e_keep_b, e_send_b = call(
        expert_step_kernel,
        [place_at, Far(e_keep_a), Far(e_got_a), Far(e_keep_b), Far(e_got_b)],
        [(e_part[1:], BF)] * 4,
    )
    qo_got, e_send_a, e_send_b = tie(swap(qo_sent), e_send_a, e_send_b)
    e_got_a, e_got_b = flip(e_send_a, PAIRS_T), flip(e_send_b, PAIRS_S)

    big_part, small_part = (groups, 2, quarter, half), (groups, 2, quarter, kv_width // 2)
    qo_keep_a, qo_send_a, qo_keep_b, qo_send_b = call(
        square_weight_kernel,
        [place_at] + [Far(v) for v in (mixed, mixed_other, grad_attended, normed, normed_other,
                                       grad_query_pre, qo_got)],
        [(big_part, BF)] * 4,
        [pltpu.VMEM((2, width, half), BF)],
    )
    kv_got, expert_out = tie(kv_got, expert_out)
    qo_got_a, qo_got_b = flip(qo_send_a, PAIRS_S), flip(qo_send_b, PAIRS_T)
    returned = exchange(expert_out, "fsdp")
    grad_kv_pre, kv_pre_sent = call(
        key_back_kernel,
        [place_at, Far(kv_got.reshape(groups, tok, 2 * kv_width)), cosine, sine],
        [((tok, 2 * kv_width), BF), ((tok, kv_width), BF)],
        micros=30,
    )
    kv_keep_a, kv_send_a, kv_keep_b, kv_send_b = call(
        key_weight_kernel,
        [place_at, Far(normed), Far(normed_other), Far(grad_kv_pre), Far(swap(kv_pre_sent))],
        [(small_part, BF)] * 4,
        [pltpu.VMEM((2, width, kv_width // 2), BF)],
    )
    kv_got_a, kv_got_b = flip(kv_send_a, PAIRS_S), flip(kv_send_b, PAIRS_T)
    e_sum = call(
        expert_end_kernel,
        [place_at, Far(e_keep_a), Far(e_got_a), Far(e_keep_b), Far(e_got_b)],
        [(e_part, BF)],
    )[0]
    e_other_y = swap_y(e_sum)
    input_grad, gain_one_part = call(
        input_kernel,
        [place_at, Far(grad_query_pre), Far(grad_kv_pre), Far(inputs[0]), Far(scale_one), gain_one,
         Far(query_weight), Far(kv_weight), Far(grad_residual)],
        [((tok, width), BF), ((1, width), F32)],
    )

    e_other_y, gain_one_part = tie(e_other_y, gain_one_part)
    e_zero_a, e_zero_b = call(pair_kernel, [place_at, Far(e_sum), Far(e_other_y)], [(e_part[1:], BF)] * 2)
    e_one_a, e_one_b = flip(e_zero_a, PAIRS_T), flip(e_zero_b, PAIRS_S)
    e_two_a, e_two_b = flip(e_zero_a, PAIRS_S), flip(e_zero_b, PAIRS_T)

    both_part = (groups, quarter, half + kv_width // 2)
    keep_a, send_a, keep_b, send_b = call(
        step_kernel,
        [place_at] + [Far(v) for v in (qo_keep_a, qo_got_a, kv_keep_a, kv_got_a, qo_keep_b,
                                       qo_got_b, kv_keep_b, kv_got_b)],
        [(both_part, BF)] * 4,
    )
    got_a, got_b = flip(send_a, PAIRS_T), flip(send_b, PAIRS_S)
    spare = HEAD_DIM
    gain_parts = jnp.stack([gain_one_part, gain_two_part]).reshape(2, groups, quarter, XS)
    gain_parts = gain_parts.transpose(1, 2, 0, 3).reshape(groups, quarter, 2 * XS).astype(BF)
    gain_parts = jnp.pad(gain_parts, ((0, 0), (0, 0), (0, spare - 2 * XS)))
    packed_width = both_part[-1] + spare
    packed = call(
        pack_kernel,
        [place_at, Far(keep_a), Far(got_a), Far(keep_b), Far(got_b), gain_parts],
        [Far((YLO, groups, quarter, packed_width), BF, 2)],
    )[0]
    packed, returned = tie(packed, returned)
    packed = exchange(packed.reshape(YLO * groups, quarter, packed_width), ("ylo", "fsdp"))
    mixture = t_dot(gate_high, returned) + t_dot(gate_low, returned)
    outputs = (residual + mixture).astype(BF)
    packed, outputs = tie(packed, outputs)
    packed = call(sum_kernel, [place_at, Far(packed)], [((YLO * XS, quarter, packed_width), BF)])[0]
    spreaded = exchange(packed, ("ylo", "x"))
    most = [e_zero_a, e_zero_b, e_one_a, e_one_b, e_two_a, e_two_b]
    *e_grads, most_mark = expert_outputs(
        expert_most_kernel, [place_at, *most, *[swap(v) for v in most]], [], e_part[1:], width, half
    )
    e_one_a, e_one_b, packed = tie(e_one_a, e_one_b, packed)
    e_three_a, e_three_b = flip(e_one_a, PAIRS_S), flip(e_one_b, PAIRS_T)
    e_three_a, e_three_b, most_mark = tie(e_three_a, e_three_b, most_mark)
    grad_gate, grad_up, grad_down, e_mark = expert_outputs(
        expert_rest_kernel,
        [place_at, e_three_a, e_three_b, swap(e_three_a), swap(e_three_b), most_mark,
         packed[0, :16, :HEAD_DIM]],
        e_grads,
        e_part[1:],
        width,
        half,
    )
    spreaded, e_mark = tie(spreaded, e_mark)
    grad_output_w, grad_query_w, grad_key_w, grad_value_w, gains_sum = call(
        final_kernel,
        [place_at, Far(spreaded), Far(swap(spreaded)), e_mark],
        [((rows, width), F32), ((rows, width), F32), ((rows, kv_width), F32),
         ((rows, kv_width), F32), ((quarter, spare), F32)],
    )
    gains_sum = gains_sum[:, : 2 * XS].reshape(quarter, 2, XS).transpose(1, 0, 2)
    gains_sum = gains_sum.reshape(2, rows)
    return (
        outputs[None],
        input_grad[None],
        gains_sum[0],
        grad_query_w,
        grad_key_w,
        grad_value_w,
        grad_output_w,
        gains_sum[1],
        grad_gate[None],
        grad_up[None],
        grad_down[None],
    )


def solution(mesh):
    shape = mesh.devices.shape
    fine = Mesh(
        mesh.devices.reshape(YLO, XS, CORES, shape[1]), ("ylo", "x", "core", "fsdp")
    )
    return jax.shard_map(
        body,
        mesh=fine,
        in_specs=(
            P(REP, "fsdp", None),
            P(REP, None),
            P("fsdp"),
            P("fsdp", None),
            P("fsdp", None),
            P("fsdp", None),
            P("fsdp", None),
            P("fsdp"),
            P(REP, "fsdp", None),
            P(REP, "fsdp", None),
            P(REP, "fsdp", None),
            P("fsdp", None, None),
            P("fsdp", None, None),
            P("fsdp", None, None),
            P(REP, "fsdp", None),
        ),
        out_specs=(
            P(REP, "fsdp", None),
            P(REP, "fsdp", None),
            P("fsdp"),
            P("fsdp", None),
            P("fsdp", None),
            P("fsdp", None),
            P("fsdp", None),
            P("fsdp"),
            P("fsdp", None, None),
            P("fsdp", None, None),
            P("fsdp", None, None),
        ),
        check_vma=False,
    )
```

time: 436 us -> 370 us (0.85)
  waiting for transfers between devices: 136 us -> 102 us
  local copies, waits for them, and re-layouts: 60.1 us -> 29.6 us
  starting transfers between devices: 108 us -> 97.5 us
  Pallas kernels: 103 us -> 111 us
    ppermute x18, waiting for transfers between devices: 60.3 us -> 23.1 us  [flip(): return lax.ppermute(v, 'x', pairs)]
    unnamed x160 -> x88, local copies, waits for them, and re-layouts: 35.4 us -> 11.5 us
    squeeze x4 -> x1, local copies, waits for them, and re-layouts: 11.2 us -> 1.28 us  [body(): packed[0, :16, :HEAD_DIM]]
    ppermute x18 -> x22, waiting for transfers between devices: 2.07 us -> 11.2 us  [swap(): return lax.ppermute(v, 'core', [(0, 1), (1, 0)])]
    pallas_call x22 -> x18, Pallas kernels: 103 us -> 111 us  [the longest x16 99.7 us: call(): pl.pallas_call(whole, out_shape=[jax.ShapeDtypeStruct(out.value, out.kind...]
    all_to_all x10 -> x9, waiting for transfers between devices: 73.1 us -> 65.9 us  [exchange(): return lax.all_to_all(v, axis, 0, 0, tiled=True)]
    all_to_all x10 -> x9, starting transfers between devices: 55.3 us -> 49.2 us  [exchange(): return lax.all_to_all(v, axis, 0, 0, tiled=True)]
    ppermute x18 -> x22, starting transfers between devices: 33.8 us -> 29 us  [swap(): return lax.ppermute(v, 'core', [(0, 1), (1, 0)])]
  transfers between devices with their start and end apart: 47 -> 50, of which waited for: 17 -> 20; matrix products, arithmetic and copies ran while one was open for 9% -> 8% of each run, Pallas kernels for 15% -> 28%
where the time goes in v1:
time: 370 us; the launch traced here: 363 us
  Pallas kernels  111 us (30%)
  waiting for transfers between devices  102 us (28%)
  starting transfers between devices  97.5 us (26%)
  local copies, waits for them, and re-layouts  29.6 us (8%)
  matrix products  11.3 us (3%)
  other arithmetic  9.35 us (3%)
    pallas_call x16, Pallas kernels, call(): pl.pallas_call(whole, out_shape=[jax.ShapeDtypeStruct(out.value, out.kind...  99.7 us
    all_to_all x9, waiting for transfers between devices, exchange(): return lax.all_to_all(v, axis, 0, 0, tiled=True)  65.9 us
    all_to_all x9, starting transfers between devices, exchange(): return lax.all_to_all(v, axis, 0, 0, tiled=True)  49.2 us
    ppermute x22, starting transfers between devices, swap(): return lax.ppermute(v, 'core', [(0, 1), (1, 0)])  29 us
    ppermute x18, waiting for transfers between devices, flip(): return lax.ppermute(v, 'x', pairs)  23.1 us
    ppermute x18, starting transfers between devices, flip(): return lax.ppermute(v, 'x', pairs)  18.9 us
    unnamed x88, local copies, waits for them, and re-layouts  11.5 us
    pallas_call x2, Pallas kernels, expert_outputs(): pl.pallas_call(kernel, out_shape=shapes, in_specs=[pl.BlockSpec(memory_sp...  11.4 us
  transfers between devices with their start and end apart: 50, of which 20 were waited for; matrix products, arithmetic and copies ran while one was open for 8% of the time, Pallas kernels for 28%

profile of v1, /device:TPU:1, one launch (start us, length us, event | category | flops | bytes accessed | tf_op | source)
XLA Modules:
  0.0 362.9 jit_solution(16534347676676166135)
XLA Ops:
  7.0 8.6 %all-to-all-start = ((bf16[8,136,1536]{2,1,0:T(8,128)(2,1)}), bf16[8,136,1536]{2,1,0:T(8,128)(2,1)}, u32[]{:S(2)}, u32[]{:S(2)}) async-start(bf16[8,136,1536]{2,1,0:T(8,128)(2,1)} %broadcast_in_dim.85), calls=%async_computation | async-start | bytes 6684672 | tf_op jit(solution)/shard_map/all_to_all | solution.py:639
  25.4 31.3 %all-to-all-done = bf16[8,136,1536]{2,1,0:T(8,128)(2,1)} async-done(((bf16[8,136,1536]{2,1,0:T(8,128)(2,1)}), bf16[8,136,1536]{2,1,0:T(8,128)(2,1)}, u32[]{:S(2)}, u32[]{:S(2)}) %all-to-all-start) | async-done | bytes 3342368 | tf_op jit(solution)/shard_map/all_to_all | solution.py:639
  61.9 4.0 %shard_map.230 = (bf16[128,1536]{1,0:T(8,128)(2,1)}, f32[128,128]{1,0:T(8,128)}, bf16[8,128,512]{2,1,0:T(8,128)(2,1)}, bf16[1536,512]{1,0:T(8,128)(2,1)}) custom-call(s32[4]{0:T(128)} %pad_add_fusion.refs_0_.place, bf16[128,1536]{1,0:T(8,128)(2,1)} %bitcast.91, f32[1,1536]{1,0:T(1,128)} %reshape.240.refs_2_.refs_5_, bf16[8,32,1536]{2,1,0:T(8,128)(2,1)} %copy-done.5, ...), custom_call_target="tpu_custom_call" | custom-call | tf_op jit(solution)/shard_map/pallas_call | solution.py:612
  65.9 3.6 all-to-all-start.1
  75.7 10.7 %all-to-all-done.1 = bf16[8,128,512]{2,1,0:T(8,128)(2,1)S(1)} async-done(((bf16[8,128,512]{2,1,0:T(8,128)(2,1)}), bf16[8,128,512]{2,1,0:T(8,128)(2,1)S(1)}, u32[]{:S(2)}, u32[]{:S(2)}) %all-to-all-start.1) | async-done | bytes 1048608 | tf_op jit(solution)/shard_map/all_to_all | solution.py:639
  87.4 4.3 %all-to-all-start.2 = ((bf16[8,80,1536]{2,1,0:T(8,128)(2,1)}), bf16[8,80,1536]{2,1,0:T(8,128)(2,1)}, u32[]{:S(2)}, u32[]{:S(2)}) async-start(bf16[8,80,1536]{2,1,0:T(8,128)(2,1)} %bitcast.84), calls=%async_computation.2 | async-start | bytes 3932160 | tf_op jit(solution)/shard_map/all_to_all | solution.py:639
  93.1 7.0 %collective-permute-done.1.refs_10_ = bf16[8,96,768]{2,1,0:T(8,128)(2,1)} collective-permute-done((bf16[8,96,768]{2,1,0:T(8,128)(2,1)}, bf16[8,96,768]{2,1,0:T(8,128)(2,1)}, u32[]{:S(2)}, u32[]{:S(2)}) %collective-permute-start.1) | collective-permute-done | bytes 1179680 | tf_op jit(solution)/shard_map/ppermute | solution.py:661
  107.1 12.7 %shard_map.231 = (bf16[8,192,1536]{2,1,0:T(8,128)(2,1)}, bf16[8,192,1536]{2,1,0:T(8,128)(2,1)}, bf16[128,1536]{1,0:T(8,128)(2,1)}, bf16[128,1536]{1,0:T(8,128)(2...) custom-call(s32[4]{0:T(128)} %pad_add_fusion.refs_0_.place, ...), custom_call_target="tpu_custom_call" | custom-call | tf_op jit(solution)/shard_map/pallas_call | solution.py:612
  119.8 6.6 %all-to-all-start.3 = ((bf16[8,80,1536]{2,1,0:T(8,128)(2,1)}), bf16[8,80,1536]{2,1,0:T(8,128)(2,1)}, u32[]{:S(2)}, u32[]{:S(2)}) async-start(bf16[8,80,1536]{2,1,0:T(8,128)(2,1)} %bitcast.97), calls=%async_computation.3 | async-start | bytes 3932160 | tf_op jit(solution)/shard_map/all_to_all | solution.py:639
  128.5 4.6 %fusion.3.refs_2_ = f32[640,768]{1,0:T(8,128)} fusion(bf16[640,1536]{1,0:T(8,128)(2,1)} %bitcast.19.refs_7_, bf16[1,768,1536]{2,1,0:T(8,128)(2,1)S(1)} %copy-done), kind=kOutput, calls=%fused_computation.6 | convolution fusion | flops 1509949440 | bytes 6291456 | tf_op jit(solution)/shard_map/dot_general | solution.py:41
  133.1 19.9 %all-to-all-done.3 = bf16[8,80,1536]{2,1,0:T(8,128)(2,1)} async-done(((bf16[8,80,1536]{2,1,0:T(8,128)(2,1)}), bf16[8,80,1536]{2,1,0:T(8,128)(2,1)}, u32[]{:S(2)}, u32[]{:S(2)}) %all-to-all-start.3) | async-done | bytes 1966112 | tf_op jit(solution)/shard_map/all_to_all | solution.py:639
  154.7 11.7 %shard_map.232 = (bf16[640,768]{1,0:T(8,128)(2,1)}, bf16[640,768]{1,0:T(8,128)(2,1)}, bf16[640,768]{1,0:T(8,128)(2,1)}, bf16[640,1536]{1,0:T(8,128)(2,1)}) custom-call(s32[4]{0:T(128)} %pad_add_fusion.refs_0_.place, bf16[640,1536]{1,0:T(8,128)(2,1)} %bitcast.21.refs_1_, f32[640,768]{1,0:T(8,128)} %fusion.3.refs_2_, bf16[1536,768]{1,0:T(8,128)(2,1)} %bitcast.94, ...), custom_call_target="tpu_custom_call" | custom-call | tf_op jit(solution)/shard_map/pallas_call | solution.py:612
  166.4 4.5 %all-to-all-start.4 = ((bf16[8,80,1536]{2,1,0:T(8,128)(2,1)}), bf16[8,80,1536]{2,1,0:T(8,128)(2,1)}, u32[]{:S(2)}, u32[]{:S(2)}) async-start(bf16[8,80,1536]{2,1,0:T(8,128)(2,1)} %bitcast.98), calls=%async_computation.4 | async-start | bytes 3932160 | tf_op jit(solution)/shard_map/all_to_all | solution.py:639
  175.9 12.9 %shard_map.233 = (bf16[2,288,768]{2,1,0:T(8,128)(2,1)}, bf16[2,288,768]{2,1,0:T(8,128)(2,1)}, bf16[2,288,768]{2,1,0:T(8,128)(2,1)}, bf16[2,288,768]{2,1,0:T(8,128)(2,1)}) custom-call(s32[4]{0:T(128)} %pad_add_fusion.refs_0_.place, bf16[640,1536]{1,0:T(8,128)(2,1)} %bitcast.21.refs_1_, bf16[640,1536]{1,0:T(8,128)(2,1)} %collective-permute-done.9.refs_2_, ...), custom_call_target="tpu_custom_call" | custom-call | tf_op jit(solution)/shard_map/pallas_call | solution.py:612
  194.0 4.1 %all-to-all-done.4 = bf16[8,80,1536]{2,1,0:T(8,128)(2,1)} async-done(((bf16[8,80,1536]{2,1,0:T(8,128)(2,1)}), bf16[8,80,1536]{2,1,0:T(8,128)(2,1)}, u32[]{:S(2)}, u32[]{:S(2)}) %all-to-all-start.4) | async-done | bytes 1966112 | tf_op jit(solution)/shard_map/all_to_all | solution.py:639
  198.1 12.1 %shard_map.234 = (f32[128,1536]{1,0:T(8,128)}, bf16[128,1536]{1,0:T(8,128)(2,1)}, f32[1,1536]{1,0:T(1,128)}, bf16[128,1536]{1,0:T(8,128)(2,1)}, bf16[1024,512]{1,0:T(8,128)(2,1)}, /*index=5*/bf16[2,128,768]{2,1,0:T(8,128)(2,1)}) custom-call(s32[4]{0:T(128)} %pad_add_fusion.refs_0_.place, bf16[640,1536]{1,0:T(8,128)(2,1)} %bitcast.26.refs_1_, ...), custom_call_target="tpu_custom_call" | custom-call | tf_op jit(solution)/shard_map/pallas_call | solution.py:612
  210.2 3.7 %all-to-all-start.5 = ((bf16[8,128,512]{2,1,0:T(8,128)(2,1)}), bf16[8,128,512]{2,1,0:T(8,128)(2,1)S(1)}, u32[]{:S(2)}, u32[]{:S(2)}) async-start(bf16[8,128,512]{2,1,0:T(8,128)(2,1)} %bitcast.101), calls=%async_computation.5 | async-start | bytes 2097152 | tf_op jit(solution)/shard_map/all_to_all | solution.py:639
  215.8 3.9 %shard_map.235 = (bf16[288,768]{1,0:T(8,128)(2,1)}, bf16[288,768]{1,0:T(8,128)(2,1)}, bf16[288,768]{1,0:T(8,128)(2,1)}, bf16[288,768]{1,0:T(8,128)(2,1)}) custom-call(s32[4]{0:T(128)} %pad_add_fusion.refs_0_.place, bf16[2,288,768]{2,1,0:T(8,128)(2,1)} %get-tuple-element.146.refs_1_, bf16[2,288,768]{2,1,0:T(8,128)(2,1)} %copy-done.17, ...), custom_call_target="tpu_custom_call" | custom-call | tf_op jit(solution)/shard_map/pallas_call | solution.py:612
  224.1 6.9 %shard_map.236 = (bf16[8,2,48,768]{3,2,1,0:T(8,128)(2,1)}, bf16[8,2,48,768]{3,2,1,0:T(8,128)(2,1)}, bf16[8,2,48,768]{3,2,1,0:T(8,128)(2,1)}, bf16[8,2,48,768]{3,2,1,0:T(8,128)(2,1)}) custom-call(s32[4]{0:T(128)} %pad_add_fusion.refs_0_.place, bf16[128,1536]{1,0:T(8,128)(2,1)} %get-tuple-element.122.refs_1_, ...), custom_call_target="tpu_custom_call" | custom-call | tf_op jit(solution)/shard_map/pallas_call | solution.py:612
  235.0 6.8 %all-to-all-start.6 = ((bf16[8,80,1536]{2,1,0:T(8,128)(2,1)}), bf16[8,80,1536]{2,1,0:T(8,128)(2,1)S(1)}, u32[]{:S(2)}, u32[]{:S(2)}) async-start(bf16[8,80,1536]{2,1,0:T(8,128)(2,1)} %bitcast.96), calls=%async_computation.6 | async-start | bytes 3932160 | tf_op jit(solution)/shard_map/all_to_all | solution.py:639
  257.2 6.1 %collective-permute-done.18.refs_4_ = bf16[8,2,48,128]{3,2,1,0:T(8,128)(2,1)S(1)} collective-permute-done((bf16[8,2,48,128]{3,2,1,0:T(8,128)(2,1)}, bf16[8,2,48,128]{3,2,1,0:T(8,128)(2,1)S(1)}, u32[]{:S(2)}, u32[]{:S(2)}) %collective-permute-start.18) | collective-permute-done | bytes 196640 | tf_op jit(solution)/shard_map/ppermute | solution.py:661
  266.7 4.9 %shard_map.239 = (bf16[8,48,896]{2,1,0:T(8,128)(2,1)}, bf16[8,48,896]{2,1,0:T(8,128)(2,1)}, bf16[8,48,896]{2,1,0:T(8,128)(2,1)}, bf16[8,48,896]{2,1,0:T(8,128)(2,1)}) custom-call(s32[4]{0:T(128)} %pad_add_fusion.refs_0_.place, bf16[8,2,48,768]{3,2,1,0:T(8,128)(2,1)} %get-tuple-element.153.refs_1_, bf16[8,2,48,768]{3,2,1,0:T(8,128)(2,1)} %copy-done.10, ...), custom_call_target="tpu_custom_call" | custom-call | tf_op jit(solution)/shard_map/pallas_call | solution.py:612
  273.0 7.2 %shard_map.241 = (bf16[128,1536]{1,0:T(8,128)(2,1)}, f32[1,1536]{1,0:T(1,128)}) custom-call(s32[4]{0:T(128)} %pad_add_fusion.refs_0_.place, bf16[128,1536]{1,0:T(8,128)(2,1)} %get-tuple-element.144.refs_6_.refs_1_, bf16[128,512]{1,0:T(8,128)(2,1)} %get-tuple-element.158.refs_3_.refs_2_, bf16[128,1536]{1,0:T(8,128)(2,1)} %bitcast.93, ...), custom_call_target="tpu_custom_call" | custom-call | tf_op jit(solution)/shard_map/pallas_call | solution.py:612
  284.4 4.2 %collective-permute-done.21.refs_2_ = bf16[8,48,896]{2,1,0:T(8,128)(2,1)S(1)} collective-permute-done((bf16[8,48,896]{2,1,0:T(8,128)(2,1)}, bf16[8,48,896]{2,1,0:T(8,128)(2,1)S(1)}, u32[]{:S(2)}, u32[]{:S(2)}) %collective-permute-start.21) | collective-permute-done | bytes 688160 | tf_op jit(solution)/shard_map/ppermute | solution.py:661
  289.4 3.7 %shard_map.242 = bf16[2,8,48,1024]{3,2,1,0:T(8,128)(2,1)} custom-call(s32[4]{0:T(128)} %pad_add_fusion.refs_0_.place, bf16[8,48,896]{2,1,0:T(8,128)(2,1)} %get-tuple-element.166.refs_1_, bf16[8,48,896]{2,1,0:T(8,128)(2,1)} %copy-done.19, bf16[8,48,896]{2,1,0:T(8,128)(2,1)} %get-tuple-element.168.refs_3_, ...), custom_call_target="tpu_custom_call" | custom-call | tf_op jit(solution)/shard_map/pallas_call | solution.py:612
  293.2 7.2 %all-to-all-start.7 = ((bf16[16,48,1024]{2,1,0:T(8,128)(2,1)}), bf16[16,48,1024]{2,1,0:T(8,128)(2,1)}, u32[]{:S(2)}, u32[]{:S(2)}) async-start(bf16[16,48,1024]{2,1,0:T(8,128)(2,1)} %bitcast.85), calls=%async_computation.7 | async-start | bytes 3145728 | tf_op jit(solution)/shard_map/all_to_all | solution.py:639
  307.9 3.8 %collective-permute-start.32 = (bf16[288,768]{1,0:T(8,128)(2,1)}, bf16[288,768]{1,0:T(8,128)(2,1)S(1)}, u32[]{:S(2)}, u32[]{:S(2)}) collective-permute-start(bf16[288,768]{1,0:T(8,128)(2,1)} %get-tuple-element.190.refs_0_), channel_id=1, source_target_pairs={{0,8},{8,0},{1,9},{9,1},{2,10},{10,2},{3,11},{11,3},{4,12},{12,4},... | collective-permute-start | bytes 1327112 | tf_op jit(solution)/shard_map/ppermute | solution.py:631
  314.2 6.9 %collective-permute-start.33 = (bf16[288,768]{1,0:T(8,128)(2,1)}, bf16[288,768]{1,0:T(8,128)(2,1)S(1)}, u32[]{:S(2)}, u32[]{:S(2)}) collective-permute-start(bf16[288,768]{1,0:T(8,128)(2,1)} %get-tuple-element.191.refs_1_), channel_id=1, source_target_pairs={{0,8},{8,0},{1,9},{9,1},{2,10},{10,2},{3,11},{11,3},{4,12},{12,4},... | collective-permute-start | bytes 1327112 | tf_op jit(solution)/shard_map/ppermute | solution.py:631
  329.4 3.9 %all-to-all-start.8 = ((bf16[8,48,1024]{2,1,0:T(8,128)(2,1)}), bf16[8,48,1024]{2,1,0:T(8,128)(2,1)S(1)}, u32[]{:S(2)}, u32[]{:S(2)}) async-start(bf16[8,48,1024]{2,1,0:T(8,128)(2,1)} %shard_map.243), calls=%async_computation.8 | async-start | bytes 1572864 | tf_op jit(solution)/shard_map/all_to_all | solution.py:639
  335.0 7.3 %shard_map.245 = (f32[1536,768]{1,0:T(8,128)}, f32[1536,768]{1,0:T(8,128)}, f32[768,1536]{1,0:T(8,128)}, f32[8,128]{1,0:T(8,128)}) custom-call(s32[4]{0:T(128)} %pad_add_fusion.refs_0_.place, bf16[288,768]{1,0:T(8,128)(2,1)} %get-tuple-element.190.refs_0_, bf16[288,768]{1,0:T(8,128)(2,1)} %get-tuple-element.191.refs_1_, ...), custom_call_target="tpu_custom_call" | custom-call | tf_op jit(solution)/shard_map/pallas_call | solution.py:307
  349.4 4.1 %shard_map.246 = (f32[1536,768]{1,0:T(8,128)}, f32[1536,768]{1,0:T(8,128)}, f32[768,1536]{1,0:T(8,128)}, f32[8,128]{1,0:T(8,128)}) custom-call(s32[4]{0:T(128)} %pad_add_fusion.refs_0_.place, bf16[288,768]{1,0:T(8,128)(2,1)} %copy-done.24, bf16[288,768]{1,0:T(8,128)(2,1)} %copy-done.25, ...), custom_call_target="tpu_custom_call", output_to_operand_aliasing={{0}: (7, {}), {1}: (8, {}), {2}: (9, {})} | custom-call | tf_op jit(solution)/shard_map/pallas_call | solution.py:307
  356.7 3.7 %shard_map.247 = (f32[192,1536]{1,0:T(8,128)}, f32[192,1536]{1,0:T(8,128)}, f32[192,256]{1,0:T(8,128)}, f32[192,256]{1,0:T(8,128)}, f32[48,128]{1,0:T(8,128)}) custom-call(s32[4]{0:T(128)} %pad_add_fusion.refs_0_.place, bf16[8,48,1024]{2,1,0:T(8,128)(2,1)} %copy-done.4, bf16[8,48,1024]{2,1,0:T(8,128)(2,1)} %copy-done.18, f32[8,128]{1,0:T(8,128)} %get-tuple-element.204.refs_3_), custom_call_target="tpu_custom_call" | custom-call | tf_op jit(solution)/shard_map/pallas_call | solution.py:612
  (240 shorter events, 118.4 us)
Async XLA Ops:
  7.0 49.6 %all-to-all-start = ((bf16[8,136,1536]{2,1,0:T(8,128)(2,1)}), bf16[8,136,1536]{2,1,0:T(8,128)(2,1)}, u32[]{:S(2)}, u32[]{:S(2)}) async-start(bf16[8,136,1536]{2,1,0:T(8,128)(2,1)} %broadcast_in_dim.85), calls=%async_computation | async-start | bytes 6684672 | tf_op jit(solution)/shard_map/all_to_all | solution.py:639
  65.9 20.5 %all-to-all-start.1 = ((bf16[8,128,512]{2,1,0:T(8,128)(2,1)}), bf16[8,128,512]{2,1,0:T(8,128)(2,1)S(1)}, u32[]{:S(2)}, u32[]{:S(2)}) async-start(bf16[8,128,512]{2,1,0:T(8,128)(2,1)} %get-tuple-element.118), calls=%async_computation.1 | async-start | bytes 2097152 | tf_op jit(solution)/shard_map/all_to_all | solution.py:639
  72.7 27.5 %collective-permute-start.1 = (bf16[8,96,768]{2,1,0:T(8,128)(2,1)}, bf16[8,96,768]{2,1,0:T(8,128)(2,1)}, u32[]{:S(2)}, u32[]{:S(2)}) collective-permute-start(bf16[8,96,768]{2,1,0:T(8,128)(2,1)} %get-tuple-element.216.refs_9_), channel_id=1, source_target_pairs={{0,16},{16,0},{32,48},{48,32},{1,17},{17,1},{33,49},{49,33},{2,18}... | collective-permute-start | bytes 3538952 | tf_op jit(solution)/shard_map/ppermute | solution.py:661
  73.9 28.4 %collective-permute-start.4 = (bf16[8,96,768]{2,1,0:T(8,128)(2,1)}, bf16[8,96,768]{2,1,0:T(8,128)(2,1)}, u32[]{:S(2)}, u32[]{:S(2)}) collective-permute-start(bf16[8,96,768]{2,1,0:T(8,128)(2,1)} %get-tuple-element.215.refs_13_), channel_id=1, source_target_pairs={{0,48},{48,0},{16,32},{32,16},{1,49},{49,1},{17,33},{33,17},{2,50}... | collective-permute-start | bytes 3538952 | tf_op jit(solution)/shard_map/ppermute | solution.py:661
  87.4 32.4 %all-to-all-start.2 = ((bf16[8,80,1536]{2,1,0:T(8,128)(2,1)}), bf16[8,80,1536]{2,1,0:T(8,128)(2,1)}, u32[]{:S(2)}, u32[]{:S(2)}) async-start(bf16[8,80,1536]{2,1,0:T(8,128)(2,1)} %bitcast.84), calls=%async_computation.2 | async-start | bytes 3932160 | tf_op jit(solution)/shard_map/all_to_all | solution.py:639
  91.7 13.3 %collective-permute-start.2 = (bf16[8,96,768]{2,1,0:T(8,128)(2,1)}, bf16[8,96,768]{2,1,0:T(8,128)(2,1)S(1)}, u32[]{:S(2)}, u32[]{:S(2)}) collective-permute-start(bf16[8,96,768]{2,1,0:T(8,128)(2,1)} %get-tuple-element.216.refs_9_), channel_id=1, source_target_pairs={{0,8},{8,0},{1,9},{9,1},{2,10},{10,2},{3,11},{11,3},{4,12},{12,4},... | collective-permute-start | bytes 3538952 | tf_op jit(solution)/shard_map/ppermute | solution.py:631
  93.1 11.9 %collective-permute-start.5 = (bf16[8,96,768]{2,1,0:T(8,128)(2,1)}, bf16[8,96,768]{2,1,0:T(8,128)(2,1)}, u32[]{:S(2)}, u32[]{:S(2)}) collective-permute-start(bf16[8,96,768]{2,1,0:T(8,128)(2,1)} %get-tuple-element.215.refs_13_), channel_id=1, source_target_pairs={{0,8},{8,0},{1,9},{9,1},{2,10},{10,2},{3,11},{11,3},{4,12},{12,4},... | collective-permute-start | bytes 3538952 | tf_op jit(solution)/shard_map/ppermute | solution.py:631
  119.8 33.1 %all-to-all-start.3 = ((bf16[8,80,1536]{2,1,0:T(8,128)(2,1)}), bf16[8,80,1536]{2,1,0:T(8,128)(2,1)}, u32[]{:S(2)}, u32[]{:S(2)}) async-start(bf16[8,80,1536]{2,1,0:T(8,128)(2,1)} %bitcast.97), calls=%async_computation.3 | async-start | bytes 3932160 | tf_op jit(solution)/shard_map/all_to_all | solution.py:639
  153.0 22.0 %collective-permute-start.9 = (bf16[640,1536]{1,0:T(8,128)(2,1)}, bf16[640,1536]{1,0:T(8,128)(2,1)}, u32[]{:S(2)}, u32[]{:S(2)}) collective-permute-start(bf16[640,1536]{1,0:T(8,128)(2,1)} %bitcast.21.refs_1_), channel_id=1, source_target_pairs={{0,8},{8,0},{1,9},{9,1},{2,10},{10,2},{3,11},{11,3},{4,12},{12,4},... | collective-permute-start | bytes 5898248 | tf_op jit(solution)/shard_map/ppermute | solution.py:631
  166.4 31.7 %all-to-all-start.4 = ((bf16[8,80,1536]{2,1,0:T(8,128)(2,1)}), bf16[8,80,1536]{2,1,0:T(8,128)(2,1)}, u32[]{:S(2)}, u32[]{:S(2)}) async-start(bf16[8,80,1536]{2,1,0:T(8,128)(2,1)} %bitcast.98), calls=%async_computation.4 | async-start | bytes 3932160 | tf_op jit(solution)/shard_map/all_to_all | solution.py:639
  188.8 26.0 %collective-permute-start.14 = (bf16[2,288,768]{2,1,0:T(8,128)(2,1)}, bf16[2,288,768]{2,1,0:T(8,128)(2,1)S(1)}, u32[]{:S(2)}, u32[]{:S(2)}) collective-permute-start(bf16[2,288,768]{2,1,0:T(8,128)(2,1)} %get-tuple-element.147), channel_id=1, source_target_pairs={{0,16},{16,0},{32,48},{48,32},{1,17},{17,1},{33,49},{49,33},{2,18}... | collective-permute-start | bytes 2654216 | tf_op jit(solution)/shard_map/ppermute | solution.py:661
  188.9 26.0 %collective-permute-start.15 = (bf16[2,288,768]{2,1,0:T(8,128)(2,1)}, bf16[2,288,768]{2,1,0:T(8,128)(2,1)}, u32[]{:S(2)}, u32[]{:S(2)}) collective-permute-start(bf16[2,288,768]{2,1,0:T(8,128)(2,1)} %get-tuple-element.149), channel_id=1, source_target_pairs={{0,48},{48,0},{16,32},{32,16},{1,49},{49,1},{17,33},{33,17},{2,50}... | collective-permute-start | bytes 2654216 | tf_op jit(solution)/shard_map/ppermute | solution.py:661
  210.2 23.8 %all-to-all-start.5 = ((bf16[8,128,512]{2,1,0:T(8,128)(2,1)}), bf16[8,128,512]{2,1,0:T(8,128)(2,1)S(1)}, u32[]{:S(2)}, u32[]{:S(2)}) async-start(bf16[8,128,512]{2,1,0:T(8,128)(2,1)} %bitcast.101), calls=%async_computation.5 | async-start | bytes 2097152 | tf_op jit(solution)/shard_map/all_to_all | solution.py:639
  219.7 22.2 %collective-permute-start.23 = (bf16[288,768]{1,0:T(8,128)(2,1)}, bf16[288,768]{1,0:T(8,128)(2,1)}, u32[]{:S(2)}, u32[]{:S(2)}) collective-permute-start(bf16[288,768]{1,0:T(8,128)(2,1)} %get-tuple-element.171), channel_id=1, source_target_pairs={{0,48},{48,0},{16,32},{32,16},{1,49},{49,1},{17,33},{33,17},{2,50}... | collective-permute-start | bytes 1327112 | tf_op jit(solution)/shard_map/ppermute | solution.py:661
  221.6 20.3 %collective-permute-start.24 = (bf16[288,768]{1,0:T(8,128)(2,1)}, bf16[288,768]{1,0:T(8,128)(2,1)}, u32[]{:S(2)}, u32[]{:S(2)}) collective-permute-start(bf16[288,768]{1,0:T(8,128)(2,1)} %get-tuple-element.173), channel_id=1, source_target_pairs={{0,16},{16,0},{32,48},{48,32},{1,17},{17,1},{33,49},{49,33},{2,18}... | collective-permute-start | bytes 1327112 | tf_op jit(solution)/shard_map/ppermute | solution.py:661
  231.0 34.6 %collective-permute-start.16 = (bf16[8,2,48,768]{3,2,1,0:T(8,128)(2,1)}, bf16[8,2,48,768]{3,2,1,0:T(8,128)(2,1)S(1)}, u32[]{:S(2)}, u32[]{:S(2)}) collective-permute-start(bf16[8,2,48,768]{3,2,1,0:T(8,128)(2,1)} %get-tuple-element.154), channel_id=1, source_target_pairs={{0,16},{16,0},{32,48},{48,32},{1,17},{17,1},{33,49},{49,33},{2,18}... | collective-permute-start | bytes 3538952 | tf_op jit(solution)/shard_map/ppermute | solution.py:661
  232.8 32.9 %collective-permute-start.19 = (bf16[8,2,48,768]{3,2,1,0:T(8,128)(2,1)}, bf16[8,2,48,768]{3,2,1,0:T(8,128)(2,1)}, u32[]{:S(2)}, u32[]{:S(2)}) collective-permute-start(bf16[8,2,48,768]{3,2,1,0:T(8,128)(2,1)} %get-tuple-element.163), channel_id=1, source_target_pairs={{0,48},{48,0},{16,32},{32,16},{1,49},{49,1},{17,33},{33,17},{2,50}... | collective-permute-start | bytes 3538952 | tf_op jit(solution)/shard_map/ppermute | solution.py:661
  235.0 58.1 %all-to-all-start.6 = ((bf16[8,80,1536]{2,1,0:T(8,128)(2,1)}), bf16[8,80,1536]{2,1,0:T(8,128)(2,1)S(1)}, u32[]{:S(2)}, u32[]{:S(2)}) async-start(bf16[8,80,1536]{2,1,0:T(8,128)(2,1)} %bitcast.96), calls=%async_computation.6 | async-start | bytes 3932160 | tf_op jit(solution)/shard_map/all_to_all | solution.py:639
  245.1 37.4 %collective-permute-start.25 = (bf16[2,288,768]{2,1,0:T(8,128)(2,1)}, bf16[2,288,768]{2,1,0:T(8,128)(2,1)}, u32[]{:S(2)}, u32[]{:S(2)}) collective-permute-start(bf16[2,288,768]{2,1,0:T(8,128)(2,1)} %shard_map.240.refs_1_), channel_id=1, source_target_pairs={{0,64},{64,0},{1,65},{65,1},{2,66},{66,2},{3,67},{67,3},{4,68},{68... | collective-permute-start | bytes 2654216 | tf_op jit(solution)/shard_map/ppermute | solution.py:635
  255.3 10.3 %collective-permute-start.20 = (bf16[8,2,48,128]{3,2,1,0:T(8,128)(2,1)}, bf16[8,2,48,128]{3,2,1,0:T(8,128)(2,1)S(1)}, u32[]{:S(2)}, u32[]{:S(2)}) collective-permute-start(bf16[8,2,48,128]{3,2,1,0:T(8,128)(2,1)} %get-tuple-element.165), channel_id=1, source_target_pairs={{0,48},{48,0},{16,32},{32,16},{1,49},{49,1},{17,33},{33,17},{2,50}... | collective-permute-start | bytes 589832 | tf_op jit(solution)/shard_map/ppermute | solution.py:661
  271.7 16.9 %collective-permute-start.21 = (bf16[8,48,896]{2,1,0:T(8,128)(2,1)}, bf16[8,48,896]{2,1,0:T(8,128)(2,1)S(1)}, u32[]{:S(2)}, u32[]{:S(2)}) collective-permute-start(bf16[8,48,896]{2,1,0:T(8,128)(2,1)} %get-tuple-element.167), channel_id=1, source_target_pairs={{0,48},{48,0},{16,32},{32,16},{1,49},{49,1},{17,33},{33,17},{2,50}... | collective-permute-start | bytes 2064392 | tf_op jit(solution)/shard_map/ppermute | solution.py:661
  272.6 16.0 %collective-permute-start.22 = (bf16[8,48,896]{2,1,0:T(8,128)(2,1)}, bf16[8,48,896]{2,1,0:T(8,128)(2,1)}, u32[]{:S(2)}, u32[]{:S(2)}) collective-permute-start(bf16[8,48,896]{2,1,0:T(8,128)(2,1)} %get-tuple-element.169), channel_id=1, source_target_pairs={{0,16},{16,0},{32,48},{48,32},{1,17},{17,1},{33,49},{49,33},{2,18}... | collective-permute-start | bytes 2064392 | tf_op jit(solution)/shard_map/ppermute | solution.py:661
  293.2 29.7 %all-to-all-start.7 = ((bf16[16,48,1024]{2,1,0:T(8,128)(2,1)}), bf16[16,48,1024]{2,1,0:T(8,128)(2,1)}, u32[]{:S(2)}, u32[]{:S(2)}) async-start(bf16[16,48,1024]{2,1,0:T(8,128)(2,1)} %bitcast.85), calls=%async_computation.7 | async-start | bytes 3145728 | tf_op jit(solution)/shard_map/all_to_all | solution.py:639
  303.6 10.6 %collective-permute-start.26 = (bf16[288,768]{1,0:T(8,128)(2,1)}, bf16[288,768]{1,0:T(8,128)(2,1)}, u32[]{:S(2)}, u32[]{:S(2)}) collective-permute-start(bf16[288,768]{1,0:T(8,128)(2,1)} %get-tuple-element.190.refs_0_), channel_id=1, source_target_pairs={{0,48},{48,0},{16,32},{32,16},{1,49},{49,1},{17,33},{33,17},{2,50}... | collective-permute-start | bytes 1327112 | tf_op jit(solution)/shard_map/ppermute | solution.py:661
  304.6 16.5 %collective-permute-start.27 = (bf16[288,768]{1,0:T(8,128)(2,1)}, bf16[288,768]{1,0:T(8,128)(2,1)}, u32[]{:S(2)}, u32[]{:S(2)}) collective-permute-start(bf16[288,768]{1,0:T(8,128)(2,1)} %get-tuple-element.191.refs_1_), channel_id=1, source_target_pairs={{0,16},{16,0},{32,48},{48,32},{1,17},{17,1},{33,49},{49,33},{2,18}... | collective-permute-start | bytes 1327112 | tf_op jit(solution)/shard_map/ppermute | solution.py:661
  304.6 21.5 %collective-permute-start.30 = (bf16[288,768]{1,0:T(8,128)(2,1)}, bf16[288,768]{1,0:T(8,128)(2,1)}, u32[]{:S(2)}, u32[]{:S(2)}) collective-permute-start(bf16[288,768]{1,0:T(8,128)(2,1)} %get-tuple-element.190.refs_0_), channel_id=1, source_target_pairs={{0,16},{16,0},{32,48},{48,32},{1,17},{17,1},{33,49},{49,33},{2,18}... | collective-permute-start | bytes 1327112 | tf_op jit(solution)/shard_map/ppermute | solution.py:661
  306.0 21.2 %collective-permute-start.31 = (bf16[288,768]{1,0:T(8,128)(2,1)}, bf16[288,768]{1,0:T(8,128)(2,1)}, u32[]{:S(2)}, u32[]{:S(2)}) collective-permute-start(bf16[288,768]{1,0:T(8,128)(2,1)} %get-tuple-element.191.refs_1_), channel_id=1, source_target_pairs={{0,48},{48,0},{16,32},{32,16},{1,49},{49,1},{17,33},{33,17},{2,50}... | collective-permute-start | bytes 1327112 | tf_op jit(solution)/shard_map/ppermute | solution.py:661
  307.9 19.5 %collective-permute-start.32 = (bf16[288,768]{1,0:T(8,128)(2,1)}, bf16[288,768]{1,0:T(8,128)(2,1)S(1)}, u32[]{:S(2)}, u32[]{:S(2)}) collective-permute-start(bf16[288,768]{1,0:T(8,128)(2,1)} %get-tuple-element.190.refs_0_), channel_id=1, source_target_pairs={{0,8},{8,0},{1,9},{9,1},{2,10},{10,2},{3,11},{11,3},{4,12},{12,4},... | collective-permute-start | bytes 1327112 | tf_op jit(solution)/shard_map/ppermute | solution.py:631
  314.2 13.6 %collective-permute-start.33 = (bf16[288,768]{1,0:T(8,128)(2,1)}, bf16[288,768]{1,0:T(8,128)(2,1)S(1)}, u32[]{:S(2)}, u32[]{:S(2)}) collective-permute-start(bf16[288,768]{1,0:T(8,128)(2,1)} %get-tuple-element.191.refs_1_), channel_id=1, source_target_pairs={{0,8},{8,0},{1,9},{9,1},{2,10},{10,2},{3,11},{11,3},{4,12},{12,4},... | collective-permute-start | bytes 1327112 | tf_op jit(solution)/shard_map/ppermute | solution.py:631
  327.8 14.5 %collective-permute-start.28 = (bf16[288,768]{1,0:T(8,128)(2,1)}, bf16[288,768]{1,0:T(8,128)(2,1)S(1)}, u32[]{:S(2)}, u32[]{:S(2)}) collective-permute-start(bf16[288,768]{1,0:T(8,128)(2,1)} %collective-permute-done.26.refs_2_), channel_id=1, source_target_pairs={{0,16},{16,0},{32,48},{48,32},{1,17},{17,1},{33,49},{49,33},{2,18}... | collective-permute-start | bytes 1327112 | tf_op jit(solution)/shard_map/ppermute | solution.py:661
  327.8 14.5 %collective-permute-start.29 = (bf16[288,768]{1,0:T(8,128)(2,1)}, bf16[288,768]{1,0:T(8,128)(2,1)S(1)}, u32[]{:S(2)}, u32[]{:S(2)}) collective-permute-start(bf16[288,768]{1,0:T(8,128)(2,1)} %collective-permute-done.27.refs_3_), channel_id=1, source_target_pairs={{0,48},{48,0},{16,32},{32,16},{1,49},{49,1},{17,33},{33,17},{2,50}... | collective-permute-start | bytes 1327112 | tf_op jit(solution)/shard_map/ppermute | solution.py:661
  329.4 24.1 %all-to-all-start.8 = ((bf16[8,48,1024]{2,1,0:T(8,128)(2,1)}), bf16[8,48,1024]{2,1,0:T(8,128)(2,1)S(1)}, u32[]{:S(2)}, u32[]{:S(2)}) async-start(bf16[8,48,1024]{2,1,0:T(8,128)(2,1)} %shard_map.243), calls=%async_computation.8 | async-start | bytes 1572864 | tf_op jit(solution)/shard_map/all_to_all | solution.py:639
  (59 other events, 448.7 us)

commit v2 on v1

--- a/solution.py
+++ b/solution.py
@@ -43,6 +43,15 @@
 
 def t_dot(a, b):
     return lax.dot_general(a, b, (((0,), (0,)), ((), ())), preferred_element_type=F32)
+
+
+def fan(pieces):
+    return [
+        pieces[0],
+        flip(pieces[1], PAIRS_S),
+        flip(pieces[2], PAIRS_T),
+        flip(pieces[3], PAIRS_ST),
+    ]
 
 
 def add(a, b):
@@ -323,7 +332,7 @@
 
 def back_kernel(
     place, back, hot_t, resid_i, scale_i, gain, cot, weight, probs_i, kv, q, cos, sin,
-    grad_resid_o, attended_o, gain_o, query_o, kv_o, sent_o,
+    grad_resid_o, attended_o, gain_o, query_o, kv_o, *sent_o,
 ):
     kv_width = kv.shape[1] // 2
     resid = resid_i[...]
@@ -369,73 +378,73 @@
         kv_o[:, at] = (grad_keys * HEAD_DIM ** (-0.5)).astype(BF)
         kv_o[:, pl.ds(kv_width + group * HEAD_DIM, HEAD_DIM)] = grad_values.astype(BF)
     kv_o.send()
-    half = resid.shape[1] // 2
-    at = pl.ds(pl.multiple_of((1 - place[0]) * half, half), half)
-    sent_o[0] = attended_o[:, at]
-    sent_o[1] = query_o[:, at]
-
-
-def put_split(s, t, total, keep_a, send_a, keep_b, send_b, which=(0, 1)):
-    groups, _, quarter, _ = keep_a.shape
-    outs = (
-        (send_a, 0, ((1 - s, 0), (1 - s, 1))),
-        (send_b, 1, ((0, 1 - t), (1, 1 - t))),
-        (keep_a, 0, ((s, 0), (s, 1))),
-        (keep_b, 1, ((0, t), (1, t))),
-    )
-    for out, k, spots in outs:
-        if k not in which:
-            continue
+    size = resid.shape[1] // XS
+    for out, part in zip(sent_o, x_parts(place)):
+        at = pl.ds(pl.multiple_of(part * size, size), size)
+        one, two = attended_o[:, at], query_o[:, at]
+        out[:, pl.ds(0, size)] = jnp.where(place[0] == 0, one, two)
+        out[:, pl.ds(size, size)] = jnp.where(place[0] == 0, two, one)
+
+
+def x_parts(place):
+    s, t = place[2], place[3]
+    return [
+        a + 3 * b - 2 * a * b for a, b in ((s, t), (1 - s, t), (s, 1 - t), (1 - s, 1 - t))
+    ]
+
+
+def collect(pieces, whole, sems, first):
+    rows = pieces[0].shape[0]
+    copies = []
+    for n, piece in enumerate(pieces):
+        copy = pltpu.make_async_copy(
+            piece, whole.at[pl.ds(n * rows, rows)], sems.at[first + n]
+        )
+        copy.start()
+        copies.append(copy)
+    return copies
+
+
+def interleave(own, other):
+    return [piece for pair in zip(own, other) for piece in pair]
+
+
+def square_weight_kernel(place, *refs):
+    own, other, left = refs[:4], refs[4:8], refs[8:16]
+    out, all_grads, all_left, sems = refs[16:]
+    size = out.shape[1]
+    copies = collect(
+        interleave(
+            [ref.at[:, pl.ds(0, size)] for ref in own],
+            [ref.at[:, pl.ds(size, size)] for ref in other],
+        ),
+        all_grads, sems, 0,
+    )
+    copies += collect(left, all_left, sems, 8)
+    for copy in copies:
+        copy.wait()
+    step = 256
+    for low in range(0, all_left.shape[1], step):
+        at = pl.ds(low, step)
+        out[at, :] = t_dot(all_left[:, at], all_grads[...]).astype(BF)
+
+
+def pack_kernel(place, square, gains, *refs):
+    grads, left = refs[:8], refs[8:16]
+    out, all_grads, all_left, total, sems = refs[16:]
+    copies = collect(interleave(grads[:4], grads[4:]), all_grads, sems, 0)
+    copies += collect(left, all_left, sems, 8)
+    for copy in copies:
+        copy.wait()
+    total[...] = t_dot(all_left[...], all_grads[...]).astype(BF)
+    size, small = square.shape[1], total.shape[1]
+    count, groups, part, _ = out.shape
+    even = place[0] == 0
+    for y in range(count):
         for f in range(groups):
-            for j, (row_s, row_t) in enumerate(spots):
-                start = (f * XS + 2 * row_s + row_t) * quarter
-                out[f, j] = total[k, pl.ds(pl.multiple_of(start, quarter), quarter), :]
-        out.send()
-
-
-def square_weight_kernel(
-    place, mixed, mixed_got, attended, normed, normed_got, query, got,
-    keep_a, send_a, keep_b, send_b, total,
-):
-    half = mixed.shape[1] // 2
-    at = pl.ds(pl.multiple_of(place[0] * half, half), half)
-    step = 256
-    for k, (left, left_got, right) in enumerate(
-        ((mixed, mixed_got, attended), (normed, normed_got, query))
-    ):
-        part = right[:, at]
-        for low in range(0, 2 * half, step):
-            cols = pl.ds(low, step)
-            total[k, cols, :] = (
-                t_dot(left[:, cols], part) + t_dot(left_got[:, cols], got[k])
-            ).astype(BF)
-        put_split(place[2], place[3], total, keep_a, send_a, keep_b, send_b, (k,))
-
-
-def step_kernel(
-    place, qk_a, qg_a, kk_a, kg_a, qk_b, qg_b, kk_b, kg_b, keep_a, send_a, keep_b, send_b
-):
-    s, t = place[2], place[3]
-    size = qk_a.shape[-1]
-    extra = kk_a.shape[-1]
-    groups = qk_a.shape[0]
-    for out, which, big, big_got, small, small_got in (
-        (send_a, 1 - t, qk_a, qg_a, kk_a, kg_a),
-        (send_b, 1 - s, qk_b, qg_b, kk_b, kg_b),
-        (keep_a, t, qk_a, qg_a, kk_a, kg_a),
-        (keep_b, s, qk_b, qg_b, kk_b, kg_b),
-    ):
-        for f in range(groups):
-            out[f, :, pl.ds(0, size)] = add(big[f, which], big_got[f, which])
-            out[f, :, pl.ds(size, extra)] = add(small[f, which], small_got[f, which])
-        out.send()
-
-
-def pack_kernel(place, keep_a, got_a, keep_b, got_b, gains, out):
-    size = keep_a.shape[-1]
-    for y, (keep, got) in enumerate(((keep_a, got_a), (keep_b, got_b))):
-        out[y, :, :, pl.ds(0, size)] = add(keep[...], got[...])
-        out[y, :, :, pl.ds(size, gains.shape[-1])] = gains[...]
+            at = pl.ds((f * count + y) * part, part)
+            out[y, f, :, pl.ds(0, size)] = square[at, :]
+            out[y, f, :, pl.ds(size, small)] = jnp.where(even, gains[f], total[at, :])
         out.send(y + 1)
 
 
@@ -449,35 +458,28 @@
 
 
 def final_kernel(place, own, other, mark, output_o, query_o, key_o, value_o, gains_o):
-    core = place[0]
-    quarter = own.shape[1]
-    half = output_o.shape[1] // 2
-    part = key_o.shape[1] // 2
-    size = half + part
-    for refs, which in ((own, core), (other, 1 - core)):
-        at = pl.ds(pl.multiple_of(which * half, half), half)
-        for piece, x in enumerate(PLACE):
-            rows = pl.ds(piece * quarter, quarter)
-            output_o[rows, at] = refs[x, :, pl.ds(0, half)].astype(F32)
-            query_o[rows, at] = refs[XS + x, :, pl.ds(0, half)].astype(F32)
-    send(output_o, query_o)
-    for piece, x in enumerate(PLACE):
-        rows = pl.ds(piece * quarter, quarter)
-        for y in range(2):
-            at = pl.ds(y * part, part)
-            mine = own[y * XS + x, :, pl.ds(half, part)].astype(F32)
-            others = other[y * XS + x, :, pl.ds(half, part)].astype(F32)
-            even = core == 0
-            key_o[rows, at] = jnp.where(even, mine, others)
-            value_o[rows, at] = jnp.where(even, others, mine)
+    even = place[0] == 0
+    part = own.shape[1]
+    size = output_o.shape[1] // XS
+    small = key_o.shape[1] * 2 // XS
     total = jnp.zeros(gains_o.shape, F32)
-    for refs in (own, other):
+    for y in range(YLO):
+        rows = pl.ds(y * part, part)
         for x in range(XS):
-            total = total + refs[x, :, pl.ds(size, gains_o.shape[1])].astype(F32)
+            mine, theirs = own[y * XS + x], other[y * XS + x]
+            first = jnp.where(even, mine, theirs).astype(F32)
+            second = jnp.where(even, theirs, mine).astype(F32)
+            at = pl.ds(x * size, size)
+            output_o[rows, at] = first[:, :size]
+            query_o[rows, at] = second[:, :size]
+            into = key_o if x < XS // 2 else value_o
+            into[rows, pl.ds(x % (XS // 2) * small, small)] = second[:, size:]
+            if y == 0:
+                total = total + first[:, size:]
     gains_o[...] = total
 
 
-def key_back_kernel(place, parts, cos, sin, pre_o, sent_o):
+def key_back_kernel(place, parts, cos, sin, pre_o, *sent_o):
     kv_width = parts.shape[-1] // 2
     total = parts[0].astype(F32)
     for k in range(1, parts.shape[0]):
@@ -488,18 +490,9 @@
         if head < KV_HEADS:
             piece = turn_back(piece, cos[...], sin[...])
         pre_o[:, low:high] = piece.astype(BF)
-    sent_o[...] = pre_o[:, pl.ds(pl.multiple_of((1 - place[0]) * kv_width, kv_width), kv_width)]
-
-
-def key_weight_kernel(
-    place, normed, normed_got, pre, pre_got, keep_a, send_a, keep_b, send_b, total
-):
-    kv_width = pre_got.shape[1]
-    part = pre[:, pl.ds(pl.multiple_of(place[0] * kv_width, kv_width), kv_width)]
-    grad = (t_dot(normed[...], part) + t_dot(normed_got[...], pre_got[...])).astype(BF)
-    total[0] = grad[:, : kv_width // 2]
-    total[1] = grad[:, kv_width // 2 :]
-    put_split(place[2], place[3], total, keep_a, send_a, keep_b, send_b)
+    size = 2 * kv_width // XS
+    for out, part in zip(sent_o, x_parts(place)):
+        out[...] = pre_o[:, pl.ds(pl.multiple_of(part * size, size), size)]
 
 
 def input_kernel(
@@ -649,7 +642,7 @@
 
 PAIRS_S = [(0, 1), (1, 0), (2, 3), (3, 2)]
 PAIRS_T = [(0, 3), (3, 0), (1, 2), (2, 1)]
-PLACE = (0, 3, 1, 2)
+PAIRS_ST = [(0, 2), (2, 0), (1, 3), (3, 1)]
 
 
 def x_bits():
@@ -710,8 +703,11 @@
         ],
         axis=1,
     )
-    weights = jnp.concatenate([kv_piece, gains, square_piece], axis=0)
-    gathered = exchange(copies(weights, groups), "fsdp")
+    kv_piece = jnp.concatenate([kv_piece, gains], axis=0)
+    gathered = exchange(copies(kv_piece, groups), "fsdp")
+    square_piece = copies(square_piece, groups)
+    gathered, square_piece, place_at = tie(gathered, square_piece, place_at)
+    squares = exchange(square_piece, "fsdp")
 
     ids = expert_ids[0].reshape(-1)
     order = priority[0, 0]
@@ -751,9 +747,7 @@
     )
     bias = jnp.where(allowed, 0.0, NEGATIVE).astype(F32)
     bias = jnp.concatenate([bias, bias], axis=1)
-    gathered, cosine, sine, place_at, one_hot_t, gate_high, gate_low, send_grad, bias = tie(
-        gathered, cosine, sine, place_at, one_hot_t, gate_high, gate_low, send_grad, bias
-    )
+    gathered, cosine, sine = tie(gathered, cosine, sine)
     kv_raw = gathered[:, :kv_rows]
     gain_one = gathered[:, kv_rows, :rows].reshape(1, width).astype(F32)
     gain_two = gathered[:, kv_rows + 1, :rows].reshape(1, width).astype(F32)
@@ -766,12 +760,14 @@
         [((tok, width), BF), ((tok, HEAD_DIM), F32), ((groups, tok, 2 * kv_width), BF),
          ((width, 2 * kv_width), BF)],
     )
-    q_own, o_own = gathered[:, kv_rows + 8 :, :half], gathered[:, kv_rows + 8 :, half:]
+    kv_send, squares, one_hot_t, gate_high, gate_low, send_grad, bias = tie(
+        kv_send, squares, one_hot_t, gate_high, gate_low, send_grad, bias
+    )
+    q_own, o_own = squares[..., :half], squares[..., half:]
     kv_all = exchange(kv_send, "fsdp").reshape(length, 2 * kv_width)
     q_got, o_got = flip(q_own, PAIRS_S), flip(o_own, PAIRS_T)
     send_grad, kv_all = tie(send_grad, kv_all)
     arrived_grad = exchange(send_grad, "fsdp")
-    normed_other = swap(normed)
     far_pieces = [
         Far(v)
         for v in (q_own, q_got, swap(q_own), swap(q_got), o_own, o_got, swap(o_own), swap(o_got))
@@ -793,12 +789,17 @@
 
     send_rows, arrived_grad = tie(send_rows, arrived_grad)
     arrived = exchange(send_rows, "fsdp")
-    mixed_other = swap(mixed)
+
+    left_a = pick(mixed, normed)
+    left_b = swap(pick(normed, mixed))
+    left_one_a, left_two_a = flip(left_a, PAIRS_S), flip(left_a, PAIRS_T)
+    left_one_b, left_two_b = flip(left_b, PAIRS_T), flip(left_b, PAIRS_S)
     upper_other = swap(lax.dynamic_slice_in_dim(arrived_grad, (1 - core) * half, half, 1))
     grad_hidden = dot_t(arrived_grad, down_weight[0])
-    arrived, grad_hidden, mixed_other, upper_other = tie(
-        arrived, grad_hidden, mixed_other, upper_other
-    )
+    arrived, grad_hidden, upper_other, left_one_a, left_two_a, left_one_b, left_two_b = tie(
+        arrived, grad_hidden, upper_other, left_one_a, left_two_a, left_one_b, left_two_b
+    )
+    left_three_a, left_three_b = flip(left_one_a, PAIRS_T), flip(left_one_b, PAIRS_S)
     arrived_other = swap(arrived)
     hidden, own_pre, sent_pre, grad_rows = call(
         expert_kernel,
@@ -818,15 +819,19 @@
     )
     expert_out = dot(hidden, down_weight[0]).astype(BF)
     e_got_a, e_got_b = flip(e_send_a, PAIRS_S), flip(e_send_b, PAIRS_T)
-    back_rows, expert_out, e_keep_a, e_keep_b = tie(back_rows, expert_out, e_keep_a, e_keep_b)
-
-    grad_residual, grad_attended, gain_two_part, grad_query_pre, kv_back, qo_sent = call(
+    back_rows, expert_out, e_keep_a, e_keep_b, left_three_a, left_three_b = tie(
+        back_rows, expert_out, e_keep_a, e_keep_b, left_three_a, left_three_b
+    )
+    left = [left_a, left_b, left_one_a, left_two_b, left_two_a, left_one_b, left_three_a,
+            left_three_b]
+
+    grad_residual, grad_attended, gain_two_part, grad_query_pre, kv_back, *qo_sent = call(
         back_kernel,
         [place_at, Far(back_rows), Far(one_hot_t), Far(residual), Far(scale_two), gain_two,
          Far(cotangent[0]), Far(output_weight), Far(probs), Far(kv_all), Far(query_rot), cosine,
          sine],
         [((tok, width), F32), ((tok, width), BF), ((1, width), F32), ((tok, width), BF),
-         ((length, 2 * kv_width), BF), ((2, tok, half), BF)],
+         ((length, 2 * kv_width), BF)] + [((tok, half), BF)] * XS,
     )
     kv_got = exchange(kv_back, "fsdp")
     e_keep_a, e_send_a, e_keep_b, e_send_b = call(
@@ -834,33 +839,26 @@
         [place_at, Far(e_keep_a), Far(e_got_a), Far(e_keep_b), Far(e_got_b)],
         [(e_part[1:], BF)] * 4,
     )
-    qo_got, e_send_a, e_send_b = tie(swap(qo_sent), e_send_a, e_send_b)
     e_got_a, e_got_b = flip(e_send_a, PAIRS_T), flip(e_send_b, PAIRS_S)
-
-    big_part, small_part = (groups, 2, quarter, half), (groups, 2, quarter, kv_width // 2)
-    qo_keep_a, qo_send_a, qo_keep_b, qo_send_b = call(
+    qo_set = fan(qo_sent)
+    whole = 2 * XS * tok
+    square_grad = call(
         square_weight_kernel,
-        [place_at] + [Far(v) for v in (mixed, mixed_other, grad_attended, normed, normed_other,
-                                       grad_query_pre, qo_got)],
-        [(big_part, BF)] * 4,
-        [pltpu.VMEM((2, width, half), BF)],
-    )
-    kv_got, expert_out = tie(kv_got, expert_out)
-    qo_got_a, qo_got_b = flip(qo_send_a, PAIRS_S), flip(qo_send_b, PAIRS_T)
-    returned = exchange(expert_out, "fsdp")
-    grad_kv_pre, kv_pre_sent = call(
+        [place_at] + [Far(v) for v in (*qo_set, *[swap(v) for v in qo_set], *left)],
+        [((width, width // XS), BF)],
+        [pltpu.VMEM((whole, width // XS), BF), pltpu.VMEM((whole, width), BF),
+         pltpu.SemaphoreType.DMA((16,))],
+        raw=range(1, 17),
+    )[0]
+    kv_got, square_grad = tie(kv_got, square_grad)
+    grad_kv_pre, *kv_sent = call(
         key_back_kernel,
         [place_at, Far(kv_got.reshape(groups, tok, 2 * kv_width)), cosine, sine],
-        [((tok, 2 * kv_width), BF), ((tok, kv_width), BF)],
-        micros=30,
-    )
-    kv_keep_a, kv_send_a, kv_keep_b, kv_send_b = call(
-        key_weight_kernel,
-        [place_at, Far(normed), Far(normed_other), Far(grad_kv_pre), Far(swap(kv_pre_sent))],
-        [(small_part, BF)] * 4,
-        [pltpu.VMEM((2, width, kv_width // 2), BF)],
-    )
-    kv_got_a, kv_got_b = flip(kv_send_a, PAIRS_S), flip(kv_send_b, PAIRS_T)
+        [((tok, 2 * kv_width), BF)] + [((tok, 2 * kv_width // XS), BF)] * XS,
+    )
+    kv_sent[0], expert_out = tie(kv_sent[0], expert_out)
+    returned = exchange(expert_out, "fsdp")
+    kv_set = fan(kv_sent)
     e_sum = call(
         expert_end_kernel,
         [place_at, Far(e_keep_a), Far(e_got_a), Far(e_keep_b), Far(e_got_b)],
@@ -874,35 +872,33 @@
         [((tok, width), BF), ((1, width), F32)],
     )
 
-    e_other_y, gain_one_part = tie(e_other_y, gain_one_part)
     e_zero_a, e_zero_b = call(pair_kernel, [place_at, Far(e_sum), Far(e_other_y)], [(e_part[1:], BF)] * 2)
     e_one_a, e_one_b = flip(e_zero_a, PAIRS_T), flip(e_zero_b, PAIRS_S)
     e_two_a, e_two_b = flip(e_zero_a, PAIRS_S), flip(e_zero_b, PAIRS_T)
 
-    both_part = (groups, quarter, half + kv_width // 2)
-    keep_a, send_a, keep_b, send_b = call(
-        step_kernel,
-        [place_at] + [Far(v) for v in (qo_keep_a, qo_got_a, kv_keep_a, kv_got_a, qo_keep_b,
-                                       qo_got_b, kv_keep_b, kv_got_b)],
-        [(both_part, BF)] * 4,
-    )
-    got_a, got_b = flip(send_a, PAIRS_T), flip(send_b, PAIRS_S)
-    spare = HEAD_DIM
-    gain_parts = jnp.stack([gain_one_part, gain_two_part]).reshape(2, groups, quarter, XS)
-    gain_parts = gain_parts.transpose(1, 2, 0, 3).reshape(groups, quarter, 2 * XS).astype(BF)
-    gain_parts = jnp.pad(gain_parts, ((0, 0), (0, 0), (0, spare - 2 * XS)))
-    packed_width = both_part[-1] + spare
+    spare = 2 * kv_width // XS
+    part = rows // YLO
+    gain_parts = jnp.concatenate([gain_one_part, gain_two_part])
+    gain_parts = gain_parts + swap(gain_parts)
+    gain_parts = gain_parts.reshape(2, groups, part, YLO).transpose(1, 2, 0, 3)
+    gain_parts = gain_parts.reshape(groups, part, 2 * YLO).astype(BF)
+    gain_parts = jnp.pad(gain_parts, ((0, 0), (0, 0), (0, spare - 2 * YLO)))
+    packed_width = width // XS + spare
     packed = call(
         pack_kernel,
-        [place_at, Far(keep_a), Far(got_a), Far(keep_b), Far(got_b), gain_parts],
-        [Far((YLO, groups, quarter, packed_width), BF, 2)],
+        [place_at, Far(square_grad), gain_parts]
+        + [Far(v) for v in (*kv_set, *[swap(v) for v in kv_set], *left)],
+        [Far((YLO, groups, part, packed_width), BF, 2)],
+        [pltpu.VMEM((whole, spare), BF), pltpu.VMEM((whole, width), BF),
+         pltpu.VMEM((width, spare), BF), pltpu.SemaphoreType.DMA((16,))],
+        raw=range(3, 19),
     )[0]
     packed, returned = tie(packed, returned)
-    packed = exchange(packed.reshape(YLO * groups, quarter, packed_width), ("ylo", "fsdp"))
+    packed = exchange(packed.reshape(YLO * groups, part, packed_width), ("ylo", "fsdp"))
     mixture = t_dot(gate_high, returned) + t_dot(gate_low, returned)
     outputs = (residual + mixture).astype(BF)
     packed, outputs = tie(packed, outputs)
-    packed = call(sum_kernel, [place_at, Far(packed)], [((YLO * XS, quarter, packed_width), BF)])[0]
+    packed = call(sum_kernel, [place_at, Far(packed)], [((YLO * XS, part, packed_width), BF)])[0]
     spreaded = exchange(packed, ("ylo", "x"))
     most = [e_zero_a, e_zero_b, e_one_a, e_one_b, e_two_a, e_two_b]
     *e_grads, most_mark = expert_outputs(
@@ -925,9 +921,9 @@
         final_kernel,
         [place_at, Far(spreaded), Far(swap(spreaded)), e_mark],
         [((rows, width), F32), ((rows, width), F32), ((rows, kv_width), F32),
-         ((rows, kv_width), F32), ((quarter, spare), F32)],
-    )
-    gains_sum = gains_sum[:, : 2 * XS].reshape(quarter, 2, XS).transpose(1, 0, 2)
+         ((rows, kv_width), F32), ((part, spare), F32)],
+    )
+    gains_sum = gains_sum[:, : 2 * YLO].reshape(part, 2, YLO).transpose(1, 0, 2)
     gains_sum = gains_sum.reshape(2, rows)
     return (
         outputs[None],

time: 370 us -> 361 us (0.976)
  waiting for transfers between devices: 102 us -> 70.5 us
  starting transfers between devices: 97.5 us -> 120 us
  Pallas kernels: 111 us -> 103 us
  local copies, waits for them, and re-layouts: 29.6 us -> 35.7 us
    all_to_all x9 -> x10, waiting for transfers between devices: 65.9 us -> 36.7 us  [exchange(): return lax.all_to_all(v, axis, 0, 0, tiled=True)]
    ppermute x18 -> x24, starting transfers between devices: 18.9 us -> 26.9 us  [flip(): return lax.ppermute(v, 'x', pairs)]
    pallas_call x16 -> x14, Pallas kernels: 99.7 us -> 92 us  [call(): pl.pallas_call(whole, out_shape=[jax.ShapeDtypeStruct(out.value, out.kind...]
    ppermute x22 -> x28, starting transfers between devices: 29 us -> 36.5 us  [swap(): return lax.ppermute(v, 'core', [(0, 1), (1, 0)])]
    all_to_all x9 -> x10, starting transfers between devices: 49.2 us -> 55.8 us  [exchange(): return lax.all_to_all(v, axis, 0, 0, tiled=True)]
    ppermute x22 -> x28, waiting for transfers between devices: 11.2 us -> 7.26 us  [swap(): return lax.ppermute(v, 'core', [(0, 1), (1, 0)])]
    ppermute x18 -> x24, waiting for transfers between devices: 23.1 us -> 26.6 us  [flip(): return lax.ppermute(v, 'x', pairs)]
    unnamed x88 -> x132, local copies, waits for them, and re-layouts: 11.5 us -> 13.9 us
  transfers between devices with their start and end apart: 50 -> 63, of which waited for: 20 -> 23; matrix products, arithmetic and copies ran while one was open for 8% -> 11% of each run, Pallas kernels for 28% -> 25%
where the time goes in v2:
time: 361 us; the launch traced here: 355 us
  starting transfers between devices  120 us (33%)
  Pallas kernels  103 us (29%)
  waiting for transfers between devices  70.5 us (20%)
  local copies, waits for them, and re-layouts  35.7 us (10%)
  matrix products  12.5 us (3%)
  other arithmetic  10.8 us (3%)
    pallas_call x14, Pallas kernels, call(): pl.pallas_call(whole, out_shape=[jax.ShapeDtypeStruct(out.value, out.kind...  92 us
    all_to_all x10, starting transfers between devices, exchange(): return lax.all_to_all(v, axis, 0, 0, tiled=True)  55.8 us
    all_to_all x10, waiting for transfers between devices, exchange(): return lax.all_to_all(v, axis, 0, 0, tiled=True)  36.7 us
    ppermute x28, starting transfers between devices, swap(): return lax.ppermute(v, 'core', [(0, 1), (1, 0)])  36.5 us
    ppermute x24, starting transfers between devices, flip(): return lax.ppermute(v, 'x', pairs)  26.9 us
    ppermute x24, waiting for transfers between devices, flip(): return lax.ppermute(v, 'x', pairs)  26.6 us
    unnamed x132, local copies, waits for them, and re-layouts  13.9 us
    pallas_call x2, Pallas kernels, expert_outputs(): pl.pallas_call(kernel, out_shape=shapes, in_specs=[pl.BlockSpec(memory_sp...  11.4 us
  transfers between devices with their start and end apart: 63, of which 23 were waited for; matrix products, arithmetic and copies ran while one was open for 11% of the time, Pallas kernels for 25%

profile of v2, /device:TPU:1, one launch (start us, length us, event | category | flops | bytes accessed | tf_op | source)
XLA Modules:
  0.0 354.5 jit_solution(18382356439005073031)
XLA Ops:
  4.2 8.5 %all-to-all-start = ((bf16[8,40,1536]{2,1,0:T(8,128)(2,1)}), bf16[8,40,1536]{2,1,0:T(8,128)(2,1)S(1)}, u32[]{:S(2)}, u32[]{:S(2)}) async-start(bf16[8,40,1536]{2,1,0:T(8,128)(2,1)} %broadcast_in_dim.91), calls=%async_computation | async-start | bytes 1966080 | tf_op jit(solution)/shard_map/all_to_all | solution.py:632
  18.0 10.0 %all-to-all-done = bf16[8,40,1536]{2,1,0:T(8,128)(2,1)S(1)} async-done(((bf16[8,40,1536]{2,1,0:T(8,128)(2,1)}), bf16[8,40,1536]{2,1,0:T(8,128)(2,1)S(1)}, u32[]{:S(2)}, u32[]{:S(2)}) %all-to-all-start) | async-done | bytes 983072 | tf_op jit(solution)/shard_map/all_to_all | solution.py:632
  28.0 4.4 %all-to-all-start.1 = ((bf16[8,96,1536]{2,1,0:T(8,128)(2,1)}), bf16[8,96,1536]{2,1,0:T(8,128)(2,1)}, u32[]{:S(2)}, u32[]{:S(2)}) async-start(bf16[8,96,1536]{2,1,0:T(8,128)(2,1)} %broadcast_in_dim.92), calls=%async_computation.1 | async-start | bytes 4718592 | tf_op jit(solution)/shard_map/all_to_all | solution.py:632
  49.6 4.0 %shard_map.230 = (bf16[128,1536]{1,0:T(8,128)(2,1)}, f32[128,128]{1,0:T(8,128)}, bf16[8,128,512]{2,1,0:T(8,128)(2,1)}, bf16[1536,512]{1,0:T(8,128)(2,1)}) custom-call(s32[4]{0:T(128)} %pad_add_fusion.refs_0_.place, bf16[128,1536]{1,0:T(8,128)(2,1)} %bitcast.90, f32[1,1536]{1,0:T(1,128)} %reshape.236.refs_2_.refs_5_, bf16[8,32,1536]{2,1,0:T(8,128)(2,1)} %slice.60.refs_3_, ...), custom_call_target="tpu_custom_call" | custom-call | tf_op jit(solution)/shard_map/pallas_call | solution.py:605
  53.6 7.8 %all-to-all-done.1 = bf16[8,96,1536]{2,1,0:T(8,128)(2,1)} async-done(((bf16[8,96,1536]{2,1,0:T(8,128)(2,1)}), bf16[8,96,1536]{2,1,0:T(8,128)(2,1)}, u32[]{:S(2)}, u32[]{:S(2)}) %all-to-all-start.1) | async-done | bytes 2359328 | tf_op jit(solution)/shard_map/all_to_all | solution.py:632
  61.5 5.0 %all-to-all-start.2 = ((bf16[8,128,512]{2,1,0:T(8,128)(2,1)}), bf16[8,128,512]{2,1,0:T(8,128)(2,1)S(1)}, u32[]{:S(2)}, u32[]{:S(2)}) async-start(bf16[8,128,512]{2,1,0:T(8,128)(2,1)} %get-tuple-element.120), calls=%async_computation.2 | async-start | bytes 2097152 | tf_op jit(solution)/shard_map/all_to_all | solution.py:632
  72.2 9.7 %all-to-all-done.2 = bf16[8,128,512]{2,1,0:T(8,128)(2,1)S(1)} async-done(((bf16[8,128,512]{2,1,0:T(8,128)(2,1)}), bf16[8,128,512]{2,1,0:T(8,128)(2,1)S(1)}, u32[]{:S(2)}, u32[]{:S(2)}) %all-to-all-start.2) | async-done | bytes 1048608 | tf_op jit(solution)/shard_map/all_to_all | solution.py:632
  82.8 4.3 %all-to-all-start.3 = ((bf16[8,80,1536]{2,1,0:T(8,128)(2,1)}), bf16[8,80,1536]{2,1,0:T(8,128)(2,1)}, u32[]{:S(2)}, u32[]{:S(2)}) async-start(bf16[8,80,1536]{2,1,0:T(8,128)(2,1)} %bitcast.83), calls=%async_computation.3 | async-start | bytes 3932160 | tf_op jit(solution)/shard_map/all_to_all | solution.py:632
  90.2 6.8 %collective-permute-done.4.refs_14_ = bf16[8,96,768]{2,1,0:T(8,128)(2,1)} collective-permute-done((bf16[8,96,768]{2,1,0:T(8,128)(2,1)}, bf16[8,96,768]{2,1,0:T(8,128)(2,1)}, u32[]{:S(2)}, u32[]{:S(2)}) %collective-permute-start.4) | collective-permute-done | bytes 1179680 | tf_op jit(solution)/shard_map/ppermute | solution.py:654
  104.1 12.7 %shard_map.231 = (bf16[8,192,1536]{2,1,0:T(8,128)(2,1)}, bf16[8,192,1536]{2,1,0:T(8,128)(2,1)}, bf16[128,1536]{1,0:T(8,128)(2,1)}, bf16[128,1536]{1,0:T(8,128)(2...) custom-call(s32[4]{0:T(128)} %pad_add_fusion.refs_0_.place, ...), custom_call_target="tpu_custom_call" | custom-call | tf_op jit(solution)/shard_map/pallas_call | solution.py:605
  116.8 6.7 %all-to-all-start.4 = ((bf16[8,80,1536]{2,1,0:T(8,128)(2,1)}), bf16[8,80,1536]{2,1,0:T(8,128)(2,1)}, u32[]{:S(2)}, u32[]{:S(2)}) async-start(bf16[8,80,1536]{2,1,0:T(8,128)(2,1)} %bitcast.96), calls=%async_computation.4 | async-start | bytes 3932160 | tf_op jit(solution)/shard_map/all_to_all | solution.py:632
  130.8 4.6 %fusion.3.refs_2_ = f32[640,768]{1,0:T(8,128)} fusion(bf16[640,1536]{1,0:T(8,128)(2,1)} %bitcast.19.refs_7_, bf16[1,768,1536]{2,1,0:T(8,128)(2,1)S(1)} %copy-done), kind=kOutput, calls=%fused_computation.6 | convolution fusion | flops 1509949440 | bytes 6291456 | tf_op jit(solution)/shard_map/dot_general | solution.py:41
  138.4 8.3 %collective-permute-done.12.refs_12_.refs_14_ = bf16[128,1536]{1,0:T(8,128)(2,1)S(1)} collective-permute-done((bf16[128,1536]{1,0:T(8,128)(2,1)S(1)}, bf16[128,1536]{1,0:T(8,128)(2,1)S(1)}, u32[]{:S(2)}, u32[]{:S(2)}) %collective-permute-start.12) | collective-permute-done | bytes 393248 | tf_op jit(solution)/shard_map/ppermute | solution.py:654
  151.8 11.6 %shard_map.232 = (bf16[640,768]{1,0:T(8,128)(2,1)}, bf16[640,768]{1,0:T(8,128)(2,1)}, bf16[640,768]{1,0:T(8,128)(2,1)}, bf16[640,1536]{1,0:T(8,128)(2,1)}) custom-call(s32[4]{0:T(128)} %pad_add_fusion.refs_0_.place, bf16[640,1536]{1,0:T(8,128)(2,1)} %bitcast.21.refs_1_, f32[640,768]{1,0:T(8,128)} %fusion.3.refs_2_, bf16[1536,768]{1,0:T(8,128)(2,1)} %bitcast.93, ...), custom_call_target="tpu_custom_call" | custom-call | tf_op jit(solution)/shard_map/pallas_call | solution.py:605
  163.5 5.2 %all-to-all-start.5 = ((bf16[8,80,1536]{2,1,0:T(8,128)(2,1)}), bf16[8,80,1536]{2,1,0:T(8,128)(2,1)}, u32[]{:S(2)}, u32[]{:S(2)}) async-start(bf16[8,80,1536]{2,1,0:T(8,128)(2,1)} %bitcast.97), calls=%async_computation.5 | async-start | bytes 3932160 | tf_op jit(solution)/shard_map/all_to_all | solution.py:632
  171.4 4.2 %convolution_convert_fusion = bf16[640,1536]{1,0:T(8,128)(2,1)} fusion(bf16[640,768]{1,0:T(8,128)(2,1)} %get-tuple-element.133.refs_5_, bf16[1,768,1536]{2,1,0:T(8,128)(2,1)S(1)} %copy-done), kind=kOutput, calls=%fused_computation.1 | convolution fusion | flops 1510932480 | bytes 5308416 | tf_op jit(solution)/shard_map/dot_general | solution.py:37
  177.0 12.8 %shard_map.233 = (bf16[2,288,768]{2,1,0:T(8,128)(2,1)}, bf16[2,288,768]{2,1,0:T(8,128)(2,1)}, bf16[2,288,768]{2,1,0:T(8,128)(2,1)}, bf16[2,288,768]{2,1,0:T(8,128)(2,1)}) custom-call(s32[4]{0:T(128)} %pad_add_fusion.refs_0_.place, bf16[640,1536]{1,0:T(8,128)(2,1)} %bitcast.21.refs_1_, bf16[640,1536]{1,0:T(8,128)(2,1)} %collective-permute-done.13.refs_2_, ...), custom_call_target="tpu_custom_call" | custom-call | tf_op jit(solution)/shard_map/pallas_call | solution.py:605
  189.8 5.8 %all-to-all-done.5 = bf16[8,80,1536]{2,1,0:T(8,128)(2,1)} async-done(((bf16[8,80,1536]{2,1,0:T(8,128)(2,1)}), bf16[8,80,1536]{2,1,0:T(8,128)(2,1)}, u32[]{:S(2)}, u32[]{:S(2)}) %all-to-all-start.5) | async-done | bytes 1966112 | tf_op jit(solution)/shard_map/all_to_all | solution.py:632
  195.6 12.4 %shard_map.234 = (f32[128,1536]{1,0:T(8,128)}, bf16[128,1536]{1,0:T(8,128)(2,1)}, f32[1,1536]{1,0:T(1,128)}, bf16[128,1536]{1,0:T(8,128)(2,1)}, bf16[1024,512]{1...) custom-call(s32[4]{0:T(128)} %pad_add_fusion.refs_0_.place, ...), custom_call_target="tpu_custom_call" | custom-call | tf_op jit(solution)/shard_map/pallas_call | solution.py:605
  208.1 3.7 %all-to-all-start.6 = ((bf16[8,128,512]{2,1,0:T(8,128)(2,1)}), bf16[8,128,512]{2,1,0:T(8,128)(2,1)S(1)}, u32[]{:S(2)}, u32[]{:S(2)}) async-start(bf16[8,128,512]{2,1,0:T(8,128)(2,1)} %bitcast.101), calls=%async_computation.6 | async-start | bytes 2097152 | tf_op jit(solution)/shard_map/all_to_all | solution.py:632
  229.1 5.9 %shard_map.235.refs_1_ = bf16[1536,384]{1,0:T(8,128)(2,1)} custom-call(s32[4]{0:T(128)} %pad_add_fusion.refs_0_.place, bf16[128,768]{1,0:T(8,128)(2,1)} %get-tuple-element.148.refs_1_, bf16[128,768]{1,0:T(8,128)(2,1)} %copy-done.37, bf16[128,768]{1,0:T(8,128)(2,1)} %copy-done.38, bf16[128,768]{1,0:T(8,128)(2,1)} %copy-done.39, bf16[128,768]{1,0:T(8,128)(2,1)} %copy-done.40, ...), custom_call_target="tpu_custom_call" | custom-call | tf_op jit(solution)/shard_map/pallas_call | solution.py:605
  239.0 6.8 %all-to-all-start.7 = ((bf16[8,80,1536]{2,1,0:T(8,128)(2,1)}), bf16[8,80,1536]{2,1,0:T(8,128)(2,1)S(1)}, u32[]{:S(2)}, u32[]{:S(2)}) async-start(bf16[8,80,1536]{2,1,0:T(8,128)(2,1)} %bitcast.95), calls=%async_computation.7 | async-start | bytes 3932160 | tf_op jit(solution)/shard_map/all_to_all | solution.py:632
  246.7 3.9 %shard_map.240 = (bf16[288,768]{1,0:T(8,128)(2,1)}, bf16[288,768]{1,0:T(8,128)(2,1)}, bf16[288,768]{1,0:T(8,128)(2,1)}, bf16[288,768]{1,0:T(8,128)(2,1)}) custom-call(s32[4]{0:T(128)} %pad_add_fusion.refs_0_.place, bf16[2,288,768]{2,1,0:T(8,128)(2,1)} %get-tuple-element.180.refs_1_, bf16[2,288,768]{2,1,0:T(8,128)(2,1)} %copy-done.20, ...), custom_call_target="tpu_custom_call" | custom-call | tf_op jit(solution)/shard_map/pallas_call | solution.py:605
  255.0 7.2 %shard_map.237 = (bf16[128,1536]{1,0:T(8,128)(2,1)}, f32[1,1536]{1,0:T(1,128)}) custom-call(s32[4]{0:T(128)} %pad_add_fusion.refs_0_.place, bf16[128,1536]{1,0:T(8,128)(2,1)} %get-tuple-element.157.refs_1_, bf16[128,512]{1,0:T(8,128)(2,1)} %get-tuple-element.159.refs_2_, bf16[128,1536]{1,0:T(8,128)(2,1)} %bitcast.92, f32[128,128]{1,0:T(8,128)} %get-tuple-element.160.refs_4_, ...), custom_call_target="tpu_custom_call" | custom-call | tf_op jit(solution)/shard_map/pallas_call | solution.py:605
  275.2 5.4 %shard_map.238 = bf16[2,8,96,512]{3,2,1,0:T(8,128)(2,1)} custom-call(s32[4]{0:T(128)} %pad_add_fusion.refs_0_.place, bf16[1536,384]{1,0:T(8,128)(2,1)} %shard_map.235.refs_1_, bf16[8,96,128]{2,1,0:T(8,128)(2,1)} %pad.9.refs_2_, bf16[128,128]{1,0:T(8,128)(2,1)} %get-tuple-element.168.refs_3_, bf16[128,128]{1,0:T(8,128)(2,1)} %copy-done.45, ...), custom_call_target="tpu_custom_call" | custom-call | tf_op jit(solution)/shard_map/pallas_call | solution.py:605
  280.6 7.7 %all-to-all-start.8 = ((bf16[16,96,512]{2,1,0:T(8,128)(2,1)}), bf16[16,96,512]{2,1,0:T(8,128)(2,1)}, u32[]{:S(2)}, u32[]{:S(2)}) async-start(bf16[16,96,512]{2,1,0:T(8,128)(2,1)} %bitcast.84), calls=%async_computation.8 | async-start | bytes 3145728 | tf_op jit(solution)/shard_map/all_to_all | solution.py:632
  297.5 5.9 %collective-permute-done.42.refs_4_ = bf16[288,768]{1,0:T(8,128)(2,1)S(1)} collective-permute-done((bf16[288,768]{1,0:T(8,128)(2,1)}, bf16[288,768]{1,0:T(8,128)(2,1)S(1)}, u32[]{:S(2)}, u32[]{:S(2)}) %collective-permute-start.42) | collective-permute-done | bytes 442400 | tf_op jit(solution)/shard_map/ppermute | solution.py:654
  305.3 3.8 %collective-permute-start.48 = (bf16[288,768]{1,0:T(8,128)(2,1)S(1)}, bf16[288,768]{1,0:T(8,128)(2,1)}, u32[]{:S(2)}, u32[]{:S(2)}) collective-permute-start(bf16[288,768]{1,0:T(8,128)(2,1)S(1)} %collective-permute-done.42.refs_4_), channel_id=1, source_target_pairs={{0,8},{8,0},{1,9},{9,1},{2,10},{10,2},{3,11},{11,3},{4,12},{12,4},... | collective-permute-start | bytes 1327112 | tf_op jit(solution)/shard_map/ppermute | solution.py:624
  325.8 7.3 %shard_map.243 = (f32[1536,768]{1,0:T(8,128)}, f32[1536,768]{1,0:T(8,128)}, f32[768,1536]{1,0:T(8,128)}, f32[8,128]{1,0:T(8,128)}) custom-call(s32[4]{0:T(128)} %pad_add_fusion.refs_0_.place, bf16[288,768]{1,0:T(8,128)(2,1)} %get-tuple-element.188.refs_0_, bf16[288,768]{1,0:T(8,128)(2,1)} %get-tuple-element.189.refs_1_, ...), custom_call_target="tpu_custom_call" | custom-call | tf_op jit(solution)/shard_map/pallas_call | solution.py:316
  333.9 4.0 %collective-permute-start.50 = (bf16[288,768]{1,0:T(8,128)(2,1)S(1)}, bf16[288,768]{1,0:T(8,128)(2,1)S(1)}, u32[]{:S(2)}, u32[]{:S(2)}) collective-permute-start(bf16[288,768]{1,0:T(8,128)(2,1)S(1)} %collective-permute-done.40.refs_0_), channel_id=1, source_target_pairs={{0,8},{8,0},{1,9},{9,1},{2,10},{10,2},{3,11},{11,3},{4,12},{12,4},... | collective-permute-start | bytes 1327112 | tf_op jit(solution)/shard_map/ppermute | solution.py:624
  340.7 4.1 %shard_map.244 = (f32[1536,768]{1,0:T(8,128)}, f32[1536,768]{1,0:T(8,128)}, f32[768,1536]{1,0:T(8,128)}, f32[8,128]{1,0:T(8,128)}) custom-call(s32[4]{0:T(128)} %pad_add_fusion.refs_0_.place, bf16[288,768]{1,0:T(8,128)(2,1)} %copy-done.26, bf16[288,768]{1,0:T(8,128)(2,1)} %copy-done.27, ...), custom_call_target="tpu_custom_call", output_to_operand_aliasing={{0}: (7, {}), {1}: (8, {}), {2}: (9, {})} | custom-call | tf_op jit(solution)/shard_map/pallas_call | solution.py:316
  348.0 3.7 %shard_map.245 = (f32[192,1536]{1,0:T(8,128)}, f32[192,1536]{1,0:T(8,128)}, f32[192,256]{1,0:T(8,128)}, f32[192,256]{1,0:T(8,128)}, f32[96,128]{1,0:T(8,128)}) custom-call(s32[4]{0:T(128)} %pad_add_fusion.refs_0_.place, bf16[8,96,512]{2,1,0:T(8,128)(2,1)} %copy-done.5, bf16[8,96,512]{2,1,0:T(8,128)(2,1)} %copy-done.21, f32[8,128]{1,0:T(8,128)} %get-tuple-element.202.refs_3_), custom_call_target="tpu_custom_call" | custom-call | tf_op jit(solution)/shard_map/pallas_call | solution.py:605
  (308 shorter events, 138.5 us)
Async XLA Ops:
  4.2 23.8 %all-to-all-start = ((bf16[8,40,1536]{2,1,0:T(8,128)(2,1)}), bf16[8,40,1536]{2,1,0:T(8,128)(2,1)S(1)}, u32[]{:S(2)}, u32[]{:S(2)}) async-start(bf16[8,40,1536]{2,1,0:T(8,128)(2,1)} %broadcast_in_dim.91), calls=%async_computation | async-start | bytes 1966080 | tf_op jit(solution)/shard_map/all_to_all | solution.py:632
  28.0 33.5 %all-to-all-start.1 = ((bf16[8,96,1536]{2,1,0:T(8,128)(2,1)}), bf16[8,96,1536]{2,1,0:T(8,128)(2,1)}, u32[]{:S(2)}, u32[]{:S(2)}) async-start(bf16[8,96,1536]{2,1,0:T(8,128)(2,1)} %broadcast_in_dim.92), calls=%async_computation.1 | async-start | bytes 4718592 | tf_op jit(solution)/shard_map/all_to_all | solution.py:632
  36.1 13.5 %collective-permute-start = (bf16[8,32,1536]{2,1,0:T(8,128)(2,1)}, bf16[8,32,1536]{2,1,0:T(8,128)(2,1)}, u32[]{:S(2)}, u32[]{:S(2)}) collective-permute-start(bf16[8,32,1536]{2,1,0:T(8,128)(2,1)} %slice.60.refs_3_), channel_id=1, source_target_pairs={{0,8},{8,0},{1,9},{9,1},{2,10},{10,2},{3,11},{11,3},{4,12},{12,4},... | collective-permute-start | bytes 2359304 | tf_op jit(solution)/shard_map/ppermute | solution.py:624
  61.5 20.3 %all-to-all-start.2 = ((bf16[8,128,512]{2,1,0:T(8,128)(2,1)}), bf16[8,128,512]{2,1,0:T(8,128)(2,1)S(1)}, u32[]{:S(2)}, u32[]{:S(2)}) async-start(bf16[8,128,512]{2,1,0:T(8,128)(2,1)} %get-tuple-element.120), calls=%async_computation.2 | async-start | bytes 2097152 | tf_op jit(solution)/shard_map/all_to_all | solution.py:632
  69.7 27.3 %collective-permute-start.4 = (bf16[8,96,768]{2,1,0:T(8,128)(2,1)}, bf16[8,96,768]{2,1,0:T(8,128)(2,1)}, u32[]{:S(2)}, u32[]{:S(2)}) collective-permute-start(bf16[8,96,768]{2,1,0:T(8,128)(2,1)} %get-tuple-element.213.refs_13_), channel_id=1, source_target_pairs={{0,48},{48,0},{16,32},{32,16},{1,49},{49,1},{17,33},{33,17},{2,50}... | collective-permute-start | bytes 3538952 | tf_op jit(solution)/shard_map/ppermute | solution.py:654
  72.2 27.4 %collective-permute-start.1 = (bf16[8,96,768]{2,1,0:T(8,128)(2,1)}, bf16[8,96,768]{2,1,0:T(8,128)(2,1)}, u32[]{:S(2)}, u32[]{:S(2)}) collective-permute-start(bf16[8,96,768]{2,1,0:T(8,128)(2,1)} %get-tuple-element.214.refs_9_), channel_id=1, source_target_pairs={{0,16},{16,0},{32,48},{48,32},{1,17},{17,1},{33,49},{49,33},{2,18}... | collective-permute-start | bytes 3538952 | tf_op jit(solution)/shard_map/ppermute | solution.py:654
  82.8 34.0 %all-to-all-start.3 = ((bf16[8,80,1536]{2,1,0:T(8,128)(2,1)}), bf16[8,80,1536]{2,1,0:T(8,128)(2,1)}, u32[]{:S(2)}, u32[]{:S(2)}) async-start(bf16[8,80,1536]{2,1,0:T(8,128)(2,1)} %bitcast.83), calls=%async_computation.3 | async-start | bytes 3932160 | tf_op jit(solution)/shard_map/all_to_all | solution.py:632
  87.2 14.5 %collective-permute-start.5 = (bf16[8,96,768]{2,1,0:T(8,128)(2,1)}, bf16[8,96,768]{2,1,0:T(8,128)(2,1)S(1)}, u32[]{:S(2)}, u32[]{:S(2)}) collective-permute-start(bf16[8,96,768]{2,1,0:T(8,128)(2,1)} %get-tuple-element.213.refs_13_), channel_id=1, source_target_pairs={{0,8},{8,0},{1,9},{9,1},{2,10},{10,2},{3,11},{11,3},{4,12},{12,4},... | collective-permute-start | bytes 3538952 | tf_op jit(solution)/shard_map/ppermute | solution.py:624
  116.8 33.2 %all-to-all-start.4 = ((bf16[8,80,1536]{2,1,0:T(8,128)(2,1)}), bf16[8,80,1536]{2,1,0:T(8,128)(2,1)}, u32[]{:S(2)}, u32[]{:S(2)}) async-start(bf16[8,80,1536]{2,1,0:T(8,128)(2,1)} %bitcast.96), calls=%async_computation.4 | async-start | bytes 3932160 | tf_op jit(solution)/shard_map/all_to_all | solution.py:632
  124.8 23.3 %collective-permute-start.7 = (bf16[640,768]{1,0:T(8,128)(2,1)S(1)}, bf16[640,768]{1,0:T(8,128)(2,1)}, u32[]{:S(2)}, u32[]{:S(2)}) collective-permute-start(bf16[640,768]{1,0:T(8,128)(2,1)S(1)} %constant_dynamic-slice_fusion), channel_id=1, source_target_pairs={{0,8},{8,0},{1,9},{9,1},{2,10},{10,2},{3,11},{11,3},{4,12},{12,4},... | collective-permute-start | bytes 2949128 | tf_op jit(solution)/shard_map/ppermute | solution.py:624
  128.3 18.3 %collective-permute-start.12 = (bf16[128,1536]{1,0:T(8,128)(2,1)S(1)}, bf16[128,1536]{1,0:T(8,128)(2,1)S(1)}, u32[]{:S(2)}, u32[]{:S(2)}) collective-permute-start(bf16[128,1536]{1,0:T(8,128)(2,1)S(1)} %collective-permute-done.10.refs_10_.refs_12_), channel_id=1, source_target_pairs={{0,16},{16,0},{32,48},{48,32},{1,17},{17,1},{33,49},{49,33},{2,18}... | collective-permute-start | bytes 1179656 | tf_op jit(solution)/shard_map/ppermute | solution.py:654
  129.8 16.9 %collective-permute-start.11 = (bf16[128,1536]{1,0:T(8,128)(2,1)S(1)}, bf16[128,1536]{1,0:T(8,128)(2,1)S(1)}, u32[]{:S(2)}, u32[]{:S(2)}) collective-permute-start(bf16[128,1536]{1,0:T(8,128)(2,1)S(1)} %collective-permute-done.10.refs_10_.refs_12_), channel_id=1, source_target_pairs={{0,48},{48,0},{16,32},{32,16},{1,49},{49,1},{17,33},{33,17},{2,50}... | collective-permute-start | bytes 1179656 | tf_op jit(solution)/shard_map/ppermute | solution.py:654
  150.0 25.7 %collective-permute-start.13 = (bf16[640,1536]{1,0:T(8,128)(2,1)}, bf16[640,1536]{1,0:T(8,128)(2,1)}, u32[]{:S(2)}, u32[]{:S(2)}) collective-permute-start(bf16[640,1536]{1,0:T(8,128)(2,1)} %bitcast.21.refs_1_), channel_id=1, source_target_pairs={{0,8},{8,0},{1,9},{9,1},{2,10},{10,2},{3,11},{11,3},{4,12},{12,4},... | collective-permute-start | bytes 5898248 | tf_op jit(solution)/shard_map/ppermute | solution.py:624
  163.5 32.2 %all-to-all-start.5 = ((bf16[8,80,1536]{2,1,0:T(8,128)(2,1)}), bf16[8,80,1536]{2,1,0:T(8,128)(2,1)}, u32[]{:S(2)}, u32[]{:S(2)}) async-start(bf16[8,80,1536]{2,1,0:T(8,128)(2,1)} %bitcast.97), calls=%async_computation.5 | async-start | bytes 3932160 | tf_op jit(solution)/shard_map/all_to_all | solution.py:632
  169.2 20.6 %collective-permute-start.16 = (bf16[128,1536]{1,0:T(8,128)(2,1)S(1)}, bf16[128,1536]{1,0:T(8,128)(2,1)S(1)}, u32[]{:S(2)}, u32[]{:S(2)}) collective-permute-start(bf16[128,1536]{1,0:T(8,128)(2,1)S(1)} %collective-permute-done.8.refs_11_.refs_13_), channel_id=1, source_target_pairs={{0,48},{48,0},{16,32},{32,16},{1,49},{49,1},{17,33},{33,17},{2,50}... | collective-permute-start | bytes 1179656 | tf_op jit(solution)/shard_map/ppermute | solution.py:654
  171.0 18.8 %collective-permute-start.17 = (bf16[128,1536]{1,0:T(8,128)(2,1)S(1)}, bf16[128,1536]{1,0:T(8,128)(2,1)}, u32[]{:S(2)}, u32[]{:S(2)}) collective-permute-start(bf16[128,1536]{1,0:T(8,128)(2,1)S(1)} %copy-done.14), channel_id=1, source_target_pairs={{0,16},{16,0},{32,48},{48,32},{1,17},{17,1},{33,49},{49,33},{2,18}... | collective-permute-start | bytes 1179656 | tf_op jit(solution)/shard_map/ppermute | solution.py:654
  208.1 26.9 %all-to-all-start.6 = ((bf16[8,128,512]{2,1,0:T(8,128)(2,1)}), bf16[8,128,512]{2,1,0:T(8,128)(2,1)S(1)}, u32[]{:S(2)}, u32[]{:S(2)}) async-start(bf16[8,128,512]{2,1,0:T(8,128)(2,1)} %bitcast.101), calls=%async_computation.6 | async-start | bytes 2097152 | tf_op jit(solution)/shard_map/all_to_all | solution.py:632
  217.1 28.7 %collective-permute-start.33 = (bf16[2,288,768]{2,1,0:T(8,128)(2,1)}, bf16[2,288,768]{2,1,0:T(8,128)(2,1)S(1)}, u32[]{:S(2)}, u32[]{:S(2)}) collective-permute-start(bf16[2,288,768]{2,1,0:T(8,128)(2,1)} %get-tuple-element.181), channel_id=1, source_target_pairs={{0,16},{16,0},{32,48},{48,32},{1,17},{17,1},{33,49},{49,33},{2,18}... | collective-permute-start | bytes 2654216 | tf_op jit(solution)/shard_map/ppermute | solution.py:654
  217.3 28.5 %collective-permute-start.34 = (bf16[2,288,768]{2,1,0:T(8,128)(2,1)}, bf16[2,288,768]{2,1,0:T(8,128)(2,1)}, u32[]{:S(2)}, u32[]{:S(2)}) collective-permute-start(bf16[2,288,768]{2,1,0:T(8,128)(2,1)} %get-tuple-element.183), channel_id=1, source_target_pairs={{0,48},{48,0},{16,32},{32,16},{1,49},{49,1},{17,33},{33,17},{2,50}... | collective-permute-start | bytes 2654216 | tf_op jit(solution)/shard_map/ppermute | solution.py:654
  239.0 41.6 %all-to-all-start.7 = ((bf16[8,80,1536]{2,1,0:T(8,128)(2,1)}), bf16[8,80,1536]{2,1,0:T(8,128)(2,1)S(1)}, u32[]{:S(2)}, u32[]{:S(2)}) async-start(bf16[8,80,1536]{2,1,0:T(8,128)(2,1)} %bitcast.95), calls=%async_computation.7 | async-start | bytes 3932160 | tf_op jit(solution)/shard_map/all_to_all | solution.py:632
  251.7 19.4 %collective-permute-start.26 = (bf16[128,128]{1,0:T(8,128)(2,1)S(1)}, bf16[128,128]{1,0:T(8,128)(2,1)S(1)}, u32[]{:S(2)}, u32[]{:S(2)}) collective-permute-start(bf16[128,128]{1,0:T(8,128)(2,1)S(1)} %copy-done.62), channel_id=1, source_target_pairs={{0,16},{16,0},{32,48},{48,32},{1,17},{17,1},{33,49},{49,33},{2,18}... | collective-permute-start | bytes 98312 | tf_op jit(solution)/shard_map/ppermute | solution.py:654
  253.1 18.1 %collective-permute-start.27 = (bf16[128,128]{1,0:T(8,128)(2,1)S(1)}, bf16[128,128]{1,0:T(8,128)(2,1)S(1)}, u32[]{:S(2)}, u32[]{:S(2)}) collective-permute-start(bf16[128,128]{1,0:T(8,128)(2,1)S(1)} %copy-done.61), channel_id=1, source_target_pairs={{0,48},{48,0},{16,32},{32,16},{1,49},{49,1},{17,33},{33,17},{2,50}... | collective-permute-start | bytes 98312 | tf_op jit(solution)/shard_map/ppermute | solution.py:654
  254.8 16.8 %collective-permute-start.28 = (bf16[128,128]{1,0:T(8,128)(2,1)S(1)}, bf16[128,128]{1,0:T(8,128)(2,1)S(1)}, u32[]{:S(2)}, u32[]{:S(2)}) collective-permute-start(bf16[128,128]{1,0:T(8,128)(2,1)S(1)} %copy-done.60), channel_id=1, source_target_pairs={{0,32},{32,0},{16,48},{48,16},{1,33},{33,1},{17,49},{49,17},{2,34}... | collective-permute-start | bytes 98312 | tf_op jit(solution)/shard_map/ppermute | solution.py:654
  267.2 21.2 %collective-permute-start.37 = (bf16[2,288,768]{2,1,0:T(8,128)(2,1)}, bf16[2,288,768]{2,1,0:T(8,128)(2,1)S(1)}, u32[]{:S(2)}, u32[]{:S(2)}) collective-permute-start(bf16[2,288,768]{2,1,0:T(8,128)(2,1)} %shard_map.241.refs_1_), channel_id=1, source_target_pairs={{0,64},{64,0},{1,65},{65,1},{2,66},{66,2},{3,67},{67,3},{4,68},{68... | collective-permute-start | bytes 2654216 | tf_op jit(solution)/shard_map/ppermute | solution.py:628
  280.6 31.8 %all-to-all-start.8 = ((bf16[16,96,512]{2,1,0:T(8,128)(2,1)}), bf16[16,96,512]{2,1,0:T(8,128)(2,1)}, u32[]{:S(2)}, u32[]{:S(2)}) async-start(bf16[16,96,512]{2,1,0:T(8,128)(2,1)} %bitcast.84), calls=%async_computation.8 | async-start | bytes 3145728 | tf_op jit(solution)/shard_map/all_to_all | solution.py:632
  295.0 22.5 %collective-permute-start.44 = (bf16[288,768]{1,0:T(8,128)(2,1)}, bf16[288,768]{1,0:T(8,128)(2,1)S(1)}, u32[]{:S(2)}, u32[]{:S(2)}) collective-permute-start(bf16[288,768]{1,0:T(8,128)(2,1)} %get-tuple-element.188.refs_0_), channel_id=1, source_target_pairs={{0,8},{8,0},{1,9},{9,1},{2,10},{10,2},{3,11},{11,3},{4,12},{12,4},... | collective-permute-start | bytes 1327112 | tf_op jit(solution)/shard_map/ppermute | solution.py:624
  296.5 21.6 %collective-permute-start.45 = (bf16[288,768]{1,0:T(8,128)(2,1)}, bf16[288,768]{1,0:T(8,128)(2,1)}, u32[]{:S(2)}, u32[]{:S(2)}) collective-permute-start(bf16[288,768]{1,0:T(8,128)(2,1)} %get-tuple-element.189.refs_1_), channel_id=1, source_target_pairs={{0,8},{8,0},{1,9},{9,1},{2,10},{10,2},{3,11},{11,3},{4,12},{12,4},... | collective-permute-start | bytes 1327112 | tf_op jit(solution)/shard_map/ppermute | solution.py:624
  296.5 21.2 %collective-permute-start.43 = (bf16[288,768]{1,0:T(8,128)(2,1)}, bf16[288,768]{1,0:T(8,128)(2,1)}, u32[]{:S(2)}, u32[]{:S(2)}) collective-permute-start(bf16[288,768]{1,0:T(8,128)(2,1)} %get-tuple-element.189.refs_1_), channel_id=1, source_target_pairs={{0,48},{48,0},{16,32},{32,16},{1,49},{49,1},{17,33},{33,17},{2,50}... | collective-permute-start | bytes 1327112 | tf_op jit(solution)/shard_map/ppermute | solution.py:654
  305.3 13.5 %collective-permute-start.48 = (bf16[288,768]{1,0:T(8,128)(2,1)S(1)}, bf16[288,768]{1,0:T(8,128)(2,1)}, u32[]{:S(2)}, u32[]{:S(2)}) collective-permute-start(bf16[288,768]{1,0:T(8,128)(2,1)S(1)} %collective-permute-done.42.refs_4_), channel_id=1, source_target_pairs={{0,8},{8,0},{1,9},{9,1},{2,10},{10,2},{3,11},{11,3},{4,12},{12,4},... | collective-permute-start | bytes 1327112 | tf_op jit(solution)/shard_map/ppermute | solution.py:624
  318.0 15.1 %collective-permute-start.40 = (bf16[288,768]{1,0:T(8,128)(2,1)}, bf16[288,768]{1,0:T(8,128)(2,1)S(1)}, u32[]{:S(2)}, u32[]{:S(2)}) collective-permute-start(bf16[288,768]{1,0:T(8,128)(2,1)} %collective-permute-done.38.refs_2_), channel_id=1, source_target_pairs={{0,16},{16,0},{32,48},{48,32},{1,17},{17,1},{33,49},{49,33},{2,18}... | collective-permute-start | bytes 1327112 | tf_op jit(solution)/shard_map/ppermute | solution.py:654
  318.8 14.3 %collective-permute-start.41 = (bf16[288,768]{1,0:T(8,128)(2,1)}, bf16[288,768]{1,0:T(8,128)(2,1)S(1)}, u32[]{:S(2)}, u32[]{:S(2)}) collective-permute-start(bf16[288,768]{1,0:T(8,128)(2,1)} %collective-permute-done.39.refs_3_), channel_id=1, source_target_pairs={{0,48},{48,0},{16,32},{32,16},{1,49},{49,1},{17,33},{33,17},{2,50}... | collective-permute-start | bytes 1327112 | tf_op jit(solution)/shard_map/ppermute | solution.py:654
  320.5 24.2 %all-to-all-start.9 = ((bf16[8,96,512]{2,1,0:T(8,128)(2,1)}), bf16[8,96,512]{2,1,0:T(8,128)(2,1)S(1)}, u32[]{:S(2)}, u32[]{:S(2)}) async-start(bf16[8,96,512]{2,1,0:T(8,128)(2,1)} %shard_map.239), calls=%async_computation.9 | async-start | bytes 1572864 | tf_op jit(solution)/shard_map/all_to_all | solution.py:632
  (94 other events, 709.2 us)

commit v3 on v2

--- a/solution.py
+++ b/solution.py
@@ -77,6 +77,15 @@
     low, rows = 2 * pair * HEAD_DIM, value.shape[0] // 2
     ref[:, pl.ds(low, HEAD_DIM)] = value[:rows]
     ref[:, pl.ds(low + HEAD_DIM, HEAD_DIM)] = value[rows:]
+
+
+def put_gain(out, total):
+    groups, _, lanes = out.shape
+    size = total.shape[1] // groups
+    for f in range(groups):
+        row = total[:, f * size : (f + 1) * size]
+        out[f, 0:1, :] = row[:, :lanes]
+        out[f, 1:2, pl.ds(0, size - lanes)] = row[:, lanes:]
 
 
 def key_kernel(place, src, gain, raw_own, raw_other, cos, sin, normed_o, scale_o, send_o, weight_o):
@@ -222,7 +231,7 @@
     keep_bo[...] = add(keep_b[s], got_b[s])
 
 
-def expert_end_kernel(place, keep_a, got_a, keep_b, got_b, out):
+def expert_end_kernel(place, keep_a, got_a, keep_b, got_b, mark, out):
     out[0] = add(keep_a[...], got_a[...])
     out[1] = add(keep_b[...], got_b[...])
 
@@ -345,7 +354,7 @@
         + scale * weighted
         - resid * (scale * scale * scale * inner * (1.0 / resid.shape[-1]))
     )
-    gain_o[...] = jnp.sum(grad_second * resid * scale, axis=0, keepdims=True)
+    put_gain(gain_o, jnp.sum(grad_second * resid * scale, axis=0, keepdims=True))
     grad_resid_o[...] = grad_resid
     grad_resid_o.send()
     attended = grad_resid.astype(BF)
@@ -429,21 +438,32 @@
         out[at, :] = t_dot(all_left[:, at], all_grads[...]).astype(BF)
 
 
-def pack_kernel(place, square, gains, *refs):
+def pack_kernel(place, square, one_own, one_got, two_own, two_got, *refs):
     grads, left = refs[:8], refs[8:16]
     out, all_grads, all_left, total, sems = refs[16:]
     copies = collect(interleave(grads[:4], grads[4:]), all_grads, sems, 0)
     copies += collect(left, all_left, sems, 8)
+    size, small = square.shape[1], total.shape[1]
+    count, groups, part, _ = out.shape
+    row = lax.broadcasted_iota(jnp.int32, (part, small), 0)
+    lane = lax.broadcasted_iota(jnp.int32, (part, small), 1)
+    short = lane < square.shape[0] // groups - small
+    gains = []
+    for f in range(groups):
+        one, two = one_own[f] + one_got[f], two_own[f] + two_got[f]
+        block = jnp.where(row == 0, one[0:1], 0.0)
+        block = jnp.where((row == 1) & short, one[1:2], block)
+        block = jnp.where(row == 2, two[0:1], block)
+        gains.append(jnp.where((row == 3) & short, two[1:2], block).astype(BF))
+        for y in range(count):
+            out[y, f, :, pl.ds(0, size)] = square[pl.ds((f * count + y) * part, part), :]
     for copy in copies:
         copy.wait()
     total[...] = t_dot(all_left[...], all_grads[...]).astype(BF)
-    size, small = square.shape[1], total.shape[1]
-    count, groups, part, _ = out.shape
     even = place[0] == 0
     for y in range(count):
         for f in range(groups):
             at = pl.ds((f * count + y) * part, part)
-            out[y, f, :, pl.ds(0, size)] = square[at, :]
             out[y, f, :, pl.ds(size, small)] = jnp.where(even, gains[f], total[at, :])
         out.send(y + 1)
 
@@ -457,12 +477,14 @@
         out[k] = total
 
 
-def final_kernel(place, own, other, mark, output_o, query_o, key_o, value_o, gains_o):
+def final_kernel(
+    place, own, other, mark, output_o, query_o, key_o, value_o, gain_one_o, gain_two_o
+):
     even = place[0] == 0
     part = own.shape[1]
     size = output_o.shape[1] // XS
     small = key_o.shape[1] * 2 // XS
-    total = jnp.zeros(gains_o.shape, F32)
+    total = jnp.zeros((8, small), F32)
     for y in range(YLO):
         rows = pl.ds(y * part, part)
         for x in range(XS):
@@ -475,8 +497,12 @@
             into = key_o if x < XS // 2 else value_o
             into[rows, pl.ds(x % (XS // 2) * small, small)] = second[:, size:]
             if y == 0:
-                total = total + first[:, size:]
-    gains_o[...] = total
+                total = total + first[:8, size:]
+    for ref, row in ((gain_one_o, 0), (gain_two_o, 2)):
+        ref[:, pl.ds(0, small)] = total[row : row + 1]
+        ref[:, pl.ds(small, ref.shape[1] - small)] = total[
+            row + 1 : row + 2, : ref.shape[1] - small
+        ]
 
 
 def key_back_kernel(place, parts, cos, sin, pre_o, *sent_o):
@@ -495,12 +521,19 @@
         out[...] = pre_o[:, pl.ds(pl.multiple_of(part * size, size), size)]
 
 
+def query_back_kernel(place, query, query_w, out):
+    out[...] = dot_t(query[...], query_w[...])
+
+
 def input_kernel(
-    place, query, pre, src, scale_i, gain, query_w, kv_w, grad_resid, input_o, gain_o
+    place, partial, pre, src, scale_i, gain, kv_w, grad_resid, input_o, gain_o, mark_o
 ):
-    grad_normed = dot_t(query[...], query_w[...]) + dot_t(pre[...], kv_w[...])
+    mark_o[...] = jnp.zeros(mark_o.shape, F32)
+    grad_normed = partial[...] + dot_t(pre[...], kv_w[...])
     source = src[...].astype(F32)
     scale = scale_i[:, :1]
+    put_gain(gain_o, jnp.sum(grad_normed * source * scale, axis=0, keepdims=True))
+    send(gain_o)
     weighted = grad_normed * gain[...]
     inner = jnp.sum(weighted * source, axis=-1, keepdims=True)
     input_o[...] = (
@@ -508,7 +541,6 @@
         + scale * weighted
         - source * (scale * scale * scale * inner * (1.0 / source.shape[-1]))
     ).astype(BF)
-    gain_o[...] = jnp.sum(grad_normed * source * scale, axis=0, keepdims=True)
 
 
 class Far:
@@ -830,7 +862,7 @@
         [place_at, Far(back_rows), Far(one_hot_t), Far(residual), Far(scale_two), gain_two,
          Far(cotangent[0]), Far(output_weight), Far(probs), Far(kv_all), Far(query_rot), cosine,
          sine],
-        [((tok, width), F32), ((tok, width), BF), ((1, width), F32), ((tok, width), BF),
+        [((tok, width), F32), ((tok, width), BF), ((groups, 2, HEAD_DIM), F32), ((tok, width), BF),
          ((length, 2 * kv_width), BF)] + [((tok, half), BF)] * XS,
     )
     kv_got = exchange(kv_back, "fsdp")
@@ -841,6 +873,12 @@
     )
     e_got_a, e_got_b = flip(e_send_a, PAIRS_T), flip(e_send_b, PAIRS_S)
     qo_set = fan(qo_sent)
+    partial = call(
+        query_back_kernel,
+        [place_at, Far(grad_query_pre), Far(query_weight)],
+        [((tok, width), F32)],
+    )[0]
+    qo_set[1], qo_set[2], qo_set[3], partial = tie(qo_set[1], qo_set[2], qo_set[3], partial)
     whole = 2 * XS * tok
     square_grad = call(
         square_weight_kernel,
@@ -850,48 +888,47 @@
          pltpu.SemaphoreType.DMA((16,))],
         raw=range(1, 17),
     )[0]
-    kv_got, square_grad = tie(kv_got, square_grad)
+    kv_got, expert_out, square_grad = tie(kv_got, expert_out, square_grad)
+    returned = exchange(expert_out, "fsdp")
     grad_kv_pre, *kv_sent = call(
         key_back_kernel,
         [place_at, Far(kv_got.reshape(groups, tok, 2 * kv_width)), cosine, sine],
         [((tok, 2 * kv_width), BF)] + [((tok, 2 * kv_width // XS), BF)] * XS,
     )
-    kv_sent[0], expert_out = tie(kv_sent[0], expert_out)
-    returned = exchange(expert_out, "fsdp")
     kv_set = fan(kv_sent)
+    input_grad, gain_one_part, mark = call(
+        input_kernel,
+        [place_at, Far(partial), Far(grad_kv_pre), Far(inputs[0]), Far(scale_one), gain_one,
+         Far(kv_weight), Far(grad_residual)],
+        [((tok, width), BF), ((groups, 2, HEAD_DIM), F32), ((8, HEAD_DIM), F32)],
+        micros=6,
+    )
+
+    kv_set[1], kv_set[2], kv_set[3], mark = tie(kv_set[1], kv_set[2], kv_set[3], mark)
+    e_got_a, e_got_b, mark = tie(e_got_a, e_got_b, mark)
     e_sum = call(
         expert_end_kernel,
-        [place_at, Far(e_keep_a), Far(e_got_a), Far(e_keep_b), Far(e_got_b)],
+        [place_at, Far(e_keep_a), Far(e_got_a), Far(e_keep_b), Far(e_got_b), mark],
         [(e_part, BF)],
     )[0]
     e_other_y = swap_y(e_sum)
-    input_grad, gain_one_part = call(
-        input_kernel,
-        [place_at, Far(grad_query_pre), Far(grad_kv_pre), Far(inputs[0]), Far(scale_one), gain_one,
-         Far(query_weight), Far(kv_weight), Far(grad_residual)],
-        [((tok, width), BF), ((1, width), F32)],
-    )
-
     e_zero_a, e_zero_b = call(pair_kernel, [place_at, Far(e_sum), Far(e_other_y)], [(e_part[1:], BF)] * 2)
     e_one_a, e_one_b = flip(e_zero_a, PAIRS_T), flip(e_zero_b, PAIRS_S)
     e_two_a, e_two_b = flip(e_zero_a, PAIRS_S), flip(e_zero_b, PAIRS_T)
 
     spare = 2 * kv_width // XS
     part = rows // YLO
-    gain_parts = jnp.concatenate([gain_one_part, gain_two_part])
-    gain_parts = gain_parts + swap(gain_parts)
-    gain_parts = gain_parts.reshape(2, groups, part, YLO).transpose(1, 2, 0, 3)
-    gain_parts = gain_parts.reshape(groups, part, 2 * YLO).astype(BF)
-    gain_parts = jnp.pad(gain_parts, ((0, 0), (0, 0), (0, spare - 2 * YLO)))
     packed_width = width // XS + spare
     packed = call(
         pack_kernel,
-        [place_at, Far(square_grad), gain_parts]
+        [place_at]
+        + [Far(v) for v in (square_grad, gain_one_part, swap(gain_one_part), gain_two_part,
+                            swap(gain_two_part))]
         + [Far(v) for v in (*kv_set, *[swap(v) for v in kv_set], *left)],
         [Far((YLO, groups, part, packed_width), BF, 2)],
         [pltpu.VMEM((whole, spare), BF), pltpu.VMEM((whole, width), BF),
          pltpu.VMEM((width, spare), BF), pltpu.SemaphoreType.DMA((16,))],
-        raw=range(3, 19),
+        raw=range(6, 22),
     )[0]
     packed, returned = tie(packed, returned)
     packed = exchange(packed.reshape(YLO * groups, part, packed_width), ("ylo", "fsdp"))
@@ -917,23 +954,21 @@
         half,
     )
     spreaded, e_mark = tie(spreaded, e_mark)
-    grad_output_w, grad_query_w, grad_key_w, grad_value_w, gains_sum = call(
+    grad_output_w, grad_query_w, grad_key_w, grad_value_w, grad_one, grad_two = call(
         final_kernel,
         [place_at, Far(spreaded), Far(swap(spreaded)), e_mark],
         [((rows, width), F32), ((rows, width), F32), ((rows, kv_width), F32),
-         ((rows, kv_width), F32), ((part, spare), F32)],
-    )
-    gains_sum = gains_sum[:, : 2 * YLO].reshape(part, 2, YLO).transpose(1, 0, 2)
-    gains_sum = gains_sum.reshape(2, rows)
+         ((rows, kv_width), F32), ((1, rows), F32), ((1, rows), F32)],
+    )
     return (
         outputs[None],
         input_grad[None],
-        gains_sum[0],
+        grad_one[0],
         grad_query_w,
         grad_key_w,
         grad_value_w,
         grad_output_w,
-        gains_sum[1],
+        grad_two[0],
         grad_gate[None],
         grad_up[None],
         grad_down[None],

time: 361 us -> 356 us (0.986)
  local copies, waits for them, and re-layouts: 35.7 us -> 29.1 us
    pallas_call x14 -> x15, Pallas kernels: 92 us -> 95 us  [call(): pl.pallas_call(whole, out_shape=[jax.ShapeDtypeStruct(out.value, out.kind...]
    ppermute x28 -> x29, starting transfers between devices: 36.5 us -> 38.5 us  [swap(): return lax.ppermute(v, 'core', [(0, 1), (1, 0)])]
    unnamed x132 -> x128, local copies, waits for them, and re-layouts: 13.9 us -> 11.9 us
    ppermute x28 -> x29, waiting for transfers between devices: 7.26 us -> 7.72 us  [swap(): return lax.ppermute(v, 'core', [(0, 1), (1, 0)])]
  transfers between devices with their start and end apart: 63 -> 64, of which waited for: 23 -> 29; matrix products, arithmetic and copies ran while one was open for 11% -> 11% of each run, Pallas kernels for 25% -> 26%
where the time goes in v3:
time: 356 us; the launch traced here: 350 us
  starting transfers between devices  118 us (33%)
  Pallas kernels  106 us (30%)
  waiting for transfers between devices  70.4 us (20%)
  local copies, waits for them, and re-layouts  29.1 us (8%)
  matrix products  12.5 us (4%)
  other arithmetic  10.9 us (3%)
    pallas_call x15, Pallas kernels, call(): pl.pallas_call(whole, out_shape=[jax.ShapeDtypeStruct(out.value, out.kind...  95 us
    all_to_all x10, starting transfers between devices, exchange(): return lax.all_to_all(v, axis, 0, 0, tiled=True)  55.4 us
    ppermute x29, starting transfers between devices, swap(): return lax.ppermute(v, 'core', [(0, 1), (1, 0)])  38.5 us
    all_to_all x10, waiting for transfers between devices, exchange(): return lax.all_to_all(v, axis, 0, 0, tiled=True)  36.8 us
    ppermute x24, waiting for transfers between devices, flip(): return lax.ppermute(v, 'x', pairs)  25.1 us
    ppermute x24, starting transfers between devices, flip(): return lax.ppermute(v, 'x', pairs)  23.9 us
    unnamed x128, local copies, waits for them, and re-layouts  11.9 us
    pallas_call x2, Pallas kernels, expert_outputs(): pl.pallas_call(kernel, out_shape=shapes, in_specs=[pl.BlockSpec(memory_sp...  11.4 us
  transfers between devices with their start and end apart: 64, of which 29 were waited for; matrix products, arithmetic and copies ran while one was open for 11% of the time, Pallas kernels for 26%

profile of v3, /device:TPU:1, one launch (start us, length us, event | category | flops | bytes accessed | tf_op | source)
XLA Modules:
  0.0 349.7 jit_solution(5523052887757568342)
XLA Ops:
  4.2 8.6 %all-to-all-start = ((bf16[8,40,1536]{2,1,0:T(8,128)(2,1)}), bf16[8,40,1536]{2,1,0:T(8,128)(2,1)S(1)}, u32[]{:S(2)}, u32[]{:S(2)}) async-start(bf16[8,40,1536]{2,1,0:T(8,128)(2,1)} %broadcast_in_dim.91), calls=%async_computation | async-start | bytes 1966080 | tf_op jit(solution)/shard_map/all_to_all | solution.py:664
  18.0 10.1 %all-to-all-done = bf16[8,40,1536]{2,1,0:T(8,128)(2,1)S(1)} async-done(((bf16[8,40,1536]{2,1,0:T(8,128)(2,1)}), bf16[8,40,1536]{2,1,0:T(8,128)(2,1)S(1)}, u32[]{:S(2)}, u32[]{:S(2)}) %all-to-all-start) | async-done | bytes 983072 | tf_op jit(solution)/shard_map/all_to_all | solution.py:664
  28.1 4.4 %all-to-all-start.1 = ((bf16[8,96,1536]{2,1,0:T(8,128)(2,1)}), bf16[8,96,1536]{2,1,0:T(8,128)(2,1)}, u32[]{:S(2)}, u32[]{:S(2)}) async-start(bf16[8,96,1536]{2,1,0:T(8,128)(2,1)} %broadcast_in_dim.92), calls=%async_computation.1 | async-start | bytes 4718592 | tf_op jit(solution)/shard_map/all_to_all | solution.py:664
  49.7 4.0 %shard_map.230 = (bf16[128,1536]{1,0:T(8,128)(2,1)}, f32[128,128]{1,0:T(8,128)}, bf16[8,128,512]{2,1,0:T(8,128)(2,1)}, bf16[1536,512]{1,0:T(8,128)(2,1)}) custom-call(s32[4]{0:T(128)} %pad_add_fusion.refs_0_.place, bf16[128,1536]{1,0:T(8,128)(2,1)} %bitcast.92, f32[1,1536]{1,0:T(1,128)} %reshape.223.refs_2_.refs_5_, bf16[8,32,1536]{2,1,0:T(8,128)(2,1)} %slice.49.refs_3_, ...), custom_call_target="tpu_custom_call" | custom-call | tf_op jit(solution)/shard_map/pallas_call | solution.py:637
  53.7 7.9 %all-to-all-done.1 = bf16[8,96,1536]{2,1,0:T(8,128)(2,1)} async-done(((bf16[8,96,1536]{2,1,0:T(8,128)(2,1)}), bf16[8,96,1536]{2,1,0:T(8,128)(2,1)}, u32[]{:S(2)}, u32[]{:S(2)}) %all-to-all-start.1) | async-done | bytes 2359328 | tf_op jit(solution)/shard_map/all_to_all | solution.py:664
  61.6 5.0 %all-to-all-start.2 = ((bf16[8,128,512]{2,1,0:T(8,128)(2,1)}), bf16[8,128,512]{2,1,0:T(8,128)(2,1)S(1)}, u32[]{:S(2)}, u32[]{:S(2)}) async-start(bf16[8,128,512]{2,1,0:T(8,128)(2,1)} %get-tuple-element.132), calls=%async_computation.2 | async-start | bytes 2097152 | tf_op jit(solution)/shard_map/all_to_all | solution.py:664
  72.8 9.1 %all-to-all-done.2 = bf16[8,128,512]{2,1,0:T(8,128)(2,1)S(1)} async-done(((bf16[8,128,512]{2,1,0:T(8,128)(2,1)}), bf16[8,128,512]{2,1,0:T(8,128)(2,1)S(1)}, u32[]{:S(2)}, u32[]{:S(2)}) %all-to-all-start.2) | async-done | bytes 1048608 | tf_op jit(solution)/shard_map/all_to_all | solution.py:664
  82.9 4.3 %all-to-all-start.3 = ((bf16[8,80,1536]{2,1,0:T(8,128)(2,1)}), bf16[8,80,1536]{2,1,0:T(8,128)(2,1)}, u32[]{:S(2)}, u32[]{:S(2)}) async-start(bf16[8,80,1536]{2,1,0:T(8,128)(2,1)} %bitcast.79), calls=%async_computation.3 | async-start | bytes 3932160 | tf_op jit(solution)/shard_map/all_to_all | solution.py:664
  90.3 5.6 %collective-permute-done.1.refs_10_ = bf16[8,96,768]{2,1,0:T(8,128)(2,1)} collective-permute-done((bf16[8,96,768]{2,1,0:T(8,128)(2,1)}, bf16[8,96,768]{2,1,0:T(8,128)(2,1)}, u32[]{:S(2)}, u32[]{:S(2)}) %collective-permute-start.1) | collective-permute-done | bytes 1179680 | tf_op jit(solution)/shard_map/ppermute | solution.py:686
  104.0 12.6 %shard_map.231 = (bf16[8,192,1536]{2,1,0:T(8,128)(2,1)}, bf16[8,192,1536]{2,1,0:T(8,128)(2,1)}, bf16[128,1536]{1,0:T(8,128)(2,1)}, bf16[128,1536]{1,0:T(8,128)(2...) custom-call(s32[4]{0:T(128)} %pad_add_fusion.refs_0_.place, ...), custom_call_target="tpu_custom_call" | custom-call | tf_op jit(solution)/shard_map/pallas_call | solution.py:637
  116.6 6.7 %all-to-all-start.4 = ((bf16[8,80,1536]{2,1,0:T(8,128)(2,1)}), bf16[8,80,1536]{2,1,0:T(8,128)(2,1)}, u32[]{:S(2)}, u32[]{:S(2)}) async-start(bf16[8,80,1536]{2,1,0:T(8,128)(2,1)} %bitcast.89), calls=%async_computation.4 | async-start | bytes 3932160 | tf_op jit(solution)/shard_map/all_to_all | solution.py:664
  130.0 4.6 %fusion.3.refs_2_ = f32[640,768]{1,0:T(8,128)} fusion(bf16[640,1536]{1,0:T(8,128)(2,1)} %bitcast.19.refs_7_, bf16[1,768,1536]{2,1,0:T(8,128)(2,1)S(1)} %copy-done), kind=kOutput, calls=%fused_computation.6 | convolution fusion | flops 1509949440 | bytes 6291456 | tf_op jit(solution)/shard_map/dot_general | solution.py:41
  137.1 8.4 %collective-permute-done.11.refs_14_.refs_19_ = bf16[128,1536]{1,0:T(8,128)(2,1)S(1)} collective-permute-done((bf16[128,1536]{1,0:T(8,128)(2,1)S(1)}, bf16[128,1536]{1,0:T(8,128)(2,1)S(1)}, u32[]{:S(2)}, u32[]{:S(2)}) %collective-permute-start.11) | collective-permute-done | bytes 393248 | tf_op jit(solution)/shard_map/ppermute | solution.py:686
  151.9 11.6 %shard_map.232 = (bf16[640,768]{1,0:T(8,128)(2,1)}, bf16[640,768]{1,0:T(8,128)(2,1)}, bf16[640,768]{1,0:T(8,128)(2,1)}, bf16[640,1536]{1,0:T(8,128)(2,1)}) custom-call(s32[4]{0:T(128)} %pad_add_fusion.refs_0_.place, bf16[640,1536]{1,0:T(8,128)(2,1)} %bitcast.21.refs_1_, f32[640,768]{1,0:T(8,128)} %fusion.3.refs_2_, bf16[1536,768]{1,0:T(8,128)(2,1)} %bitcast.86, ...), custom_call_target="tpu_custom_call" | custom-call | tf_op jit(solution)/shard_map/pallas_call | solution.py:637
  163.6 4.4 %all-to-all-start.5 = ((bf16[8,80,1536]{2,1,0:T(8,128)(2,1)}), bf16[8,80,1536]{2,1,0:T(8,128)(2,1)}, u32[]{:S(2)}, u32[]{:S(2)}) async-start(bf16[8,80,1536]{2,1,0:T(8,128)(2,1)} %bitcast.90), calls=%async_computation.5 | async-start | bytes 3932160 | tf_op jit(solution)/shard_map/all_to_all | solution.py:664
  170.5 4.1 %convolution_convert_fusion = bf16[640,1536]{1,0:T(8,128)(2,1)} fusion(bf16[640,768]{1,0:T(8,128)(2,1)} %get-tuple-element.145.refs_5_, bf16[1,768,1536]{2,1,0:T(8,128)(2,1)S(1)} %copy-done), kind=kOutput, calls=%fused_computation.1 | convolution fusion | flops 1510932480 | bytes 5308416 | tf_op jit(solution)/shard_map/dot_general | solution.py:37
  176.0 12.9 %shard_map.233 = (bf16[2,288,768]{2,1,0:T(8,128)(2,1)}, bf16[2,288,768]{2,1,0:T(8,128)(2,1)}, bf16[2,288,768]{2,1,0:T(8,128)(2,1)}, bf16[2,288,768]{2,1,0:T(8,128)(2,1)}) custom-call(s32[4]{0:T(128)} %pad_add_fusion.refs_0_.place, bf16[640,1536]{1,0:T(8,128)(2,1)} %bitcast.21.refs_1_, bf16[640,1536]{1,0:T(8,128)(2,1)} %collective-permute-done.13.refs_2_, ...), custom_call_target="tpu_custom_call" | custom-call | tf_op jit(solution)/shard_map/pallas_call | solution.py:637
  189.6 5.5 %all-to-all-done.5 = bf16[8,80,1536]{2,1,0:T(8,128)(2,1)} async-done(((bf16[8,80,1536]{2,1,0:T(8,128)(2,1)}), bf16[8,80,1536]{2,1,0:T(8,128)(2,1)}, u32[]{:S(2)}, u32[]{:S(2)}) %all-to-all-start.5) | async-done | bytes 1966112 | tf_op jit(solution)/shard_map/all_to_all | solution.py:664
  195.1 12.4 %shard_map.234 = (f32[128,1536]{1,0:T(8,128)}, bf16[128,1536]{1,0:T(8,128)(2,1)}, f32[8,2,128]{2,1,0:T(2,128)}, bf16[128,1536]{1,0:T(8,128)(2,1)}, bf16[1024,512...) custom-call(s32[4]{0:T(128)} %pad_add_fusion.refs_0_.place, ...), custom_call_target="tpu_custom_call" | custom-call | tf_op jit(solution)/shard_map/pallas_call | solution.py:637
  218.8 5.7 %shard_map.235.refs_1_ = f32[128,1536]{1,0:T(8,128)} custom-call(s32[4]{0:T(128)} %pad_add_fusion.refs_0_.place, bf16[128,1536]{1,0:T(8,128)(2,1)} %get-tuple-element.165.refs_1_, bf16[1536,1536]{1,0:T(8,128)(2,1)} %bitcast.82), custom_call_target="tpu_custom_call" | custom-call | tf_op jit(solution)/shard_map/pallas_call | solution.py:637
  230.8 5.9 %shard_map.236.refs_1_ = bf16[1536,384]{1,0:T(8,128)(2,1)} custom-call(s32[4]{0:T(128)} %pad_add_fusion.refs_0_.place, bf16[128,768]{1,0:T(8,128)(2,1)} %get-tuple-element.161.refs_1_, bf16[128,768]{1,0:T(8,128)(2,1)} %copy-done.35, bf16[128,768]{1,0:T(8,128)(2,1)} %copy-done.36, bf16[128,768]{1,0:T(8,128)(2,1)} %copy-done.37, bf16[128,768]{1,0:T(8,128)(2,1)} %copy-done.38, ...), custom_call_target="tpu_custom_call" | custom-call | tf_op jit(solution)/shard_map/pallas_call | solution.py:637
  237.7 6.8 %all-to-all-start.7 = ((bf16[8,80,1536]{2,1,0:T(8,128)(2,1)}), bf16[8,80,1536]{2,1,0:T(8,128)(2,1)S(1)}, u32[]{:S(2)}, u32[]{:S(2)}) async-start(bf16[8,80,1536]{2,1,0:T(8,128)(2,1)} %bitcast.88), calls=%async_computation.7 | async-start | bytes 3932160 | tf_op jit(solution)/shard_map/all_to_all | solution.py:664
  244.5 3.9 %shard_map.241 = (bf16[288,768]{1,0:T(8,128)(2,1)}, bf16[288,768]{1,0:T(8,128)(2,1)}, bf16[288,768]{1,0:T(8,128)(2,1)}, bf16[288,768]{1,0:T(8,128)(2,1)}) custom-call(s32[4]{0:T(128)} %pad_add_fusion.refs_0_.place, bf16[2,288,768]{2,1,0:T(8,128)(2,1)} %get-tuple-element.199.refs_1_, bf16[2,288,768]{2,1,0:T(8,128)(2,1)} %collective-permute-done.34.refs_2_, ...), custom_call_target="tpu_custom_call" | custom-call | tf_op jit(solution)/shard_map/pallas_call | solution.py:637
  255.7 4.5 %shard_map.238 = (bf16[128,1536]{1,0:T(8,128)(2,1)}, f32[8,2,128]{2,1,0:T(2,128)}, f32[8,128]{1,0:T(8,128)}) custom-call(s32[4]{0:T(128)} %pad_add_fusion.refs_0_.place, f32[128,1536]{1,0:T(8,128)} %shard_map.235.refs_1_, bf16[128,512]{1,0:T(8,128)(2,1)} %get-tuple-element.177.refs_2_, bf16[128,1536]{1,0:T(8,128)(2,1)} %bitcast.94, ...), custom_call_target="tpu_custom_call" | custom-call | flops 6000000000 | tf_op jit(solution)/shard_map/pallas_call | solution.py:637
  273.2 5.4 %shard_map.239 = bf16[2,8,96,512]{3,2,1,0:T(8,128)(2,1)} custom-call(s32[4]{0:T(128)} %pad_add_fusion.refs_0_.place, bf16[1536,384]{1,0:T(8,128)(2,1)} %shard_map.236.refs_1_, f32[8,2,128]{2,1,0:T(2,128)} %get-tuple-element.181.refs_2_, f32[8,2,128]{2,1,0:T(2,128)} %copy-done.54, f32[8,2,128]{2,1,0:T(2,128)} %get-tuple-element.182.refs_4_, ...), custom_call_target="tpu_custom_call" | custom-call | tf_op jit(solution)/shard_map/pallas_call | solution.py:637
  278.6 7.5 %all-to-all-start.8 = ((bf16[16,96,512]{2,1,0:T(8,128)(2,1)}), bf16[16,96,512]{2,1,0:T(8,128)(2,1)}, u32[]{:S(2)}, u32[]{:S(2)}) async-start(bf16[16,96,512]{2,1,0:T(8,128)(2,1)} %bitcast.80), calls=%async_computation.8 | async-start | bytes 3145728 | tf_op jit(solution)/shard_map/all_to_all | solution.py:664
  295.4 4.1 %collective-permute-start.45 = (bf16[288,768]{1,0:T(8,128)(2,1)}, bf16[288,768]{1,0:T(8,128)(2,1)S(1)}, u32[]{:S(2)}, u32[]{:S(2)}) collective-permute-start(bf16[288,768]{1,0:T(8,128)(2,1)} %get-tuple-element.211.refs_0_), channel_id=1, source_target_pairs={{0,8},{8,0},{1,9},{9,1},{2,10},{10,2},{3,11},{11,3},{4,12},{12,4},... | collective-permute-start | bytes 1327112 | tf_op jit(solution)/shard_map/ppermute | solution.py:656
  301.4 7.4 %collective-permute-start.46 = (bf16[288,768]{1,0:T(8,128)(2,1)}, bf16[288,768]{1,0:T(8,128)(2,1)S(1)}, u32[]{:S(2)}, u32[]{:S(2)}) collective-permute-start(bf16[288,768]{1,0:T(8,128)(2,1)} %get-tuple-element.212.refs_1_), channel_id=1, source_target_pairs={{0,8},{8,0},{1,9},{9,1},{2,10},{10,2},{3,11},{11,3},{4,12},{12,4},... | collective-permute-start | bytes 1327112 | tf_op jit(solution)/shard_map/ppermute | solution.py:656
  317.6 4.0 %all-to-all-start.9 = ((bf16[8,96,512]{2,1,0:T(8,128)(2,1)}), bf16[8,96,512]{2,1,0:T(8,128)(2,1)S(1)}, u32[]{:S(2)}, u32[]{:S(2)}) async-start(bf16[8,96,512]{2,1,0:T(8,128)(2,1)} %shard_map.240), calls=%async_computation.9 | async-start | bytes 1572864 | tf_op jit(solution)/shard_map/all_to_all | solution.py:664
  323.4 7.3 %shard_map.244 = (f32[1536,768]{1,0:T(8,128)}, f32[1536,768]{1,0:T(8,128)}, f32[768,1536]{1,0:T(8,128)}, f32[8,128]{1,0:T(8,128)}) custom-call(s32[4]{0:T(128)} %pad_add_fusion.refs_0_.place, bf16[288,768]{1,0:T(8,128)(2,1)} %get-tuple-element.211.refs_0_, bf16[288,768]{1,0:T(8,128)(2,1)} %get-tuple-element.212.refs_1_, ...), custom_call_target="tpu_custom_call" | custom-call | tf_op jit(solution)/shard_map/pallas_call | solution.py:325
  338.1 4.1 %shard_map.245 = (f32[1536,768]{1,0:T(8,128)}, f32[1536,768]{1,0:T(8,128)}, f32[768,1536]{1,0:T(8,128)}, f32[8,128]{1,0:T(8,128)}) custom-call(s32[4]{0:T(128)} %pad_add_fusion.refs_0_.place, bf16[288,768]{1,0:T(8,128)(2,1)} %copy-done.24, bf16[288,768]{1,0:T(8,128)(2,1)} %copy-done.26, ...), custom_call_target="tpu_custom_call", output_to_operand_aliasing={{0}: (7, {}), {1}: (8, {}), {2}: (9, {})} | custom-call | tf_op jit(solution)/shard_map/pallas_call | solution.py:325
  345.5 3.7 %shard_map.246 = (f32[192,1536]{1,0:T(8,128)}, f32[192,1536]{1,0:T(8,128)}, f32[192,256]{1,0:T(8,128)}, f32[192,256]{1,0:T(8,128)}, f32[1,192]{1,0:T(1,128)}, /*index=5*/f32[1,192]{1,0:T(1,128)}) custom-call(s32[4]{0:T(128)} %pad_add_fusion.refs_0_.place, bf16[8,96,512]{2,1,0:T(8,128)(2,1)} %copy-done.5, bf16[8,96,512]{2,1,0:T(8,128)(2,1)} %copy-done.19, ...), custom_call_target="tpu_custom_call" | custom-call | tf_op jit(solution)/shard_map/pallas_call | solution.py:637
  (295 shorter events, 135.1 us)
Async XLA Ops:
  4.2 23.9 %all-to-all-start = ((bf16[8,40,1536]{2,1,0:T(8,128)(2,1)}), bf16[8,40,1536]{2,1,0:T(8,128)(2,1)S(1)}, u32[]{:S(2)}, u32[]{:S(2)}) async-start(bf16[8,40,1536]{2,1,0:T(8,128)(2,1)} %broadcast_in_dim.91), calls=%async_computation | async-start | bytes 1966080 | tf_op jit(solution)/shard_map/all_to_all | solution.py:664
  28.1 33.5 %all-to-all-start.1 = ((bf16[8,96,1536]{2,1,0:T(8,128)(2,1)}), bf16[8,96,1536]{2,1,0:T(8,128)(2,1)}, u32[]{:S(2)}, u32[]{:S(2)}) async-start(bf16[8,96,1536]{2,1,0:T(8,128)(2,1)} %broadcast_in_dim.92), calls=%async_computation.1 | async-start | bytes 4718592 | tf_op jit(solution)/shard_map/all_to_all | solution.py:664
  36.2 13.5 %collective-permute-start = (bf16[8,32,1536]{2,1,0:T(8,128)(2,1)}, bf16[8,32,1536]{2,1,0:T(8,128)(2,1)}, u32[]{:S(2)}, u32[]{:S(2)}) collective-permute-start(bf16[8,32,1536]{2,1,0:T(8,128)(2,1)} %slice.49.refs_3_), channel_id=1, source_target_pairs={{0,8},{8,0},{1,9},{9,1},{2,10},{10,2},{3,11},{11,3},{4,12},{12,4},... | collective-permute-start | bytes 2359304 | tf_op jit(solution)/shard_map/ppermute | solution.py:656
  61.6 20.3 %all-to-all-start.2 = ((bf16[8,128,512]{2,1,0:T(8,128)(2,1)}), bf16[8,128,512]{2,1,0:T(8,128)(2,1)S(1)}, u32[]{:S(2)}, u32[]{:S(2)}) async-start(bf16[8,128,512]{2,1,0:T(8,128)(2,1)} %get-tuple-element.132), calls=%async_computation.2 | async-start | bytes 2097152 | tf_op jit(solution)/shard_map/all_to_all | solution.py:664
  69.8 26.1 %collective-permute-start.1 = (bf16[8,96,768]{2,1,0:T(8,128)(2,1)}, bf16[8,96,768]{2,1,0:T(8,128)(2,1)}, u32[]{:S(2)}, u32[]{:S(2)}) collective-permute-start(bf16[8,96,768]{2,1,0:T(8,128)(2,1)} %get-tuple-element.238.refs_9_), channel_id=1, source_target_pairs={{0,16},{16,0},{32,48},{48,32},{1,17},{17,1},{33,49},{49,33},{2,18}... | collective-permute-start | bytes 3538952 | tf_op jit(solution)/shard_map/ppermute | solution.py:686
  71.0 27.5 %collective-permute-start.4 = (bf16[8,96,768]{2,1,0:T(8,128)(2,1)}, bf16[8,96,768]{2,1,0:T(8,128)(2,1)}, u32[]{:S(2)}, u32[]{:S(2)}) collective-permute-start(bf16[8,96,768]{2,1,0:T(8,128)(2,1)} %get-tuple-element.237.refs_13_), channel_id=1, source_target_pairs={{0,48},{48,0},{16,32},{32,16},{1,49},{49,1},{17,33},{33,17},{2,50}... | collective-permute-start | bytes 3538952 | tf_op jit(solution)/shard_map/ppermute | solution.py:686
  82.9 33.7 %all-to-all-start.3 = ((bf16[8,80,1536]{2,1,0:T(8,128)(2,1)}), bf16[8,80,1536]{2,1,0:T(8,128)(2,1)}, u32[]{:S(2)}, u32[]{:S(2)}) async-start(bf16[8,80,1536]{2,1,0:T(8,128)(2,1)} %bitcast.79), calls=%async_computation.3 | async-start | bytes 3932160 | tf_op jit(solution)/shard_map/all_to_all | solution.py:664
  87.3 14.6 %collective-permute-start.2 = (bf16[8,96,768]{2,1,0:T(8,128)(2,1)}, bf16[8,96,768]{2,1,0:T(8,128)(2,1)S(1)}, u32[]{:S(2)}, u32[]{:S(2)}) collective-permute-start(bf16[8,96,768]{2,1,0:T(8,128)(2,1)} %get-tuple-element.238.refs_9_), channel_id=1, source_target_pairs={{0,8},{8,0},{1,9},{9,1},{2,10},{10,2},{3,11},{11,3},{4,12},{12,4},... | collective-permute-start | bytes 3538952 | tf_op jit(solution)/shard_map/ppermute | solution.py:656
  116.6 33.2 %all-to-all-start.4 = ((bf16[8,80,1536]{2,1,0:T(8,128)(2,1)}), bf16[8,80,1536]{2,1,0:T(8,128)(2,1)}, u32[]{:S(2)}, u32[]{:S(2)}) async-start(bf16[8,80,1536]{2,1,0:T(8,128)(2,1)} %bitcast.89), calls=%async_computation.4 | async-start | bytes 3932160 | tf_op jit(solution)/shard_map/all_to_all | solution.py:664
  124.7 21.7 %collective-permute-start.7 = (bf16[640,768]{1,0:T(8,128)(2,1)S(1)}, bf16[640,768]{1,0:T(8,128)(2,1)}, u32[]{:S(2)}, u32[]{:S(2)}) collective-permute-start(bf16[640,768]{1,0:T(8,128)(2,1)S(1)} %constant_dynamic-slice_fusion), channel_id=1, source_target_pairs={{0,8},{8,0},{1,9},{9,1},{2,10},{10,2},{3,11},{11,3},{4,12},{12,4},... | collective-permute-start | bytes 2949128 | tf_op jit(solution)/shard_map/ppermute | solution.py:656
  128.2 17.4 %collective-permute-start.11 = (bf16[128,1536]{1,0:T(8,128)(2,1)S(1)}, bf16[128,1536]{1,0:T(8,128)(2,1)S(1)}, u32[]{:S(2)}, u32[]{:S(2)}) collective-permute-start(bf16[128,1536]{1,0:T(8,128)(2,1)S(1)} %collective-permute-done.10.refs_10_.refs_15_), channel_id=1, source_target_pairs={{0,48},{48,0},{16,32},{32,16},{1,49},{49,1},{17,33},{33,17},{2,50}... | collective-permute-start | bytes 1179656 | tf_op jit(solution)/shard_map/ppermute | solution.py:686
  130.0 15.6 %collective-permute-start.12 = (bf16[128,1536]{1,0:T(8,128)(2,1)S(1)}, bf16[128,1536]{1,0:T(8,128)(2,1)S(1)}, u32[]{:S(2)}, u32[]{:S(2)}) collective-permute-start(bf16[128,1536]{1,0:T(8,128)(2,1)S(1)} %collective-permute-done.10.refs_10_.refs_15_), channel_id=1, source_target_pairs={{0,16},{16,0},{32,48},{48,32},{1,17},{17,1},{33,49},{49,33},{2,18}... | collective-permute-start | bytes 1179656 | tf_op jit(solution)/shard_map/ppermute | solution.py:686
  149.9 24.8 %collective-permute-start.13 = (bf16[640,1536]{1,0:T(8,128)(2,1)}, bf16[640,1536]{1,0:T(8,128)(2,1)}, u32[]{:S(2)}, u32[]{:S(2)}) collective-permute-start(bf16[640,1536]{1,0:T(8,128)(2,1)} %bitcast.21.refs_1_), channel_id=1, source_target_pairs={{0,8},{8,0},{1,9},{9,1},{2,10},{10,2},{3,11},{11,3},{4,12},{12,4},... | collective-permute-start | bytes 5898248 | tf_op jit(solution)/shard_map/ppermute | solution.py:656
  163.6 31.6 %all-to-all-start.5 = ((bf16[8,80,1536]{2,1,0:T(8,128)(2,1)}), bf16[8,80,1536]{2,1,0:T(8,128)(2,1)}, u32[]{:S(2)}, u32[]{:S(2)}) async-start(bf16[8,80,1536]{2,1,0:T(8,128)(2,1)} %bitcast.90), calls=%async_computation.5 | async-start | bytes 3932160 | tf_op jit(solution)/shard_map/all_to_all | solution.py:664
  168.5 20.3 %collective-permute-start.16 = (bf16[128,1536]{1,0:T(8,128)(2,1)S(1)}, bf16[128,1536]{1,0:T(8,128)(2,1)S(1)}, u32[]{:S(2)}, u32[]{:S(2)}) collective-permute-start(bf16[128,1536]{1,0:T(8,128)(2,1)S(1)} %collective-permute-done.8.refs_11_.refs_16_), channel_id=1, source_target_pairs={{0,48},{48,0},{16,32},{32,16},{1,49},{49,1},{17,33},{33,17},{2,50}... | collective-permute-start | bytes 1179656 | tf_op jit(solution)/shard_map/ppermute | solution.py:686
  170.4 19.2 %collective-permute-start.17 = (bf16[128,1536]{1,0:T(8,128)(2,1)S(1)}, bf16[128,1536]{1,0:T(8,128)(2,1)}, u32[]{:S(2)}, u32[]{:S(2)}) collective-permute-start(bf16[128,1536]{1,0:T(8,128)(2,1)S(1)} %collective-permute-done.11.refs_14_.refs_19_), channel_id=1, source_target_pairs={{0,16},{16,0},{32,48},{48,32},{1,17},{17,1},{33,49},{49,33},{2,18}... | collective-permute-start | bytes 1179656 | tf_op jit(solution)/shard_map/ppermute | solution.py:686
  207.6 29.1 %all-to-all-start.6 = ((bf16[8,128,512]{2,1,0:T(8,128)(2,1)}), bf16[8,128,512]{2,1,0:T(8,128)(2,1)S(1)}, u32[]{:S(2)}, u32[]{:S(2)}) async-start(bf16[8,128,512]{2,1,0:T(8,128)(2,1)} %bitcast.96), calls=%async_computation.6 | async-start | bytes 2097152 | tf_op jit(solution)/shard_map/all_to_all | solution.py:664
  216.4 28.1 %collective-permute-start.34 = (bf16[2,288,768]{2,1,0:T(8,128)(2,1)}, bf16[2,288,768]{2,1,0:T(8,128)(2,1)}, u32[]{:S(2)}, u32[]{:S(2)}) collective-permute-start(bf16[2,288,768]{2,1,0:T(8,128)(2,1)} %get-tuple-element.200), channel_id=1, source_target_pairs={{0,16},{16,0},{32,48},{48,32},{1,17},{17,1},{33,49},{49,33},{2,18}... | collective-permute-start | bytes 2654216 | tf_op jit(solution)/shard_map/ppermute | solution.py:686
  217.0 27.5 %collective-permute-start.35 = (bf16[2,288,768]{2,1,0:T(8,128)(2,1)}, bf16[2,288,768]{2,1,0:T(8,128)(2,1)}, u32[]{:S(2)}, u32[]{:S(2)}) collective-permute-start(bf16[2,288,768]{2,1,0:T(8,128)(2,1)} %get-tuple-element.202), channel_id=1, source_target_pairs={{0,48},{48,0},{16,32},{32,16},{1,49},{49,1},{17,33},{33,17},{2,50}... | collective-permute-start | bytes 2654216 | tf_op jit(solution)/shard_map/ppermute | solution.py:686
  237.7 40.9 %all-to-all-start.7 = ((bf16[8,80,1536]{2,1,0:T(8,128)(2,1)}), bf16[8,80,1536]{2,1,0:T(8,128)(2,1)S(1)}, u32[]{:S(2)}, u32[]{:S(2)}) async-start(bf16[8,80,1536]{2,1,0:T(8,128)(2,1)} %bitcast.88), calls=%async_computation.7 | async-start | bytes 3932160 | tf_op jit(solution)/shard_map/all_to_all | solution.py:664
  248.4 14.9 %collective-permute-start.36 = (bf16[288,768]{1,0:T(8,128)(2,1)}, bf16[288,768]{1,0:T(8,128)(2,1)S(1)}, u32[]{:S(2)}, u32[]{:S(2)}) collective-permute-start(bf16[288,768]{1,0:T(8,128)(2,1)} %get-tuple-element.204), channel_id=1, source_target_pairs={{0,48},{48,0},{16,32},{32,16},{1,49},{49,1},{17,33},{33,17},{2,50}... | collective-permute-start | bytes 1327112 | tf_op jit(solution)/shard_map/ppermute | solution.py:686
  249.3 14.0 %collective-permute-start.37 = (bf16[288,768]{1,0:T(8,128)(2,1)}, bf16[288,768]{1,0:T(8,128)(2,1)S(1)}, u32[]{:S(2)}, u32[]{:S(2)}) collective-permute-start(bf16[288,768]{1,0:T(8,128)(2,1)} %get-tuple-element.205), channel_id=1, source_target_pairs={{0,16},{16,0},{32,48},{48,32},{1,17},{17,1},{33,49},{49,33},{2,18}... | collective-permute-start | bytes 1327112 | tf_op jit(solution)/shard_map/ppermute | solution.py:686
  267.4 19.7 %collective-permute-start.38 = (bf16[2,288,768]{2,1,0:T(8,128)(2,1)}, bf16[2,288,768]{2,1,0:T(8,128)(2,1)S(1)}, u32[]{:S(2)}, u32[]{:S(2)}) collective-permute-start(bf16[2,288,768]{2,1,0:T(8,128)(2,1)} %shard_map.242.refs_1_), channel_id=1, source_target_pairs={{0,64},{64,0},{1,65},{65,1},{2,66},{66,2},{3,67},{67,3},{4,68},{68... | collective-permute-start | bytes 2654216 | tf_op jit(solution)/shard_map/ppermute | solution.py:660
  278.6 32.7 %all-to-all-start.8 = ((bf16[16,96,512]{2,1,0:T(8,128)(2,1)}), bf16[16,96,512]{2,1,0:T(8,128)(2,1)}, u32[]{:S(2)}, u32[]{:S(2)}) async-start(bf16[16,96,512]{2,1,0:T(8,128)(2,1)} %bitcast.80), calls=%async_computation.8 | async-start | bytes 3145728 | tf_op jit(solution)/shard_map/all_to_all | solution.py:664
  292.1 16.7 %collective-permute-start.40 = (bf16[288,768]{1,0:T(8,128)(2,1)}, bf16[288,768]{1,0:T(8,128)(2,1)}, u32[]{:S(2)}, u32[]{:S(2)}) collective-permute-start(bf16[288,768]{1,0:T(8,128)(2,1)} %get-tuple-element.212.refs_1_), channel_id=1, source_target_pairs={{0,16},{16,0},{32,48},{48,32},{1,17},{17,1},{33,49},{49,33},{2,18}... | collective-permute-start | bytes 1327112 | tf_op jit(solution)/shard_map/ppermute | solution.py:686
  292.1 22.4 %collective-permute-start.43 = (bf16[288,768]{1,0:T(8,128)(2,1)}, bf16[288,768]{1,0:T(8,128)(2,1)}, u32[]{:S(2)}, u32[]{:S(2)}) collective-permute-start(bf16[288,768]{1,0:T(8,128)(2,1)} %get-tuple-element.211.refs_0_), channel_id=1, source_target_pairs={{0,16},{16,0},{32,48},{48,32},{1,17},{17,1},{33,49},{49,33},{2,18}... | collective-permute-start | bytes 1327112 | tf_op jit(solution)/shard_map/ppermute | solution.py:686
  293.5 22.4 %collective-permute-start.44 = (bf16[288,768]{1,0:T(8,128)(2,1)}, bf16[288,768]{1,0:T(8,128)(2,1)}, u32[]{:S(2)}, u32[]{:S(2)}) collective-permute-start(bf16[288,768]{1,0:T(8,128)(2,1)} %get-tuple-element.212.refs_1_), channel_id=1, source_target_pairs={{0,48},{48,0},{16,32},{32,16},{1,49},{49,1},{17,33},{33,17},{2,50}... | collective-permute-start | bytes 1327112 | tf_op jit(solution)/shard_map/ppermute | solution.py:686
  295.4 20.7 %collective-permute-start.45 = (bf16[288,768]{1,0:T(8,128)(2,1)}, bf16[288,768]{1,0:T(8,128)(2,1)S(1)}, u32[]{:S(2)}, u32[]{:S(2)}) collective-permute-start(bf16[288,768]{1,0:T(8,128)(2,1)} %get-tuple-element.211.refs_0_), channel_id=1, source_target_pairs={{0,8},{8,0},{1,9},{9,1},{2,10},{10,2},{3,11},{11,3},{4,12},{12,4},... | collective-permute-start | bytes 1327112 | tf_op jit(solution)/shard_map/ppermute | solution.py:656
  301.4 15.0 %collective-permute-start.46 = (bf16[288,768]{1,0:T(8,128)(2,1)}, bf16[288,768]{1,0:T(8,128)(2,1)S(1)}, u32[]{:S(2)}, u32[]{:S(2)}) collective-permute-start(bf16[288,768]{1,0:T(8,128)(2,1)} %get-tuple-element.212.refs_1_), channel_id=1, source_target_pairs={{0,8},{8,0},{1,9},{9,1},{2,10},{10,2},{3,11},{11,3},{4,12},{12,4},... | collective-permute-start | bytes 1327112 | tf_op jit(solution)/shard_map/ppermute | solution.py:656
  316.5 14.2 %collective-permute-start.41 = (bf16[288,768]{1,0:T(8,128)(2,1)}, bf16[288,768]{1,0:T(8,128)(2,1)S(1)}, u32[]{:S(2)}, u32[]{:S(2)}) collective-permute-start(bf16[288,768]{1,0:T(8,128)(2,1)} %collective-permute-done.39.refs_2_), channel_id=1, source_target_pairs={{0,16},{16,0},{32,48},{48,32},{1,17},{17,1},{33,49},{49,33},{2,18}... | collective-permute-start | bytes 1327112 | tf_op jit(solution)/shard_map/ppermute | solution.py:686
  316.5 17.2 %collective-permute-start.42 = (bf16[288,768]{1,0:T(8,128)(2,1)}, bf16[288,768]{1,0:T(8,128)(2,1)S(1)}, u32[]{:S(2)}, u32[]{:S(2)}) collective-permute-start(bf16[288,768]{1,0:T(8,128)(2,1)} %collective-permute-done.40.refs_3_), channel_id=1, source_target_pairs={{0,48},{48,0},{16,32},{32,16},{1,49},{49,1},{17,33},{33,17},{2,50}... | collective-permute-start | bytes 1327112 | tf_op jit(solution)/shard_map/ppermute | solution.py:686
  317.6 24.6 %all-to-all-start.9 = ((bf16[8,96,512]{2,1,0:T(8,128)(2,1)}), bf16[8,96,512]{2,1,0:T(8,128)(2,1)S(1)}, u32[]{:S(2)}, u32[]{:S(2)}) async-start(bf16[8,96,512]{2,1,0:T(8,128)(2,1)} %shard_map.240), calls=%async_computation.9 | async-start | bytes 1572864 | tf_op jit(solution)/shard_map/all_to_all | solution.py:664
  (93 other events, 671.7 us)

commit v4 on v3

--- a/solution.py
+++ b/solution.py
@@ -170,13 +170,13 @@
     step = count // 2
     for n, low in enumerate(range(0, count, step)):
         at = pl.ds(low, step)
-        block = rows[at, :]
+        block = rows.part(n)[at, :]
         gate = dot(block, gate_w[...])
         up = dot(block, up_w[...])
         sigmoid = 1.0 / (1.0 + jnp.exp(-gate))
         silu = gate * sigmoid
         hidden_o[at, :] = (silu * up).astype(BF)
-        grad = grad_hidden[at, :]
+        grad = grad_hidden.part(n)[at, :]
         grad_gate = (grad * up * (sigmoid * (1.0 + gate * (1.0 - sigmoid)))).astype(BF)
         grad_up = (grad * silu).astype(BF)
         own_o[at, :] = jnp.where(core == 0, grad_gate, grad_up)
@@ -459,7 +459,7 @@
             out[y, f, :, pl.ds(0, size)] = square[pl.ds((f * count + y) * part, part), :]
     for copy in copies:
         copy.wait()
-    total[...] = t_dot(all_left[...], all_grads[...]).astype(BF)
+    total[...] = t_dot(all_grads[...], all_left[...]).T.astype(BF)
     even = place[0] == 0
     for y in range(count):
         for f in range(groups):
@@ -468,10 +468,16 @@
         out.send(y + 1)
 
 
+def sum_parts(parts):
+    half = parts.shape[0] // 2
+    total = parts.part(0)[0].astype(F32)
+    for k in range(1, 2 * half):
+        total = total + parts.part(k // half)[k].astype(F32)
+    return total
+
+
 def sum_kernel(place, parts, out):
-    total = parts[0].astype(F32)
-    for k in range(1, parts.shape[0]):
-        total = total + parts[k].astype(F32)
+    total = sum_parts(parts)
     total = total.astype(BF)
     for k in range(out.shape[0]):
         out[k] = total
@@ -507,9 +513,7 @@
 
 def key_back_kernel(place, parts, cos, sin, pre_o, *sent_o):
     kv_width = parts.shape[-1] // 2
-    total = parts[0].astype(F32)
-    for k in range(1, parts.shape[0]):
-        total = total + parts[k].astype(F32)
+    total = sum_parts(parts)
     for head in range(2 * KV_HEADS):
         low, high = head * HEAD_DIM, (head + 1) * HEAD_DIM
         piece = total[:, low:high]
@@ -549,16 +553,26 @@
 
 
 class Coming:
-    def __init__(self, source, ref, sem):
-        self.copy, self.ref, self.waits = pltpu.make_async_copy(source, ref, sem), ref, True
-        self.shape = ref.shape
-        self.copy.start()
+    def __init__(self, source, ref, sems):
+        self.ref, self.shape, self.left = ref, ref.shape, 0
+        rows = ref.shape[0] // len(sems)
+        self.copies = [
+            pltpu.make_async_copy(
+                source.at[pl.ds(n * rows, rows)], ref.at[pl.ds(n * rows, rows)], sem
+            )
+            for n, sem in enumerate(sems)
+        ]
+        for copy in self.copies:
+            copy.start()
+
+    def part(self, n):
+        for copy in self.copies[self.left : n + 1]:
+            copy.wait()
+        self.left = max(self.left, n + 1)
+        return self.ref
 
     def now(self):
-        if self.waits:
-            self.copy.wait()
-            self.waits = False
-        return self.ref
+        return self.part(len(self.copies) - 1)
 
     def __getitem__(self, index):
         return self.now()[index]
@@ -614,9 +628,12 @@
         own = refs[count + made : count + made + len(scratch)]
         rest = refs[count + made + len(scratch) :]
         landing, leaving, sems = rest[: len(far)], rest[len(far) : len(far) + made], rest[-1]
+        used = 0
         for n, i in enumerate(far):
-            ins[i] = Coming(ins[i], landing[n], sems.at[n])
-        going, used = [], len(far)
+            parts = args[i].parts
+            ins[i] = Coming(ins[i], landing[n], [sems.at[used + k] for k in range(parts)])
+            used += parts
+        going = []
         for out, ref, target in zip(outs, leaving, results):
             going.append(
                 Going(ref, target, [sems.at[used + n] for n in range(out.parts)], out.parts)
@@ -643,7 +660,7 @@
             *scratch,
             *[pltpu.VMEM(values[i].shape, values[i].dtype) for i in far],
             *[pltpu.VMEM(out.value, out.kind) for out in outs],
-            pltpu.SemaphoreType.DMA((len(far) + sum(out.parts for out in outs),)),
+            pltpu.SemaphoreType.DMA((sum(args[i].parts for i in far) + sum(out.parts for out in outs),)),
         ],
         compiler_params=pltpu.CompilerParams(vmem_limit_bytes=56 * 1024 * 1024),
         cost_estimate=pl.CostEstimate(
@@ -835,7 +852,7 @@
     arrived_other = swap(arrived)
     hidden, own_pre, sent_pre, grad_rows = call(
         expert_kernel,
-        [place_at, Far(arrived), Far(grad_hidden), gate_weight[0], up_weight[0]],
+        [place_at, Far(arrived, parts=2), Far(grad_hidden, parts=2), gate_weight[0], up_weight[0]],
         [Far((slots_all, half), BF, 2)] * 3 + [Far((slots_all, width), BF, 2)],
     )
     back_rows = exchange(grad_rows, "fsdp")
@@ -892,7 +909,7 @@
     returned = exchange(expert_out, "fsdp")
     grad_kv_pre, *kv_sent = call(
         key_back_kernel,
-        [place_at, Far(kv_got.reshape(groups, tok, 2 * kv_width)), cosine, sine],
+        [place_at, Far(kv_got.reshape(groups, tok, 2 * kv_width), parts=2), cosine, sine],
         [((tok, 2 * kv_width), BF)] + [((tok, 2 * kv_width // XS), BF)] * XS,
     )
     kv_set = fan(kv_sent)
@@ -935,7 +952,7 @@
     mixture = t_dot(gate_high, returned) + t_dot(gate_low, returned)
     outputs = (residual + mixture).astype(BF)
     packed, outputs = tie(packed, outputs)
-    packed = call(sum_kernel, [place_at, Far(packed)], [((YLO * XS, part, packed_width), BF)])[0]
+    packed = call(sum_kernel, [place_at, Far(packed, parts=2)], [((YLO * XS, part, packed_width), BF)])[0]
     spreaded = exchange(packed, ("ylo", "x"))
     most = [e_zero_a, e_zero_b, e_one_a, e_one_b, e_two_a, e_two_b]
     *e_grads, most_mark = expert_outputs(

time: 356 us -> 355 us (level)
  waiting for transfers between devices: 70.4 us -> 66.4 us
    ppermute x24, waiting for transfers between devices: 25.1 us -> 21.4 us  [flip(): return lax.ppermute(v, 'x', pairs)]
  transfers between devices with their start and end apart: 64 -> 64, of which waited for: 29 -> 27; matrix products, arithmetic and copies ran while one was open for 11% -> 11% of each run, Pallas kernels for 26% -> 26%
where the time goes in v4:
time: 355 us; the launch traced here: 348 us
  starting transfers between devices  121 us (34%)
  Pallas kernels  106 us (30%)
  waiting for transfers between devices  66.4 us (19%)
  local copies, waits for them, and re-layouts  29.8 us (8%)
  matrix products  12.5 us (4%)
  other arithmetic  10.9 us (3%)
    pallas_call x15, Pallas kernels, call(): pl.pallas_call(whole, out_shape=[jax.ShapeDtypeStruct(out.value, out.kind...  94.4 us
    all_to_all x10, starting transfers between devices, exchange(): return lax.all_to_all(v, axis, 0, 0, tiled=True)  54.9 us
    ppermute x29, starting transfers between devices, swap(): return lax.ppermute(v, 'core', [(0, 1), (1, 0)])  41.1 us
    all_to_all x10, waiting for transfers between devices, exchange(): return lax.all_to_all(v, axis, 0, 0, tiled=True)  36.1 us
    ppermute x24, starting transfers between devices, flip(): return lax.ppermute(v, 'x', pairs)  24.5 us
    ppermute x24, waiting for transfers between devices, flip(): return lax.ppermute(v, 'x', pairs)  21.4 us
    unnamed x128, local copies, waits for them, and re-layouts  12.7 us
    pallas_call x2, Pallas kernels, expert_outputs(): pl.pallas_call(kernel, out_shape=shapes, in_specs=[pl.BlockSpec(memory_sp...  11.4 us
  transfers between devices with their start and end apart: 64, of which 27 were waited for; matrix products, arithmetic and copies ran while one was open for 11% of the time, Pallas kernels for 26%

profile of v4, /device:TPU:1, one launch (start us, length us, event | category | flops | bytes accessed | tf_op | source)
XLA Modules:
  0.0 348.4 jit_solution(8845310468150932456)
XLA Ops:
  4.2 8.6 %all-to-all-start = ((bf16[8,40,1536]{2,1,0:T(8,128)(2,1)}), bf16[8,40,1536]{2,1,0:T(8,128)(2,1)S(1)}, u32[]{:S(2)}, u32[]{:S(2)}) async-start(bf16[8,40,1536]{2,1,0:T(8,128)(2,1)} %broadcast_in_dim.91), calls=%async_computation | async-start | bytes 1966080 | tf_op jit(solution)/shard_map/all_to_all | solution.py:681
  18.0 10.1 %all-to-all-done = bf16[8,40,1536]{2,1,0:T(8,128)(2,1)S(1)} async-done(((bf16[8,40,1536]{2,1,0:T(8,128)(2,1)}), bf16[8,40,1536]{2,1,0:T(8,128)(2,1)S(1)}, u32[]{:S(2)}, u32[]{:S(2)}) %all-to-all-start) | async-done | bytes 983072 | tf_op jit(solution)/shard_map/all_to_all | solution.py:681
  28.1 4.4 %all-to-all-start.1 = ((bf16[8,96,1536]{2,1,0:T(8,128)(2,1)}), bf16[8,96,1536]{2,1,0:T(8,128)(2,1)}, u32[]{:S(2)}, u32[]{:S(2)}) async-start(bf16[8,96,1536]{2,1,0:T(8,128)(2,1)} %broadcast_in_dim.92), calls=%async_computation.1 | async-start | bytes 4718592 | tf_op jit(solution)/shard_map/all_to_all | solution.py:681
  49.7 4.0 %shard_map.230 = (bf16[128,1536]{1,0:T(8,128)(2,1)}, f32[128,128]{1,0:T(8,128)}, bf16[8,128,512]{2,1,0:T(8,128)(2,1)}, bf16[1536,512]{1,0:T(8,128)(2,1)}) custom-call(s32[4]{0:T(128)} %pad_add_fusion.refs_0_.place, bf16[128,1536]{1,0:T(8,128)(2,1)} %bitcast.92, f32[1,1536]{1,0:T(1,128)} %reshape.223.refs_2_.refs_5_, bf16[8,32,1536]{2,1,0:T(8,128)(2,1)} %slice.49.refs_3_, ...), custom_call_target="tpu_custom_call" | custom-call | tf_op jit(solution)/shard_map/pallas_call | solution.py:654
  53.7 7.9 %all-to-all-done.1 = bf16[8,96,1536]{2,1,0:T(8,128)(2,1)} async-done(((bf16[8,96,1536]{2,1,0:T(8,128)(2,1)}), bf16[8,96,1536]{2,1,0:T(8,128)(2,1)}, u32[]{:S(2)}, u32[]{:S(2)}) %all-to-all-start.1) | async-done | bytes 2359328 | tf_op jit(solution)/shard_map/all_to_all | solution.py:681
  61.6 5.0 %all-to-all-start.2 = ((bf16[8,128,512]{2,1,0:T(8,128)(2,1)}), bf16[8,128,512]{2,1,0:T(8,128)(2,1)S(1)}, u32[]{:S(2)}, u32[]{:S(2)}) async-start(bf16[8,128,512]{2,1,0:T(8,128)(2,1)} %get-tuple-element.132), calls=%async_computation.2 | async-start | bytes 2097152 | tf_op jit(solution)/shard_map/all_to_all | solution.py:681
  72.8 9.1 %all-to-all-done.2 = bf16[8,128,512]{2,1,0:T(8,128)(2,1)S(1)} async-done(((bf16[8,128,512]{2,1,0:T(8,128)(2,1)}), bf16[8,128,512]{2,1,0:T(8,128)(2,1)S(1)}, u32[]{:S(2)}, u32[]{:S(2)}) %all-to-all-start.2) | async-done | bytes 1048608 | tf_op jit(solution)/shard_map/all_to_all | solution.py:681
  82.9 4.3 %all-to-all-start.3 = ((bf16[8,80,1536]{2,1,0:T(8,128)(2,1)}), bf16[8,80,1536]{2,1,0:T(8,128)(2,1)}, u32[]{:S(2)}, u32[]{:S(2)}) async-start(bf16[8,80,1536]{2,1,0:T(8,128)(2,1)} %bitcast.79), calls=%async_computation.3 | async-start | bytes 3932160 | tf_op jit(solution)/shard_map/all_to_all | solution.py:681
  90.3 5.6 %collective-permute-done.1.refs_10_ = bf16[8,96,768]{2,1,0:T(8,128)(2,1)} collective-permute-done((bf16[8,96,768]{2,1,0:T(8,128)(2,1)}, bf16[8,96,768]{2,1,0:T(8,128)(2,1)}, u32[]{:S(2)}, u32[]{:S(2)}) %collective-permute-start.1) | collective-permute-done | bytes 1179680 | tf_op jit(solution)/shard_map/ppermute | solution.py:703
  104.0 12.6 %shard_map.231 = (bf16[8,192,1536]{2,1,0:T(8,128)(2,1)}, bf16[8,192,1536]{2,1,0:T(8,128)(2,1)}, bf16[128,1536]{1,0:T(8,128)(2,1)}, bf16[128,1536]{1,0:T(8,128)(2...) custom-call(s32[4]{0:T(128)} %pad_add_fusion.refs_0_.place, ...), custom_call_target="tpu_custom_call" | custom-call | tf_op jit(solution)/shard_map/pallas_call | solution.py:654
  116.6 6.7 %all-to-all-start.4 = ((bf16[8,80,1536]{2,1,0:T(8,128)(2,1)}), bf16[8,80,1536]{2,1,0:T(8,128)(2,1)}, u32[]{:S(2)}, u32[]{:S(2)}) async-start(bf16[8,80,1536]{2,1,0:T(8,128)(2,1)} %bitcast.89), calls=%async_computation.4 | async-start | bytes 3932160 | tf_op jit(solution)/shard_map/all_to_all | solution.py:681
  130.0 4.6 %fusion.3.refs_2_ = f32[640,768]{1,0:T(8,128)} fusion(bf16[640,1536]{1,0:T(8,128)(2,1)} %bitcast.19.refs_7_, bf16[1,768,1536]{2,1,0:T(8,128)(2,1)S(1)} %copy-done), kind=kOutput, calls=%fused_computation.6 | convolution fusion | flops 1509949440 | bytes 6291456 | tf_op jit(solution)/shard_map/dot_general | solution.py:41
  137.1 8.4 %collective-permute-done.11.refs_14_.refs_19_ = bf16[128,1536]{1,0:T(8,128)(2,1)S(1)} collective-permute-done((bf16[128,1536]{1,0:T(8,128)(2,1)S(1)}, bf16[128,1536]{1,0:T(8,128)(2,1)S(1)}, u32[]{:S(2)}, u32[]{:S(2)}) %collective-permute-start.11) | collective-permute-done | bytes 393248 | tf_op jit(solution)/shard_map/ppermute | solution.py:703
  151.9 11.6 %shard_map.232 = (bf16[640,768]{1,0:T(8,128)(2,1)}, bf16[640,768]{1,0:T(8,128)(2,1)}, bf16[640,768]{1,0:T(8,128)(2,1)}, bf16[640,1536]{1,0:T(8,128)(2,1)}) custom-call(s32[4]{0:T(128)} %pad_add_fusion.refs_0_.place, bf16[640,1536]{1,0:T(8,128)(2,1)} %bitcast.21.refs_1_, f32[640,768]{1,0:T(8,128)} %fusion.3.refs_2_, bf16[1536,768]{1,0:T(8,128)(2,1)} %bitcast.86, ...), custom_call_target="tpu_custom_call" | custom-call | tf_op jit(solution)/shard_map/pallas_call | solution.py:654
  163.5 4.4 %all-to-all-start.5 = ((bf16[8,80,1536]{2,1,0:T(8,128)(2,1)}), bf16[8,80,1536]{2,1,0:T(8,128)(2,1)}, u32[]{:S(2)}, u32[]{:S(2)}) async-start(bf16[8,80,1536]{2,1,0:T(8,128)(2,1)} %bitcast.90), calls=%async_computation.5 | async-start | bytes 3932160 | tf_op jit(solution)/shard_map/all_to_all | solution.py:681
  170.5 4.1 %convolution_convert_fusion = bf16[640,1536]{1,0:T(8,128)(2,1)} fusion(bf16[640,768]{1,0:T(8,128)(2,1)} %get-tuple-element.145.refs_5_, bf16[1,768,1536]{2,1,0:T(8,128)(2,1)S(1)} %copy-done), kind=kOutput, calls=%fused_computation.1 | convolution fusion | flops 1510932480 | bytes 5308416 | tf_op jit(solution)/shard_map/dot_general | solution.py:37
  175.9 12.9 %shard_map.233 = (bf16[2,288,768]{2,1,0:T(8,128)(2,1)}, bf16[2,288,768]{2,1,0:T(8,128)(2,1)}, bf16[2,288,768]{2,1,0:T(8,128)(2,1)}, bf16[2,288,768]{2,1,0:T(8,128)(2,1)}) custom-call(s32[4]{0:T(128)} %pad_add_fusion.refs_0_.place, bf16[640,1536]{1,0:T(8,128)(2,1)} %bitcast.21.refs_1_, bf16[640,1536]{1,0:T(8,128)(2,1)} %collective-permute-done.13.refs_2_, ...), custom_call_target="tpu_custom_call" | custom-call | tf_op jit(solution)/shard_map/pallas_call | solution.py:654
  189.6 5.5 %all-to-all-done.5 = bf16[8,80,1536]{2,1,0:T(8,128)(2,1)} async-done(((bf16[8,80,1536]{2,1,0:T(8,128)(2,1)}), bf16[8,80,1536]{2,1,0:T(8,128)(2,1)}, u32[]{:S(2)}, u32[]{:S(2)}) %all-to-all-start.5) | async-done | bytes 1966112 | tf_op jit(solution)/shard_map/all_to_all | solution.py:681
  195.1 12.4 %shard_map.234 = (f32[128,1536]{1,0:T(8,128)}, bf16[128,1536]{1,0:T(8,128)(2,1)}, f32[8,2,128]{2,1,0:T(2,128)}, bf16[128,1536]{1,0:T(8,128)(2,1)}, bf16[1024,512...) custom-call(s32[4]{0:T(128)} %pad_add_fusion.refs_0_.place, ...), custom_call_target="tpu_custom_call" | custom-call | tf_op jit(solution)/shard_map/pallas_call | solution.py:654
  218.8 5.7 %shard_map.235.refs_1_ = f32[128,1536]{1,0:T(8,128)} custom-call(s32[4]{0:T(128)} %pad_add_fusion.refs_0_.place, bf16[128,1536]{1,0:T(8,128)(2,1)} %get-tuple-element.165.refs_1_, bf16[1536,1536]{1,0:T(8,128)(2,1)} %bitcast.82), custom_call_target="tpu_custom_call" | custom-call | tf_op jit(solution)/shard_map/pallas_call | solution.py:654
  230.8 5.9 %shard_map.236.refs_1_ = bf16[1536,384]{1,0:T(8,128)(2,1)} custom-call(s32[4]{0:T(128)} %pad_add_fusion.refs_0_.place, bf16[128,768]{1,0:T(8,128)(2,1)} %get-tuple-element.161.refs_1_, bf16[128,768]{1,0:T(8,128)(2,1)} %copy-done.35, bf16[128,768]{1,0:T(8,128)(2,1)} %copy-done.36, bf16[128,768]{1,0:T(8,128)(2,1)} %copy-done.37, bf16[128,768]{1,0:T(8,128)(2,1)} %copy-done.38, ...), custom_call_target="tpu_custom_call" | custom-call | tf_op jit(solution)/shard_map/pallas_call | solution.py:654
  237.6 6.8 %all-to-all-start.7 = ((bf16[8,80,1536]{2,1,0:T(8,128)(2,1)}), bf16[8,80,1536]{2,1,0:T(8,128)(2,1)S(1)}, u32[]{:S(2)}, u32[]{:S(2)}) async-start(bf16[8,80,1536]{2,1,0:T(8,128)(2,1)} %bitcast.88), calls=%async_computation.7 | async-start | bytes 3932160 | tf_op jit(solution)/shard_map/all_to_all | solution.py:681
  244.4 3.9 %shard_map.241 = (bf16[288,768]{1,0:T(8,128)(2,1)}, bf16[288,768]{1,0:T(8,128)(2,1)}, bf16[288,768]{1,0:T(8,128)(2,1)}, bf16[288,768]{1,0:T(8,128)(2,1)}) custom-call(s32[4]{0:T(128)} %pad_add_fusion.refs_0_.place, bf16[2,288,768]{2,1,0:T(8,128)(2,1)} %get-tuple-element.199.refs_1_, bf16[2,288,768]{2,1,0:T(8,128)(2,1)} %collective-permute-done.34.refs_2_, ...), custom_call_target="tpu_custom_call" | custom-call | tf_op jit(solution)/shard_map/pallas_call | solution.py:654
  255.6 4.5 %shard_map.238 = (bf16[128,1536]{1,0:T(8,128)(2,1)}, f32[8,2,128]{2,1,0:T(2,128)}, f32[8,128]{1,0:T(8,128)}) custom-call(s32[4]{0:T(128)} %pad_add_fusion.refs_0_.place, f32[128,1536]{1,0:T(8,128)} %shard_map.235.refs_1_, bf16[128,512]{1,0:T(8,128)(2,1)} %get-tuple-element.177.refs_2_, bf16[128,1536]{1,0:T(8,128)(2,1)} %bitcast.94, ...), custom_call_target="tpu_custom_call" | custom-call | flops 6000000000 | tf_op jit(solution)/shard_map/pallas_call | solution.py:654
  273.1 5.1 %shard_map.239 = bf16[2,8,96,512]{3,2,1,0:T(8,128)(2,1)} custom-call(s32[4]{0:T(128)} %pad_add_fusion.refs_0_.place, bf16[1536,384]{1,0:T(8,128)(2,1)} %shard_map.236.refs_1_, f32[8,2,128]{2,1,0:T(2,128)} %get-tuple-element.181.refs_2_, f32[8,2,128]{2,1,0:T(2,128)} %copy-done.54, f32[8,2,128]{2,1,0:T(2,128)} %get-tuple-element.182.refs_4_, ...), custom_call_target="tpu_custom_call" | custom-call | tf_op jit(solution)/shard_map/pallas_call | solution.py:654
  278.2 7.5 %all-to-all-start.8 = ((bf16[16,96,512]{2,1,0:T(8,128)(2,1)}), bf16[16,96,512]{2,1,0:T(8,128)(2,1)}, u32[]{:S(2)}, u32[]{:S(2)}) async-start(bf16[16,96,512]{2,1,0:T(8,128)(2,1)} %bitcast.80), calls=%async_computation.8 | async-start | bytes 3145728 | tf_op jit(solution)/shard_map/all_to_all | solution.py:681
  295.3 4.5 %collective-permute-start.45 = (bf16[288,768]{1,0:T(8,128)(2,1)}, bf16[288,768]{1,0:T(8,128)(2,1)S(1)}, u32[]{:S(2)}, u32[]{:S(2)}) collective-permute-start(bf16[288,768]{1,0:T(8,128)(2,1)} %get-tuple-element.211.refs_0_), channel_id=1, source_target_pairs={{0,8},{8,0},{1,9},{9,1},{2,10},{10,2},{3,11},{11,3},{4,12},{12,4},... | collective-permute-start | bytes 1327112 | tf_op jit(solution)/shard_map/ppermute | solution.py:673
  301.0 8.1 %collective-permute-start.46 = (bf16[288,768]{1,0:T(8,128)(2,1)}, bf16[288,768]{1,0:T(8,128)(2,1)S(1)}, u32[]{:S(2)}, u32[]{:S(2)}) collective-permute-start(bf16[288,768]{1,0:T(8,128)(2,1)} %get-tuple-element.212.refs_1_), channel_id=1, source_target_pairs={{0,8},{8,0},{1,9},{9,1},{2,10},{10,2},{3,11},{11,3},{4,12},{12,4},... | collective-permute-start | bytes 1327112 | tf_op jit(solution)/shard_map/ppermute | solution.py:673
  322.2 7.3 %shard_map.244 = (f32[1536,768]{1,0:T(8,128)}, f32[1536,768]{1,0:T(8,128)}, f32[768,1536]{1,0:T(8,128)}, f32[8,128]{1,0:T(8,128)}) custom-call(s32[4]{0:T(128)} %pad_add_fusion.refs_0_.place, bf16[288,768]{1,0:T(8,128)(2,1)} %get-tuple-element.211.refs_0_, bf16[288,768]{1,0:T(8,128)(2,1)} %get-tuple-element.212.refs_1_, ...), custom_call_target="tpu_custom_call" | custom-call | tf_op jit(solution)/shard_map/pallas_call | solution.py:325
  330.2 3.8 %collective-permute-start.51 = (bf16[288,768]{1,0:T(8,128)(2,1)S(1)}, bf16[288,768]{1,0:T(8,128)(2,1)S(1)}, u32[]{:S(2)}, u32[]{:S(2)}) collective-permute-start(bf16[288,768]{1,0:T(8,128)(2,1)S(1)} %collective-permute-done.41.refs_0_), channel_id=1, source_target_pairs={{0,8},{8,0},{1,9},{9,1},{2,10},{10,2},{3,11},{11,3},{4,12},{12,4},... | collective-permute-start | bytes 1327112 | tf_op jit(solution)/shard_map/ppermute | solution.py:673
  336.8 4.1 %shard_map.245 = (f32[1536,768]{1,0:T(8,128)}, f32[1536,768]{1,0:T(8,128)}, f32[768,1536]{1,0:T(8,128)}, f32[8,128]{1,0:T(8,128)}) custom-call(s32[4]{0:T(128)} %pad_add_fusion.refs_0_.place, bf16[288,768]{1,0:T(8,128)(2,1)} %copy-done.24, bf16[288,768]{1,0:T(8,128)(2,1)} %copy-done.26, ...), custom_call_target="tpu_custom_call", output_to_operand_aliasing={{0}: (7, {}), {1}: (8, {}), {2}: (9, {})} | custom-call | tf_op jit(solution)/shard_map/pallas_call | solution.py:325
  344.2 3.7 %shard_map.246 = (f32[192,1536]{1,0:T(8,128)}, f32[192,1536]{1,0:T(8,128)}, f32[192,256]{1,0:T(8,128)}, f32[192,256]{1,0:T(8,128)}, f32[1,192]{1,0:T(1,128)}, /*index=5*/f32[1,192]{1,0:T(1,128)}) custom-call(s32[4]{0:T(128)} %pad_add_fusion.refs_0_.place, bf16[8,96,512]{2,1,0:T(8,128)(2,1)} %copy-done.5, bf16[8,96,512]{2,1,0:T(8,128)(2,1)} %copy-done.19, ...), custom_call_target="tpu_custom_call" | custom-call | tf_op jit(solution)/shard_map/pallas_call | solution.py:654
  (295 shorter events, 133.3 us)
Async XLA Ops:
  4.2 23.9 %all-to-all-start = ((bf16[8,40,1536]{2,1,0:T(8,128)(2,1)}), bf16[8,40,1536]{2,1,0:T(8,128)(2,1)S(1)}, u32[]{:S(2)}, u32[]{:S(2)}) async-start(bf16[8,40,1536]{2,1,0:T(8,128)(2,1)} %broadcast_in_dim.91), calls=%async_computation | async-start | bytes 1966080 | tf_op jit(solution)/shard_map/all_to_all | solution.py:681
  28.1 33.5 %all-to-all-start.1 = ((bf16[8,96,1536]{2,1,0:T(8,128)(2,1)}), bf16[8,96,1536]{2,1,0:T(8,128)(2,1)}, u32[]{:S(2)}, u32[]{:S(2)}) async-start(bf16[8,96,1536]{2,1,0:T(8,128)(2,1)} %broadcast_in_dim.92), calls=%async_computation.1 | async-start | bytes 4718592 | tf_op jit(solution)/shard_map/all_to_all | solution.py:681
  36.2 13.5 %collective-permute-start = (bf16[8,32,1536]{2,1,0:T(8,128)(2,1)}, bf16[8,32,1536]{2,1,0:T(8,128)(2,1)}, u32[]{:S(2)}, u32[]{:S(2)}) collective-permute-start(bf16[8,32,1536]{2,1,0:T(8,128)(2,1)} %slice.49.refs_3_), channel_id=1, source_target_pairs={{0,8},{8,0},{1,9},{9,1},{2,10},{10,2},{3,11},{11,3},{4,12},{12,4},... | collective-permute-start | bytes 2359304 | tf_op jit(solution)/shard_map/ppermute | solution.py:673
  61.6 20.3 %all-to-all-start.2 = ((bf16[8,128,512]{2,1,0:T(8,128)(2,1)}), bf16[8,128,512]{2,1,0:T(8,128)(2,1)S(1)}, u32[]{:S(2)}, u32[]{:S(2)}) async-start(bf16[8,128,512]{2,1,0:T(8,128)(2,1)} %get-tuple-element.132), calls=%async_computation.2 | async-start | bytes 2097152 | tf_op jit(solution)/shard_map/all_to_all | solution.py:681
  69.8 26.1 %collective-permute-start.1 = (bf16[8,96,768]{2,1,0:T(8,128)(2,1)}, bf16[8,96,768]{2,1,0:T(8,128)(2,1)}, u32[]{:S(2)}, u32[]{:S(2)}) collective-permute-start(bf16[8,96,768]{2,1,0:T(8,128)(2,1)} %get-tuple-element.238.refs_9_), channel_id=1, source_target_pairs={{0,16},{16,0},{32,48},{48,32},{1,17},{17,1},{33,49},{49,33},{2,18}... | collective-permute-start | bytes 3538952 | tf_op jit(solution)/shard_map/ppermute | solution.py:703
  71.0 27.5 %collective-permute-start.4 = (bf16[8,96,768]{2,1,0:T(8,128)(2,1)}, bf16[8,96,768]{2,1,0:T(8,128)(2,1)}, u32[]{:S(2)}, u32[]{:S(2)}) collective-permute-start(bf16[8,96,768]{2,1,0:T(8,128)(2,1)} %get-tuple-element.237.refs_13_), channel_id=1, source_target_pairs={{0,48},{48,0},{16,32},{32,16},{1,49},{49,1},{17,33},{33,17},{2,50}... | collective-permute-start | bytes 3538952 | tf_op jit(solution)/shard_map/ppermute | solution.py:703
  82.9 33.7 %all-to-all-start.3 = ((bf16[8,80,1536]{2,1,0:T(8,128)(2,1)}), bf16[8,80,1536]{2,1,0:T(8,128)(2,1)}, u32[]{:S(2)}, u32[]{:S(2)}) async-start(bf16[8,80,1536]{2,1,0:T(8,128)(2,1)} %bitcast.79), calls=%async_computation.3 | async-start | bytes 3932160 | tf_op jit(solution)/shard_map/all_to_all | solution.py:681
  87.3 14.6 %collective-permute-start.2 = (bf16[8,96,768]{2,1,0:T(8,128)(2,1)}, bf16[8,96,768]{2,1,0:T(8,128)(2,1)S(1)}, u32[]{:S(2)}, u32[]{:S(2)}) collective-permute-start(bf16[8,96,768]{2,1,0:T(8,128)(2,1)} %get-tuple-element.238.refs_9_), channel_id=1, source_target_pairs={{0,8},{8,0},{1,9},{9,1},{2,10},{10,2},{3,11},{11,3},{4,12},{12,4},... | collective-permute-start | bytes 3538952 | tf_op jit(solution)/shard_map/ppermute | solution.py:673
  116.6 33.2 %all-to-all-start.4 = ((bf16[8,80,1536]{2,1,0:T(8,128)(2,1)}), bf16[8,80,1536]{2,1,0:T(8,128)(2,1)}, u32[]{:S(2)}, u32[]{:S(2)}) async-start(bf16[8,80,1536]{2,1,0:T(8,128)(2,1)} %bitcast.89), calls=%async_computation.4 | async-start | bytes 3932160 | tf_op jit(solution)/shard_map/all_to_all | solution.py:681
  124.7 21.7 %collective-permute-start.7 = (bf16[640,768]{1,0:T(8,128)(2,1)S(1)}, bf16[640,768]{1,0:T(8,128)(2,1)}, u32[]{:S(2)}, u32[]{:S(2)}) collective-permute-start(bf16[640,768]{1,0:T(8,128)(2,1)S(1)} %constant_dynamic-slice_fusion), channel_id=1, source_target_pairs={{0,8},{8,0},{1,9},{9,1},{2,10},{10,2},{3,11},{11,3},{4,12},{12,4},... | collective-permute-start | bytes 2949128 | tf_op jit(solution)/shard_map/ppermute | solution.py:673
  128.2 17.4 %collective-permute-start.11 = (bf16[128,1536]{1,0:T(8,128)(2,1)S(1)}, bf16[128,1536]{1,0:T(8,128)(2,1)S(1)}, u32[]{:S(2)}, u32[]{:S(2)}) collective-permute-start(bf16[128,1536]{1,0:T(8,128)(2,1)S(1)} %collective-permute-done.10.refs_10_.refs_15_), channel_id=1, source_target_pairs={{0,48},{48,0},{16,32},{32,16},{1,49},{49,1},{17,33},{33,17},{2,50}... | collective-permute-start | bytes 1179656 | tf_op jit(solution)/shard_map/ppermute | solution.py:703
  130.0 15.6 %collective-permute-start.12 = (bf16[128,1536]{1,0:T(8,128)(2,1)S(1)}, bf16[128,1536]{1,0:T(8,128)(2,1)S(1)}, u32[]{:S(2)}, u32[]{:S(2)}) collective-permute-start(bf16[128,1536]{1,0:T(8,128)(2,1)S(1)} %collective-permute-done.10.refs_10_.refs_15_), channel_id=1, source_target_pairs={{0,16},{16,0},{32,48},{48,32},{1,17},{17,1},{33,49},{49,33},{2,18}... | collective-permute-start | bytes 1179656 | tf_op jit(solution)/shard_map/ppermute | solution.py:703
  149.9 24.8 %collective-permute-start.13 = (bf16[640,1536]{1,0:T(8,128)(2,1)}, bf16[640,1536]{1,0:T(8,128)(2,1)}, u32[]{:S(2)}, u32[]{:S(2)}) collective-permute-start(bf16[640,1536]{1,0:T(8,128)(2,1)} %bitcast.21.refs_1_), channel_id=1, source_target_pairs={{0,8},{8,0},{1,9},{9,1},{2,10},{10,2},{3,11},{11,3},{4,12},{12,4},... | collective-permute-start | bytes 5898248 | tf_op jit(solution)/shard_map/ppermute | solution.py:673
  163.5 31.6 %all-to-all-start.5 = ((bf16[8,80,1536]{2,1,0:T(8,128)(2,1)}), bf16[8,80,1536]{2,1,0:T(8,128)(2,1)}, u32[]{:S(2)}, u32[]{:S(2)}) async-start(bf16[8,80,1536]{2,1,0:T(8,128)(2,1)} %bitcast.90), calls=%async_computation.5 | async-start | bytes 3932160 | tf_op jit(solution)/shard_map/all_to_all | solution.py:681
  168.5 20.3 %collective-permute-start.16 = (bf16[128,1536]{1,0:T(8,128)(2,1)S(1)}, bf16[128,1536]{1,0:T(8,128)(2,1)S(1)}, u32[]{:S(2)}, u32[]{:S(2)}) collective-permute-start(bf16[128,1536]{1,0:T(8,128)(2,1)S(1)} %collective-permute-done.8.refs_11_.refs_16_), channel_id=1, source_target_pairs={{0,48},{48,0},{16,32},{32,16},{1,49},{49,1},{17,33},{33,17},{2,50}... | collective-permute-start | bytes 1179656 | tf_op jit(solution)/shard_map/ppermute | solution.py:703
  170.3 19.2 %collective-permute-start.17 = (bf16[128,1536]{1,0:T(8,128)(2,1)S(1)}, bf16[128,1536]{1,0:T(8,128)(2,1)}, u32[]{:S(2)}, u32[]{:S(2)}) collective-permute-start(bf16[128,1536]{1,0:T(8,128)(2,1)S(1)} %collective-permute-done.11.refs_14_.refs_19_), channel_id=1, source_target_pairs={{0,16},{16,0},{32,48},{48,32},{1,17},{17,1},{33,49},{49,33},{2,18}... | collective-permute-start | bytes 1179656 | tf_op jit(solution)/shard_map/ppermute | solution.py:703
  207.6 29.1 %all-to-all-start.6 = ((bf16[8,128,512]{2,1,0:T(8,128)(2,1)}), bf16[8,128,512]{2,1,0:T(8,128)(2,1)S(1)}, u32[]{:S(2)}, u32[]{:S(2)}) async-start(bf16[8,128,512]{2,1,0:T(8,128)(2,1)} %bitcast.96), calls=%async_computation.6 | async-start | bytes 2097152 | tf_op jit(solution)/shard_map/all_to_all | solution.py:681
  216.3 28.1 %collective-permute-start.34 = (bf16[2,288,768]{2,1,0:T(8,128)(2,1)}, bf16[2,288,768]{2,1,0:T(8,128)(2,1)}, u32[]{:S(2)}, u32[]{:S(2)}) collective-permute-start(bf16[2,288,768]{2,1,0:T(8,128)(2,1)} %get-tuple-element.200), channel_id=1, source_target_pairs={{0,16},{16,0},{32,48},{48,32},{1,17},{17,1},{33,49},{49,33},{2,18}... | collective-permute-start | bytes 2654216 | tf_op jit(solution)/shard_map/ppermute | solution.py:703
  216.9 27.5 %collective-permute-start.35 = (bf16[2,288,768]{2,1,0:T(8,128)(2,1)}, bf16[2,288,768]{2,1,0:T(8,128)(2,1)}, u32[]{:S(2)}, u32[]{:S(2)}) collective-permute-start(bf16[2,288,768]{2,1,0:T(8,128)(2,1)} %get-tuple-element.202), channel_id=1, source_target_pairs={{0,48},{48,0},{16,32},{32,16},{1,49},{49,1},{17,33},{33,17},{2,50}... | collective-permute-start | bytes 2654216 | tf_op jit(solution)/shard_map/ppermute | solution.py:703
  237.6 40.6 %all-to-all-start.7 = ((bf16[8,80,1536]{2,1,0:T(8,128)(2,1)}), bf16[8,80,1536]{2,1,0:T(8,128)(2,1)S(1)}, u32[]{:S(2)}, u32[]{:S(2)}) async-start(bf16[8,80,1536]{2,1,0:T(8,128)(2,1)} %bitcast.88), calls=%async_computation.7 | async-start | bytes 3932160 | tf_op jit(solution)/shard_map/all_to_all | solution.py:681
  248.3 14.9 %collective-permute-start.36 = (bf16[288,768]{1,0:T(8,128)(2,1)}, bf16[288,768]{1,0:T(8,128)(2,1)S(1)}, u32[]{:S(2)}, u32[]{:S(2)}) collective-permute-start(bf16[288,768]{1,0:T(8,128)(2,1)} %get-tuple-element.204), channel_id=1, source_target_pairs={{0,48},{48,0},{16,32},{32,16},{1,49},{49,1},{17,33},{33,17},{2,50}... | collective-permute-start | bytes 1327112 | tf_op jit(solution)/shard_map/ppermute | solution.py:703
  249.3 14.0 %collective-permute-start.37 = (bf16[288,768]{1,0:T(8,128)(2,1)}, bf16[288,768]{1,0:T(8,128)(2,1)S(1)}, u32[]{:S(2)}, u32[]{:S(2)}) collective-permute-start(bf16[288,768]{1,0:T(8,128)(2,1)} %get-tuple-element.205), channel_id=1, source_target_pairs={{0,16},{16,0},{32,48},{48,32},{1,17},{17,1},{33,49},{49,33},{2,18}... | collective-permute-start | bytes 1327112 | tf_op jit(solution)/shard_map/ppermute | solution.py:703
  267.3 19.7 %collective-permute-start.38 = (bf16[2,288,768]{2,1,0:T(8,128)(2,1)}, bf16[2,288,768]{2,1,0:T(8,128)(2,1)S(1)}, u32[]{:S(2)}, u32[]{:S(2)}) collective-permute-start(bf16[2,288,768]{2,1,0:T(8,128)(2,1)} %shard_map.242.refs_1_), channel_id=1, source_target_pairs={{0,64},{64,0},{1,65},{65,1},{2,66},{66,2},{3,67},{67,3},{4,68},{68... | collective-permute-start | bytes 2654216 | tf_op jit(solution)/shard_map/ppermute | solution.py:677
  278.2 32.7 %all-to-all-start.8 = ((bf16[16,96,512]{2,1,0:T(8,128)(2,1)}), bf16[16,96,512]{2,1,0:T(8,128)(2,1)}, u32[]{:S(2)}, u32[]{:S(2)}) async-start(bf16[16,96,512]{2,1,0:T(8,128)(2,1)} %bitcast.80), calls=%async_computation.8 | async-start | bytes 3145728 | tf_op jit(solution)/shard_map/all_to_all | solution.py:681
  292.0 17.1 %collective-permute-start.40 = (bf16[288,768]{1,0:T(8,128)(2,1)}, bf16[288,768]{1,0:T(8,128)(2,1)}, u32[]{:S(2)}, u32[]{:S(2)}) collective-permute-start(bf16[288,768]{1,0:T(8,128)(2,1)} %get-tuple-element.212.refs_1_), channel_id=1, source_target_pairs={{0,16},{16,0},{32,48},{48,32},{1,17},{17,1},{33,49},{49,33},{2,18}... | collective-permute-start | bytes 1327112 | tf_op jit(solution)/shard_map/ppermute | solution.py:703
  292.0 22.0 %collective-permute-start.43 = (bf16[288,768]{1,0:T(8,128)(2,1)}, bf16[288,768]{1,0:T(8,128)(2,1)}, u32[]{:S(2)}, u32[]{:S(2)}) collective-permute-start(bf16[288,768]{1,0:T(8,128)(2,1)} %get-tuple-element.211.refs_0_), channel_id=1, source_target_pairs={{0,16},{16,0},{32,48},{48,32},{1,17},{17,1},{33,49},{49,33},{2,18}... | collective-permute-start | bytes 1327112 | tf_op jit(solution)/shard_map/ppermute | solution.py:703
  293.5 21.2 %collective-permute-start.44 = (bf16[288,768]{1,0:T(8,128)(2,1)}, bf16[288,768]{1,0:T(8,128)(2,1)}, u32[]{:S(2)}, u32[]{:S(2)}) collective-permute-start(bf16[288,768]{1,0:T(8,128)(2,1)} %get-tuple-element.212.refs_1_), channel_id=1, source_target_pairs={{0,48},{48,0},{16,32},{32,16},{1,49},{49,1},{17,33},{33,17},{2,50}... | collective-permute-start | bytes 1327112 | tf_op jit(solution)/shard_map/ppermute | solution.py:703
  295.3 19.5 %collective-permute-start.45 = (bf16[288,768]{1,0:T(8,128)(2,1)}, bf16[288,768]{1,0:T(8,128)(2,1)S(1)}, u32[]{:S(2)}, u32[]{:S(2)}) collective-permute-start(bf16[288,768]{1,0:T(8,128)(2,1)} %get-tuple-element.211.refs_0_), channel_id=1, source_target_pairs={{0,8},{8,0},{1,9},{9,1},{2,10},{10,2},{3,11},{11,3},{4,12},{12,4},... | collective-permute-start | bytes 1327112 | tf_op jit(solution)/shard_map/ppermute | solution.py:673
  301.0 14.2 %collective-permute-start.46 = (bf16[288,768]{1,0:T(8,128)(2,1)}, bf16[288,768]{1,0:T(8,128)(2,1)S(1)}, u32[]{:S(2)}, u32[]{:S(2)}) collective-permute-start(bf16[288,768]{1,0:T(8,128)(2,1)} %get-tuple-element.212.refs_1_), channel_id=1, source_target_pairs={{0,8},{8,0},{1,9},{9,1},{2,10},{10,2},{3,11},{11,3},{4,12},{12,4},... | collective-permute-start | bytes 1327112 | tf_op jit(solution)/shard_map/ppermute | solution.py:673
  315.2 14.3 %collective-permute-start.41 = (bf16[288,768]{1,0:T(8,128)(2,1)}, bf16[288,768]{1,0:T(8,128)(2,1)S(1)}, u32[]{:S(2)}, u32[]{:S(2)}) collective-permute-start(bf16[288,768]{1,0:T(8,128)(2,1)} %collective-permute-done.39.refs_2_), channel_id=1, source_target_pairs={{0,16},{16,0},{32,48},{48,32},{1,17},{17,1},{33,49},{49,33},{2,18}... | collective-permute-start | bytes 1327112 | tf_op jit(solution)/shard_map/ppermute | solution.py:703
  315.2 14.3 %collective-permute-start.42 = (bf16[288,768]{1,0:T(8,128)(2,1)}, bf16[288,768]{1,0:T(8,128)(2,1)S(1)}, u32[]{:S(2)}, u32[]{:S(2)}) collective-permute-start(bf16[288,768]{1,0:T(8,128)(2,1)} %collective-permute-done.40.refs_3_), channel_id=1, source_target_pairs={{0,48},{48,0},{16,32},{32,16},{1,49},{49,1},{17,33},{33,17},{2,50}... | collective-permute-start | bytes 1327112 | tf_op jit(solution)/shard_map/ppermute | solution.py:703
  316.9 24.1 %all-to-all-start.9 = ((bf16[8,96,512]{2,1,0:T(8,128)(2,1)}), bf16[8,96,512]{2,1,0:T(8,128)(2,1)S(1)}, u32[]{:S(2)}, u32[]{:S(2)}) async-start(bf16[8,96,512]{2,1,0:T(8,128)(2,1)} %shard_map.240), calls=%async_computation.9 | async-start | bytes 1572864 | tf_op jit(solution)/shard_map/all_to_all | solution.py:681
  (93 other events, 675.6 us)

commit v5 on v4

--- a/solution.py
+++ b/solution.py
@@ -494,7 +494,7 @@
     for y in range(YLO):
         rows = pl.ds(y * part, part)
         for x in range(XS):
-            mine, theirs = own[y * XS + x], other[y * XS + x]
+            mine, theirs = own.part(y)[y * XS + x], other.part(y)[y * XS + x]
             first = jnp.where(even, mine, theirs).astype(F32)
             second = jnp.where(even, theirs, mine).astype(F32)
             at = pl.ds(x * size, size)
@@ -504,6 +504,8 @@
             into[rows, pl.ds(x % (XS // 2) * small, small)] = second[:, size:]
             if y == 0:
                 total = total + first[:8, size:]
+        for out in (output_o, query_o, key_o, value_o):
+            out.send(y + 1)
     for ref, row in ((gain_one_o, 0), (gain_two_o, 2)):
         ref[:, pl.ds(0, small)] = total[row : row + 1]
         ref[:, pl.ds(small, ref.shape[1] - small)] = total[
@@ -973,9 +975,9 @@
     spreaded, e_mark = tie(spreaded, e_mark)
     grad_output_w, grad_query_w, grad_key_w, grad_value_w, grad_one, grad_two = call(
         final_kernel,
-        [place_at, Far(spreaded), Far(swap(spreaded)), e_mark],
-        [((rows, width), F32), ((rows, width), F32), ((rows, kv_width), F32),
-         ((rows, kv_width), F32), ((1, rows), F32), ((1, rows), F32)],
+        [place_at, Far(spreaded, parts=2), Far(swap(spreaded), parts=2), e_mark],
+        [Far((rows, width), F32, 2), Far((rows, width), F32, 2), Far((rows, kv_width), F32, 2),
+         Far((rows, kv_width), F32, 2), ((1, rows), F32), ((1, rows), F32)],
     )
     return (
         outputs[None],

time: 355 us -> 355 us (level)
  no operation moved by 1% of the time
where the time goes in v5:
time: 355 us; the launch traced here: 348 us
  starting transfers between devices  121 us (34%)
  Pallas kernels  106 us (30%)
  waiting for transfers between devices  66.4 us (19%)
  local copies, waits for them, and re-layouts  29.8 us (8%)
  matrix products  12.5 us (4%)
  other arithmetic  10.9 us (3%)
    pallas_call x15, Pallas kernels, call(): pl.pallas_call(whole, out_shape=[jax.ShapeDtypeStruct(out.value, out.kind...  94.3 us
    all_to_all x10, starting transfers between devices, exchange(): return lax.all_to_all(v, axis, 0, 0, tiled=True)  54.9 us
    ppermute x29, starting transfers between devices, swap(): return lax.ppermute(v, 'core', [(0, 1), (1, 0)])  41.1 us
    all_to_all x10, waiting for transfers between devices, exchange(): return lax.all_to_all(v, axis, 0, 0, tiled=True)  36.1 us
    ppermute x24, starting transfers between devices, flip(): return lax.ppermute(v, 'x', pairs)  24.5 us
    ppermute x24, waiting for transfers between devices, flip(): return lax.ppermute(v, 'x', pairs)  21.4 us
    unnamed x128, local copies, waits for them, and re-layouts  12.7 us
    pallas_call x2, Pallas kernels, expert_outputs(): pl.pallas_call(kernel, out_shape=shapes, in_specs=[pl.BlockSpec(memory_sp...  11.4 us
  transfers between devices with their start and end apart: 64, of which 27 were waited for; matrix products, arithmetic and copies ran while one was open for 11% of the time, Pallas kernels for 26%

profile of v5, /device:TPU:1, one launch (start us, length us, event | category | flops | bytes accessed | tf_op | source)
XLA Modules:
  0.0 348.3 jit_solution(8049561305851541368)
XLA Ops:
  4.2 8.6 %all-to-all-start = ((bf16[8,40,1536]{2,1,0:T(8,128)(2,1)}), bf16[8,40,1536]{2,1,0:T(8,128)(2,1)S(1)}, u32[]{:S(2)}, u32[]{:S(2)}) async-start(bf16[8,40,1536]{2,1,0:T(8,128)(2,1)} %broadcast_in_dim.91), calls=%async_computation | async-start | bytes 1966080 | tf_op jit(solution)/shard_map/all_to_all | solution.py:683
  18.0 10.1 %all-to-all-done = bf16[8,40,1536]{2,1,0:T(8,128)(2,1)S(1)} async-done(((bf16[8,40,1536]{2,1,0:T(8,128)(2,1)}), bf16[8,40,1536]{2,1,0:T(8,128)(2,1)S(1)}, u32[]{:S(2)}, u32[]{:S(2)}) %all-to-all-start) | async-done | bytes 983072 | tf_op jit(solution)/shard_map/all_to_all | solution.py:683
  28.1 4.4 %all-to-all-start.1 = ((bf16[8,96,1536]{2,1,0:T(8,128)(2,1)}), bf16[8,96,1536]{2,1,0:T(8,128)(2,1)}, u32[]{:S(2)}, u32[]{:S(2)}) async-start(bf16[8,96,1536]{2,1,0:T(8,128)(2,1)} %broadcast_in_dim.92), calls=%async_computation.1 | async-start | bytes 4718592 | tf_op jit(solution)/shard_map/all_to_all | solution.py:683
  49.7 4.0 %shard_map.230 = (bf16[128,1536]{1,0:T(8,128)(2,1)}, f32[128,128]{1,0:T(8,128)}, bf16[8,128,512]{2,1,0:T(8,128)(2,1)}, bf16[1536,512]{1,0:T(8,128)(2,1)}) custom-call(s32[4]{0:T(128)} %pad_add_fusion.refs_0_.place, bf16[128,1536]{1,0:T(8,128)(2,1)} %bitcast.92, f32[1,1536]{1,0:T(1,128)} %reshape.223.refs_2_.refs_5_, bf16[8,32,1536]{2,1,0:T(8,128)(2,1)} %slice.49.refs_3_, ...), custom_call_target="tpu_custom_call" | custom-call | tf_op jit(solution)/shard_map/pallas_call | solution.py:656
  53.7 7.9 %all-to-all-done.1 = bf16[8,96,1536]{2,1,0:T(8,128)(2,1)} async-done(((bf16[8,96,1536]{2,1,0:T(8,128)(2,1)}), bf16[8,96,1536]{2,1,0:T(8,128)(2,1)}, u32[]{:S(2)}, u32[]{:S(2)}) %all-to-all-start.1) | async-done | bytes 2359328 | tf_op jit(solution)/shard_map/all_to_all | solution.py:683
  61.6 5.0 %all-to-all-start.2 = ((bf16[8,128,512]{2,1,0:T(8,128)(2,1)}), bf16[8,128,512]{2,1,0:T(8,128)(2,1)S(1)}, u32[]{:S(2)}, u32[]{:S(2)}) async-start(bf16[8,128,512]{2,1,0:T(8,128)(2,1)} %get-tuple-element.132), calls=%async_computation.2 | async-start | bytes 2097152 | tf_op jit(solution)/shard_map/all_to_all | solution.py:683
  72.8 9.1 %all-to-all-done.2 = bf16[8,128,512]{2,1,0:T(8,128)(2,1)S(1)} async-done(((bf16[8,128,512]{2,1,0:T(8,128)(2,1)}), bf16[8,128,512]{2,1,0:T(8,128)(2,1)S(1)}, u32[]{:S(2)}, u32[]{:S(2)}) %all-to-all-start.2) | async-done | bytes 1048608 | tf_op jit(solution)/shard_map/all_to_all | solution.py:683
  82.9 4.3 %all-to-all-start.3 = ((bf16[8,80,1536]{2,1,0:T(8,128)(2,1)}), bf16[8,80,1536]{2,1,0:T(8,128)(2,1)}, u32[]{:S(2)}, u32[]{:S(2)}) async-start(bf16[8,80,1536]{2,1,0:T(8,128)(2,1)} %bitcast.79), calls=%async_computation.3 | async-start | bytes 3932160 | tf_op jit(solution)/shard_map/all_to_all | solution.py:683
  90.3 5.6 %collective-permute-done.1.refs_10_ = bf16[8,96,768]{2,1,0:T(8,128)(2,1)} collective-permute-done((bf16[8,96,768]{2,1,0:T(8,128)(2,1)}, bf16[8,96,768]{2,1,0:T(8,128)(2,1)}, u32[]{:S(2)}, u32[]{:S(2)}) %collective-permute-start.1) | collective-permute-done | bytes 1179680 | tf_op jit(solution)/shard_map/ppermute | solution.py:705
  104.0 12.6 %shard_map.231 = (bf16[8,192,1536]{2,1,0:T(8,128)(2,1)}, bf16[8,192,1536]{2,1,0:T(8,128)(2,1)}, bf16[128,1536]{1,0:T(8,128)(2,1)}, bf16[128,1536]{1,0:T(8,128)(2...) custom-call(s32[4]{0:T(128)} %pad_add_fusion.refs_0_.place, ...), custom_call_target="tpu_custom_call" | custom-call | tf_op jit(solution)/shard_map/pallas_call | solution.py:656
  116.6 6.7 %all-to-all-start.4 = ((bf16[8,80,1536]{2,1,0:T(8,128)(2,1)}), bf16[8,80,1536]{2,1,0:T(8,128)(2,1)}, u32[]{:S(2)}, u32[]{:S(2)}) async-start(bf16[8,80,1536]{2,1,0:T(8,128)(2,1)} %bitcast.89), calls=%async_computation.4 | async-start | bytes 3932160 | tf_op jit(solution)/shard_map/all_to_all | solution.py:683
  130.0 4.6 %fusion.3.refs_2_ = f32[640,768]{1,0:T(8,128)} fusion(bf16[640,1536]{1,0:T(8,128)(2,1)} %bitcast.19.refs_7_, bf16[1,768,1536]{2,1,0:T(8,128)(2,1)S(1)} %copy-done), kind=kOutput, calls=%fused_computation.6 | convolution fusion | flops 1509949440 | bytes 6291456 | tf_op jit(solution)/shard_map/dot_general | solution.py:41
  137.1 8.4 %collective-permute-done.11.refs_14_.refs_19_ = bf16[128,1536]{1,0:T(8,128)(2,1)S(1)} collective-permute-done((bf16[128,1536]{1,0:T(8,128)(2,1)S(1)}, bf16[128,1536]{1,0:T(8,128)(2,1)S(1)}, u32[]{:S(2)}, u32[]{:S(2)}) %collective-permute-start.11) | collective-permute-done | bytes 393248 | tf_op jit(solution)/shard_map/ppermute | solution.py:705
  151.9 11.6 %shard_map.232 = (bf16[640,768]{1,0:T(8,128)(2,1)}, bf16[640,768]{1,0:T(8,128)(2,1)}, bf16[640,768]{1,0:T(8,128)(2,1)}, bf16[640,1536]{1,0:T(8,128)(2,1)}) custom-call(s32[4]{0:T(128)} %pad_add_fusion.refs_0_.place, bf16[640,1536]{1,0:T(8,128)(2,1)} %bitcast.21.refs_1_, f32[640,768]{1,0:T(8,128)} %fusion.3.refs_2_, bf16[1536,768]{1,0:T(8,128)(2,1)} %bitcast.86, ...), custom_call_target="tpu_custom_call" | custom-call | tf_op jit(solution)/shard_map/pallas_call | solution.py:656
  163.5 4.4 %all-to-all-start.5 = ((bf16[8,80,1536]{2,1,0:T(8,128)(2,1)}), bf16[8,80,1536]{2,1,0:T(8,128)(2,1)}, u32[]{:S(2)}, u32[]{:S(2)}) async-start(bf16[8,80,1536]{2,1,0:T(8,128)(2,1)} %bitcast.90), calls=%async_computation.5 | async-start | bytes 3932160 | tf_op jit(solution)/shard_map/all_to_all | solution.py:683
  170.5 4.1 %convolution_convert_fusion = bf16[640,1536]{1,0:T(8,128)(2,1)} fusion(bf16[640,768]{1,0:T(8,128)(2,1)} %get-tuple-element.145.refs_5_, bf16[1,768,1536]{2,1,0:T(8,128)(2,1)S(1)} %copy-done), kind=kOutput, calls=%fused_computation.1 | convolution fusion | flops 1510932480 | bytes 5308416 | tf_op jit(solution)/shard_map/dot_general | solution.py:37
  175.9 12.9 %shard_map.233 = (bf16[2,288,768]{2,1,0:T(8,128)(2,1)}, bf16[2,288,768]{2,1,0:T(8,128)(2,1)}, bf16[2,288,768]{2,1,0:T(8,128)(2,1)}, bf16[2,288,768]{2,1,0:T(8,128)(2,1)}) custom-call(s32[4]{0:T(128)} %pad_add_fusion.refs_0_.place, bf16[640,1536]{1,0:T(8,128)(2,1)} %bitcast.21.refs_1_, bf16[640,1536]{1,0:T(8,128)(2,1)} %collective-permute-done.13.refs_2_, ...), custom_call_target="tpu_custom_call" | custom-call | tf_op jit(solution)/shard_map/pallas_call | solution.py:656
  189.6 5.5 %all-to-all-done.5 = bf16[8,80,1536]{2,1,0:T(8,128)(2,1)} async-done(((bf16[8,80,1536]{2,1,0:T(8,128)(2,1)}), bf16[8,80,1536]{2,1,0:T(8,128)(2,1)}, u32[]{:S(2)}, u32[]{:S(2)}) %all-to-all-start.5) | async-done | bytes 1966112 | tf_op jit(solution)/shard_map/all_to_all | solution.py:683
  195.1 12.4 %shard_map.234 = (f32[128,1536]{1,0:T(8,128)}, bf16[128,1536]{1,0:T(8,128)(2,1)}, f32[8,2,128]{2,1,0:T(2,128)}, bf16[128,1536]{1,0:T(8,128)(2,1)}, bf16[1024,512...) custom-call(s32[4]{0:T(128)} %pad_add_fusion.refs_0_.place, ...), custom_call_target="tpu_custom_call" | custom-call | tf_op jit(solution)/shard_map/pallas_call | solution.py:656
  207.6 3.7 %all-to-all-start.6 = ((bf16[8,128,512]{2,1,0:T(8,128)(2,1)}), bf16[8,128,512]{2,1,0:T(8,128)(2,1)S(1)}, u32[]{:S(2)}, u32[]{:S(2)}) async-start(bf16[8,128,512]{2,1,0:T(8,128)(2,1)} %bitcast.96), calls=%async_computation.6 | async-start | bytes 2097152 | tf_op jit(solution)/shard_map/all_to_all | solution.py:683
  218.8 5.7 %shard_map.235.refs_1_ = f32[128,1536]{1,0:T(8,128)} custom-call(s32[4]{0:T(128)} %pad_add_fusion.refs_0_.place, bf16[128,1536]{1,0:T(8,128)(2,1)} %get-tuple-element.165.refs_1_, bf16[1536,1536]{1,0:T(8,128)(2,1)} %bitcast.82), custom_call_target="tpu_custom_call" | custom-call | tf_op jit(solution)/shard_map/pallas_call | solution.py:656
  230.8 5.9 %shard_map.236.refs_1_ = bf16[1536,384]{1,0:T(8,128)(2,1)} custom-call(s32[4]{0:T(128)} %pad_add_fusion.refs_0_.place, bf16[128,768]{1,0:T(8,128)(2,1)} %get-tuple-element.161.refs_1_, bf16[128,768]{1,0:T(8,128)(2,1)} %copy-done.35, bf16[128,768]{1,0:T(8,128)(2,1)} %copy-done.36, bf16[128,768]{1,0:T(8,128)(2,1)} %copy-done.37, bf16[128,768]{1,0:T(8,128)(2,1)} %copy-done.38, ...), custom_call_target="tpu_custom_call" | custom-call | tf_op jit(solution)/shard_map/pallas_call | solution.py:656
  237.6 6.8 %all-to-all-start.7 = ((bf16[8,80,1536]{2,1,0:T(8,128)(2,1)}), bf16[8,80,1536]{2,1,0:T(8,128)(2,1)S(1)}, u32[]{:S(2)}, u32[]{:S(2)}) async-start(bf16[8,80,1536]{2,1,0:T(8,128)(2,1)} %bitcast.88), calls=%async_computation.7 | async-start | bytes 3932160 | tf_op jit(solution)/shard_map/all_to_all | solution.py:683
  244.4 3.9 %shard_map.241 = (bf16[288,768]{1,0:T(8,128)(2,1)}, bf16[288,768]{1,0:T(8,128)(2,1)}, bf16[288,768]{1,0:T(8,128)(2,1)}, bf16[288,768]{1,0:T(8,128)(2,1)}) custom-call(s32[4]{0:T(128)} %pad_add_fusion.refs_0_.place, bf16[2,288,768]{2,1,0:T(8,128)(2,1)} %get-tuple-element.199.refs_1_, bf16[2,288,768]{2,1,0:T(8,128)(2,1)} %collective-permute-done.34.refs_2_, ...), custom_call_target="tpu_custom_call" | custom-call | tf_op jit(solution)/shard_map/pallas_call | solution.py:656
  255.6 4.5 %shard_map.238 = (bf16[128,1536]{1,0:T(8,128)(2,1)}, f32[8,2,128]{2,1,0:T(2,128)}, f32[8,128]{1,0:T(8,128)}) custom-call(s32[4]{0:T(128)} %pad_add_fusion.refs_0_.place, f32[128,1536]{1,0:T(8,128)} %shard_map.235.refs_1_, bf16[128,512]{1,0:T(8,128)(2,1)} %get-tuple-element.177.refs_2_, bf16[128,1536]{1,0:T(8,128)(2,1)} %bitcast.94, ...), custom_call_target="tpu_custom_call" | custom-call | flops 6000000000 | tf_op jit(solution)/shard_map/pallas_call | solution.py:656
  273.1 5.1 %shard_map.239 = bf16[2,8,96,512]{3,2,1,0:T(8,128)(2,1)} custom-call(s32[4]{0:T(128)} %pad_add_fusion.refs_0_.place, bf16[1536,384]{1,0:T(8,128)(2,1)} %shard_map.236.refs_1_, f32[8,2,128]{2,1,0:T(2,128)} %get-tuple-element.181.refs_2_, f32[8,2,128]{2,1,0:T(2,128)} %copy-done.54, f32[8,2,128]{2,1,0:T(2,128)} %get-tuple-element.182.refs_4_, ...), custom_call_target="tpu_custom_call" | custom-call | tf_op jit(solution)/shard_map/pallas_call | solution.py:656
  278.2 7.5 %all-to-all-start.8 = ((bf16[16,96,512]{2,1,0:T(8,128)(2,1)}), bf16[16,96,512]{2,1,0:T(8,128)(2,1)}, u32[]{:S(2)}, u32[]{:S(2)}) async-start(bf16[16,96,512]{2,1,0:T(8,128)(2,1)} %bitcast.80), calls=%async_computation.8 | async-start | bytes 3145728 | tf_op jit(solution)/shard_map/all_to_all | solution.py:683
  295.3 4.5 %collective-permute-start.45 = (bf16[288,768]{1,0:T(8,128)(2,1)}, bf16[288,768]{1,0:T(8,128)(2,1)S(1)}, u32[]{:S(2)}, u32[]{:S(2)}) collective-permute-start(bf16[288,768]{1,0:T(8,128)(2,1)} %get-tuple-element.211.refs_0_), channel_id=1, source_target_pairs={{0,8},{8,0},{1,9},{9,1},{2,10},{10,2},{3,11},{11,3},{4,12},{12,4},... | collective-permute-start | bytes 1327112 | tf_op jit(solution)/shard_map/ppermute | solution.py:675
  301.0 8.1 %collective-permute-start.46 = (bf16[288,768]{1,0:T(8,128)(2,1)}, bf16[288,768]{1,0:T(8,128)(2,1)S(1)}, u32[]{:S(2)}, u32[]{:S(2)}) collective-permute-start(bf16[288,768]{1,0:T(8,128)(2,1)} %get-tuple-element.212.refs_1_), channel_id=1, source_target_pairs={{0,8},{8,0},{1,9},{9,1},{2,10},{10,2},{3,11},{11,3},{4,12},{12,4},... | collective-permute-start | bytes 1327112 | tf_op jit(solution)/shard_map/ppermute | solution.py:675
  322.2 7.3 %shard_map.244 = (f32[1536,768]{1,0:T(8,128)}, f32[1536,768]{1,0:T(8,128)}, f32[768,1536]{1,0:T(8,128)}, f32[8,128]{1,0:T(8,128)}) custom-call(s32[4]{0:T(128)} %pad_add_fusion.refs_0_.place, bf16[288,768]{1,0:T(8,128)(2,1)} %get-tuple-element.211.refs_0_, bf16[288,768]{1,0:T(8,128)(2,1)} %get-tuple-element.212.refs_1_, ...), custom_call_target="tpu_custom_call" | custom-call | tf_op jit(solution)/shard_map/pallas_call | solution.py:325
  330.2 3.8 %collective-permute-start.51 = (bf16[288,768]{1,0:T(8,128)(2,1)S(1)}, bf16[288,768]{1,0:T(8,128)(2,1)S(1)}, u32[]{:S(2)}, u32[]{:S(2)}) collective-permute-start(bf16[288,768]{1,0:T(8,128)(2,1)S(1)} %collective-permute-done.41.refs_0_), channel_id=1, source_target_pairs={{0,8},{8,0},{1,9},{9,1},{2,10},{10,2},{3,11},{11,3},{4,12},{12,4},... | collective-permute-start | bytes 1327112 | tf_op jit(solution)/shard_map/ppermute | solution.py:675
  336.8 4.1 %shard_map.245 = (f32[1536,768]{1,0:T(8,128)}, f32[1536,768]{1,0:T(8,128)}, f32[768,1536]{1,0:T(8,128)}, f32[8,128]{1,0:T(8,128)}) custom-call(s32[4]{0:T(128)} %pad_add_fusion.refs_0_.place, bf16[288,768]{1,0:T(8,128)(2,1)} %copy-done.24, bf16[288,768]{1,0:T(8,128)(2,1)} %copy-done.26, ...), custom_call_target="tpu_custom_call", output_to_operand_aliasing={{0}: (7, {}), {1}: (8, {}), {2}: (9, {})} | custom-call | tf_op jit(solution)/shard_map/pallas_call | solution.py:325
  (295 shorter events, 133.3 us)
Async XLA Ops:
  4.2 23.9 %all-to-all-start = ((bf16[8,40,1536]{2,1,0:T(8,128)(2,1)}), bf16[8,40,1536]{2,1,0:T(8,128)(2,1)S(1)}, u32[]{:S(2)}, u32[]{:S(2)}) async-start(bf16[8,40,1536]{2,1,0:T(8,128)(2,1)} %broadcast_in_dim.91), calls=%async_computation | async-start | bytes 1966080 | tf_op jit(solution)/shard_map/all_to_all | solution.py:683
  28.1 33.5 %all-to-all-start.1 = ((bf16[8,96,1536]{2,1,0:T(8,128)(2,1)}), bf16[8,96,1536]{2,1,0:T(8,128)(2,1)}, u32[]{:S(2)}, u32[]{:S(2)}) async-start(bf16[8,96,1536]{2,1,0:T(8,128)(2,1)} %broadcast_in_dim.92), calls=%async_computation.1 | async-start | bytes 4718592 | tf_op jit(solution)/shard_map/all_to_all | solution.py:683
  36.2 13.5 %collective-permute-start = (bf16[8,32,1536]{2,1,0:T(8,128)(2,1)}, bf16[8,32,1536]{2,1,0:T(8,128)(2,1)}, u32[]{:S(2)}, u32[]{:S(2)}) collective-permute-start(bf16[8,32,1536]{2,1,0:T(8,128)(2,1)} %slice.49.refs_3_), channel_id=1, source_target_pairs={{0,8},{8,0},{1,9},{9,1},{2,10},{10,2},{3,11},{11,3},{4,12},{12,4},... | collective-permute-start | bytes 2359304 | tf_op jit(solution)/shard_map/ppermute | solution.py:675
  61.6 20.3 %all-to-all-start.2 = ((bf16[8,128,512]{2,1,0:T(8,128)(2,1)}), bf16[8,128,512]{2,1,0:T(8,128)(2,1)S(1)}, u32[]{:S(2)}, u32[]{:S(2)}) async-start(bf16[8,128,512]{2,1,0:T(8,128)(2,1)} %get-tuple-element.132), calls=%async_computation.2 | async-start | bytes 2097152 | tf_op jit(solution)/shard_map/all_to_all | solution.py:683
  69.8 26.1 %collective-permute-start.1 = (bf16[8,96,768]{2,1,0:T(8,128)(2,1)}, bf16[8,96,768]{2,1,0:T(8,128)(2,1)}, u32[]{:S(2)}, u32[]{:S(2)}) collective-permute-start(bf16[8,96,768]{2,1,0:T(8,128)(2,1)} %get-tuple-element.238.refs_9_), channel_id=1, source_target_pairs={{0,16},{16,0},{32,48},{48,32},{1,17},{17,1},{33,49},{49,33},{2,18}... | collective-permute-start | bytes 3538952 | tf_op jit(solution)/shard_map/ppermute | solution.py:705
  71.0 27.5 %collective-permute-start.4 = (bf16[8,96,768]{2,1,0:T(8,128)(2,1)}, bf16[8,96,768]{2,1,0:T(8,128)(2,1)}, u32[]{:S(2)}, u32[]{:S(2)}) collective-permute-start(bf16[8,96,768]{2,1,0:T(8,128)(2,1)} %get-tuple-element.237.refs_13_), channel_id=1, source_target_pairs={{0,48},{48,0},{16,32},{32,16},{1,49},{49,1},{17,33},{33,17},{2,50}... | collective-permute-start | bytes 3538952 | tf_op jit(solution)/shard_map/ppermute | solution.py:705
  82.9 33.7 %all-to-all-start.3 = ((bf16[8,80,1536]{2,1,0:T(8,128)(2,1)}), bf16[8,80,1536]{2,1,0:T(8,128)(2,1)}, u32[]{:S(2)}, u32[]{:S(2)}) async-start(bf16[8,80,1536]{2,1,0:T(8,128)(2,1)} %bitcast.79), calls=%async_computation.3 | async-start | bytes 3932160 | tf_op jit(solution)/shard_map/all_to_all | solution.py:683
  87.3 14.6 %collective-permute-start.2 = (bf16[8,96,768]{2,1,0:T(8,128)(2,1)}, bf16[8,96,768]{2,1,0:T(8,128)(2,1)S(1)}, u32[]{:S(2)}, u32[]{:S(2)}) collective-permute-start(bf16[8,96,768]{2,1,0:T(8,128)(2,1)} %get-tuple-element.238.refs_9_), channel_id=1, source_target_pairs={{0,8},{8,0},{1,9},{9,1},{2,10},{10,2},{3,11},{11,3},{4,12},{12,4},... | collective-permute-start | bytes 3538952 | tf_op jit(solution)/shard_map/ppermute | solution.py:675
  116.6 33.2 %all-to-all-start.4 = ((bf16[8,80,1536]{2,1,0:T(8,128)(2,1)}), bf16[8,80,1536]{2,1,0:T(8,128)(2,1)}, u32[]{:S(2)}, u32[]{:S(2)}) async-start(bf16[8,80,1536]{2,1,0:T(8,128)(2,1)} %bitcast.89), calls=%async_computation.4 | async-start | bytes 3932160 | tf_op jit(solution)/shard_map/all_to_all | solution.py:683
  124.7 21.7 %collective-permute-start.7 = (bf16[640,768]{1,0:T(8,128)(2,1)S(1)}, bf16[640,768]{1,0:T(8,128)(2,1)}, u32[]{:S(2)}, u32[]{:S(2)}) collective-permute-start(bf16[640,768]{1,0:T(8,128)(2,1)S(1)} %constant_dynamic-slice_fusion), channel_id=1, source_target_pairs={{0,8},{8,0},{1,9},{9,1},{2,10},{10,2},{3,11},{11,3},{4,12},{12,4},... | collective-permute-start | bytes 2949128 | tf_op jit(solution)/shard_map/ppermute | solution.py:675
  128.2 17.4 %collective-permute-start.11 = (bf16[128,1536]{1,0:T(8,128)(2,1)S(1)}, bf16[128,1536]{1,0:T(8,128)(2,1)S(1)}, u32[]{:S(2)}, u32[]{:S(2)}) collective-permute-start(bf16[128,1536]{1,0:T(8,128)(2,1)S(1)} %collective-permute-done.10.refs_10_.refs_15_), channel_id=1, source_target_pairs={{0,48},{48,0},{16,32},{32,16},{1,49},{49,1},{17,33},{33,17},{2,50}... | collective-permute-start | bytes 1179656 | tf_op jit(solution)/shard_map/ppermute | solution.py:705
  130.0 15.6 %collective-permute-start.12 = (bf16[128,1536]{1,0:T(8,128)(2,1)S(1)}, bf16[128,1536]{1,0:T(8,128)(2,1)S(1)}, u32[]{:S(2)}, u32[]{:S(2)}) collective-permute-start(bf16[128,1536]{1,0:T(8,128)(2,1)S(1)} %collective-permute-done.10.refs_10_.refs_15_), channel_id=1, source_target_pairs={{0,16},{16,0},{32,48},{48,32},{1,17},{17,1},{33,49},{49,33},{2,18}... | collective-permute-start | bytes 1179656 | tf_op jit(solution)/shard_map/ppermute | solution.py:705
  149.9 24.8 %collective-permute-start.13 = (bf16[640,1536]{1,0:T(8,128)(2,1)}, bf16[640,1536]{1,0:T(8,128)(2,1)}, u32[]{:S(2)}, u32[]{:S(2)}) collective-permute-start(bf16[640,1536]{1,0:T(8,128)(2,1)} %bitcast.21.refs_1_), channel_id=1, source_target_pairs={{0,8},{8,0},{1,9},{9,1},{2,10},{10,2},{3,11},{11,3},{4,12},{12,4},... | collective-permute-start | bytes 5898248 | tf_op jit(solution)/shard_map/ppermute | solution.py:675
  163.5 31.6 %all-to-all-start.5 = ((bf16[8,80,1536]{2,1,0:T(8,128)(2,1)}), bf16[8,80,1536]{2,1,0:T(8,128)(2,1)}, u32[]{:S(2)}, u32[]{:S(2)}) async-start(bf16[8,80,1536]{2,1,0:T(8,128)(2,1)} %bitcast.90), calls=%async_computation.5 | async-start | bytes 3932160 | tf_op jit(solution)/shard_map/all_to_all | solution.py:683
  168.5 20.3 %collective-permute-start.16 = (bf16[128,1536]{1,0:T(8,128)(2,1)S(1)}, bf16[128,1536]{1,0:T(8,128)(2,1)S(1)}, u32[]{:S(2)}, u32[]{:S(2)}) collective-permute-start(bf16[128,1536]{1,0:T(8,128)(2,1)S(1)} %collective-permute-done.8.refs_11_.refs_16_), channel_id=1, source_target_pairs={{0,48},{48,0},{16,32},{32,16},{1,49},{49,1},{17,33},{33,17},{2,50}... | collective-permute-start | bytes 1179656 | tf_op jit(solution)/shard_map/ppermute | solution.py:705
  170.3 19.2 %collective-permute-start.17 = (bf16[128,1536]{1,0:T(8,128)(2,1)S(1)}, bf16[128,1536]{1,0:T(8,128)(2,1)}, u32[]{:S(2)}, u32[]{:S(2)}) collective-permute-start(bf16[128,1536]{1,0:T(8,128)(2,1)S(1)} %collective-permute-done.11.refs_14_.refs_19_), channel_id=1, source_target_pairs={{0,16},{16,0},{32,48},{48,32},{1,17},{17,1},{33,49},{49,33},{2,18}... | collective-permute-start | bytes 1179656 | tf_op jit(solution)/shard_map/ppermute | solution.py:705
  207.6 29.1 %all-to-all-start.6 = ((bf16[8,128,512]{2,1,0:T(8,128)(2,1)}), bf16[8,128,512]{2,1,0:T(8,128)(2,1)S(1)}, u32[]{:S(2)}, u32[]{:S(2)}) async-start(bf16[8,128,512]{2,1,0:T(8,128)(2,1)} %bitcast.96), calls=%async_computation.6 | async-start | bytes 2097152 | tf_op jit(solution)/shard_map/all_to_all | solution.py:683
  216.3 28.1 %collective-permute-start.34 = (bf16[2,288,768]{2,1,0:T(8,128)(2,1)}, bf16[2,288,768]{2,1,0:T(8,128)(2,1)}, u32[]{:S(2)}, u32[]{:S(2)}) collective-permute-start(bf16[2,288,768]{2,1,0:T(8,128)(2,1)} %get-tuple-element.200), channel_id=1, source_target_pairs={{0,16},{16,0},{32,48},{48,32},{1,17},{17,1},{33,49},{49,33},{2,18}... | collective-permute-start | bytes 2654216 | tf_op jit(solution)/shard_map/ppermute | solution.py:705
  216.9 27.5 %collective-permute-start.35 = (bf16[2,288,768]{2,1,0:T(8,128)(2,1)}, bf16[2,288,768]{2,1,0:T(8,128)(2,1)}, u32[]{:S(2)}, u32[]{:S(2)}) collective-permute-start(bf16[2,288,768]{2,1,0:T(8,128)(2,1)} %get-tuple-element.202), channel_id=1, source_target_pairs={{0,48},{48,0},{16,32},{32,16},{1,49},{49,1},{17,33},{33,17},{2,50}... | collective-permute-start | bytes 2654216 | tf_op jit(solution)/shard_map/ppermute | solution.py:705
  237.6 40.6 %all-to-all-start.7 = ((bf16[8,80,1536]{2,1,0:T(8,128)(2,1)}), bf16[8,80,1536]{2,1,0:T(8,128)(2,1)S(1)}, u32[]{:S(2)}, u32[]{:S(2)}) async-start(bf16[8,80,1536]{2,1,0:T(8,128)(2,1)} %bitcast.88), calls=%async_computation.7 | async-start | bytes 3932160 | tf_op jit(solution)/shard_map/all_to_all | solution.py:683
  248.3 14.9 %collective-permute-start.36 = (bf16[288,768]{1,0:T(8,128)(2,1)}, bf16[288,768]{1,0:T(8,128)(2,1)S(1)}, u32[]{:S(2)}, u32[]{:S(2)}) collective-permute-start(bf16[288,768]{1,0:T(8,128)(2,1)} %get-tuple-element.204), channel_id=1, source_target_pairs={{0,48},{48,0},{16,32},{32,16},{1,49},{49,1},{17,33},{33,17},{2,50}... | collective-permute-start | bytes 1327112 | tf_op jit(solution)/shard_map/ppermute | solution.py:705
  249.3 14.0 %collective-permute-start.37 = (bf16[288,768]{1,0:T(8,128)(2,1)}, bf16[288,768]{1,0:T(8,128)(2,1)S(1)}, u32[]{:S(2)}, u32[]{:S(2)}) collective-permute-start(bf16[288,768]{1,0:T(8,128)(2,1)} %get-tuple-element.205), channel_id=1, source_target_pairs={{0,16},{16,0},{32,48},{48,32},{1,17},{17,1},{33,49},{49,33},{2,18}... | collective-permute-start | bytes 1327112 | tf_op jit(solution)/shard_map/ppermute | solution.py:705
  267.3 19.7 %collective-permute-start.38 = (bf16[2,288,768]{2,1,0:T(8,128)(2,1)}, bf16[2,288,768]{2,1,0:T(8,128)(2,1)S(1)}, u32[]{:S(2)}, u32[]{:S(2)}) collective-permute-start(bf16[2,288,768]{2,1,0:T(8,128)(2,1)} %shard_map.242.refs_1_), channel_id=1, source_target_pairs={{0,64},{64,0},{1,65},{65,1},{2,66},{66,2},{3,67},{67,3},{4,68},{68... | collective-permute-start | bytes 2654216 | tf_op jit(solution)/shard_map/ppermute | solution.py:679
  278.2 32.7 %all-to-all-start.8 = ((bf16[16,96,512]{2,1,0:T(8,128)(2,1)}), bf16[16,96,512]{2,1,0:T(8,128)(2,1)}, u32[]{:S(2)}, u32[]{:S(2)}) async-start(bf16[16,96,512]{2,1,0:T(8,128)(2,1)} %bitcast.80), calls=%async_computation.8 | async-start | bytes 3145728 | tf_op jit(solution)/shard_map/all_to_all | solution.py:683
  292.0 17.1 %collective-permute-start.40 = (bf16[288,768]{1,0:T(8,128)(2,1)}, bf16[288,768]{1,0:T(8,128)(2,1)}, u32[]{:S(2)}, u32[]{:S(2)}) collective-permute-start(bf16[288,768]{1,0:T(8,128)(2,1)} %get-tuple-element.212.refs_1_), channel_id=1, source_target_pairs={{0,16},{16,0},{32,48},{48,32},{1,17},{17,1},{33,49},{49,33},{2,18}... | collective-permute-start | bytes 1327112 | tf_op jit(solution)/shard_map/ppermute | solution.py:705
  292.0 22.0 %collective-permute-start.43 = (bf16[288,768]{1,0:T(8,128)(2,1)}, bf16[288,768]{1,0:T(8,128)(2,1)}, u32[]{:S(2)}, u32[]{:S(2)}) collective-permute-start(bf16[288,768]{1,0:T(8,128)(2,1)} %get-tuple-element.211.refs_0_), channel_id=1, source_target_pairs={{0,16},{16,0},{32,48},{48,32},{1,17},{17,1},{33,49},{49,33},{2,18}... | collective-permute-start | bytes 1327112 | tf_op jit(solution)/shard_map/ppermute | solution.py:705
  293.5 21.2 %collective-permute-start.44 = (bf16[288,768]{1,0:T(8,128)(2,1)}, bf16[288,768]{1,0:T(8,128)(2,1)}, u32[]{:S(2)}, u32[]{:S(2)}) collective-permute-start(bf16[288,768]{1,0:T(8,128)(2,1)} %get-tuple-element.212.refs_1_), channel_id=1, source_target_pairs={{0,48},{48,0},{16,32},{32,16},{1,49},{49,1},{17,33},{33,17},{2,50}... | collective-permute-start | bytes 1327112 | tf_op jit(solution)/shard_map/ppermute | solution.py:705
  295.3 19.5 %collective-permute-start.45 = (bf16[288,768]{1,0:T(8,128)(2,1)}, bf16[288,768]{1,0:T(8,128)(2,1)S(1)}, u32[]{:S(2)}, u32[]{:S(2)}) collective-permute-start(bf16[288,768]{1,0:T(8,128)(2,1)} %get-tuple-element.211.refs_0_), channel_id=1, source_target_pairs={{0,8},{8,0},{1,9},{9,1},{2,10},{10,2},{3,11},{11,3},{4,12},{12,4},... | collective-permute-start | bytes 1327112 | tf_op jit(solution)/shard_map/ppermute | solution.py:675
  301.0 14.2 %collective-permute-start.46 = (bf16[288,768]{1,0:T(8,128)(2,1)}, bf16[288,768]{1,0:T(8,128)(2,1)S(1)}, u32[]{:S(2)}, u32[]{:S(2)}) collective-permute-start(bf16[288,768]{1,0:T(8,128)(2,1)} %get-tuple-element.212.refs_1_), channel_id=1, source_target_pairs={{0,8},{8,0},{1,9},{9,1},{2,10},{10,2},{3,11},{11,3},{4,12},{12,4},... | collective-permute-start | bytes 1327112 | tf_op jit(solution)/shard_map/ppermute | solution.py:675
  315.2 14.3 %collective-permute-start.41 = (bf16[288,768]{1,0:T(8,128)(2,1)}, bf16[288,768]{1,0:T(8,128)(2,1)S(1)}, u32[]{:S(2)}, u32[]{:S(2)}) collective-permute-start(bf16[288,768]{1,0:T(8,128)(2,1)} %collective-permute-done.39.refs_2_), channel_id=1, source_target_pairs={{0,16},{16,0},{32,48},{48,32},{1,17},{17,1},{33,49},{49,33},{2,18}... | collective-permute-start | bytes 1327112 | tf_op jit(solution)/shard_map/ppermute | solution.py:705
  315.2 14.3 %collective-permute-start.42 = (bf16[288,768]{1,0:T(8,128)(2,1)}, bf16[288,768]{1,0:T(8,128)(2,1)S(1)}, u32[]{:S(2)}, u32[]{:S(2)}) collective-permute-start(bf16[288,768]{1,0:T(8,128)(2,1)} %collective-permute-done.40.refs_3_), channel_id=1, source_target_pairs={{0,48},{48,0},{16,32},{32,16},{1,49},{49,1},{17,33},{33,17},{2,50}... | collective-permute-start | bytes 1327112 | tf_op jit(solution)/shard_map/ppermute | solution.py:705
  316.9 24.1 %all-to-all-start.9 = ((bf16[8,96,512]{2,1,0:T(8,128)(2,1)}), bf16[8,96,512]{2,1,0:T(8,128)(2,1)S(1)}, u32[]{:S(2)}, u32[]{:S(2)}) async-start(bf16[8,96,512]{2,1,0:T(8,128)(2,1)} %shard_map.240), calls=%async_computation.9 | async-start | bytes 1572864 | tf_op jit(solution)/shard_map/all_to_all | solution.py:683
  (93 other events, 675.4 us)
